TPU v7x, 32 devices: a whole 2x2x4 slice. The times are simulated.
32 devices in a mesh: seq: 8 (over z, x), mp: 4 (over y, core).
Axes of the slice: x: 2, y: 2, z: 4, core: 2. Of those that a mesh axis runs over, the one named last changes fastest.
Arguments:
- hidden: bfloat16 [2048, 4096], P('seq', 'mp'), may hold values from -6 to 6
- cotangent: bfloat16 [2048, 4096], P('seq', 'mp'), may hold values from -6 to 6
- neighbour_ids: int32 [32, 2, 128], P('seq'), may hold values from 0 to 63999
- neighbour_lengths: int32 [32, 2], replicated, may hold values from 1 to 128
- embed_table: bfloat16 [64000, 896], P('mp'), may hold values from -6 to 6
- enc_up: bfloat16 [3584, 896], P('mp'), may hold values from -0.1875 to 0.1875
- enc_down: bfloat16 [3584, 896], P('mp'), may hold values from -0.09375 to 0.09375
- w_query: bfloat16 [4096, 32, 128], P('seq', 'mp'), may hold values from -0.125 to 0.125
- w_keyval: bfloat16 [896, 32, 2, 128], P('seq', 'mp'), may hold values from -0.1875 to 0.1875
- w_out: bfloat16 [4096, 32, 128], P('seq', 'mp'), may hold values from -0.75 to 0.75
Outputs:
- cca_out: bfloat16 [2048, 4096], P('seq', 'mp')
- hidden_grad: bfloat16 [2048, 4096], P('seq', 'mp')
All inputs are finite; a program needn't handle non-finite values.
Results may differ from a plain program's by a relative error of at most 0.012.
Values may be sent and summed in bfloat16 or wider, within the bound.
No kernel may reach another device: no remote copies, remote signals or barrier semaphores. Data moves between devices by JAX's collectives and lax.ppermute only.
A program may use at most 128 MiB of HBM per device.

v0:
```python
import jax
import jax.numpy as jnp
from jax import lax
from jax.sharding import PartitionSpec as P


def from_behind(shard, axis, by):
    count = lax.axis_size(axis)
    pairs = [(i, i + by) for i in range(count) if 0 <= i + by < count]
    return lax.ppermute(shard, axis, pairs)


def rms_rows(values):
    return values * lax.rsqrt(jnp.mean(values * values, axis=-1, keepdims=True) + 1e-06)


def shift_rows(flat, span_len):
    width = flat.shape[1]
    front = jnp.zeros((1, width), flat.dtype)
    back = jnp.zeros((span_len - 1, width), flat.dtype)
    return jnp.concatenate([front, flat, back], axis=0)


def contract_heads(left, right):
    return lax.dot_general(
        left, right, (((1,), (1,)), ((), ())), preferred_element_type=jnp.float32
    )


def per_device(
    hidden,
    cotangent,
    neighbour_ids,
    neighbour_lengths,
    embed_table,
    enc_up,
    enc_down,
    w_query,
    w_keyval,
    w_out,
):
    spans_here, neigh, nlen = neighbour_ids.shape
    tok_rows = hidden.shape[0]
    span_len = tok_rows // spans_here
    groups = spans_here + 1
    keys_per = neigh * nlen
    id_rows = spans_here * keys_per
    vocab_here = embed_table.shape[0]
    local_ids = neighbour_ids.reshape(id_rows) - lax.axis_index("mp") * vocab_here
    inside = jnp.logical_and(local_ids >= 0, local_ids < vocab_here)
    picked = jnp.take(embed_table, jnp.clip(local_ids, 0, vocab_here - 1), axis=0)
    masked = jnp.where(inside[:, None], picked, jnp.zeros((), picked.dtype))
    emb_share = (
        lax.psum_scatter(masked, "mp", scatter_dimension=0, tiled=True)
        .astype(jnp.float32)
        .astype(jnp.bfloat16)
    )
    emb = lax.all_gather(emb_share, "mp", axis=0, tiled=True)
    whole_hidden, whole_cot = (
        lax.all_gather(hidden, "mp", axis=1, tiled=True),
        lax.all_gather(cotangent, "mp", axis=1, tiled=True),
    )
    wq_full, wkv_full, wo_full = (
        lax.all_gather(w_query, "seq", axis=0, tiled=True),
        lax.all_gather(w_keyval, "seq", axis=0, tiled=True),
        lax.all_gather(w_out, "seq", axis=0, tiled=True),
    )
    width = whole_hidden.shape[1]
    heads_here = wq_full.shape[1]
    head_dim = wq_full.shape[2]
    inner = heads_here * head_dim
    scale = head_dim ** (-0.5)
    wq_flat = wq_full.reshape(width, inner)
    wo_flat = wo_full.reshape(width, inner)
    enc_width = emb.shape[1]
    wkv_flat = wkv_full.reshape(enc_width, 2 * inner)
    emb_wide = emb.astype(jnp.float32)
    normed = rms_rows(emb_wide).astype(jnp.bfloat16)
    act_cols = jax.nn.gelu(contract_heads(enc_up, normed)).astype(jnp.bfloat16)
    ffn_part = lax.dot_general(
        act_cols, enc_down, (((0,), (0,)), ((), ())), preferred_element_type=jnp.float32
    )
    share = lax.psum_scatter(ffn_part, "mp", scatter_dimension=0, tiled=True)
    count = share.shape[0]
    mine = lax.dynamic_slice_in_dim(emb_wide, lax.axis_index("mp") * count, count, 0)
    enc_share = rms_rows(mine + share).astype(jnp.bfloat16)
    encoded = lax.all_gather(enc_share, "mp", axis=0, tiled=True)
    keyval = jnp.dot(encoded, wkv_flat, preferred_element_type=jnp.float32).astype(jnp.bfloat16)
    keyval = keyval.reshape(spans_here, keys_per, 2 * inner)
    last_rows = encoded.reshape(spans_here, keys_per, enc_width)[spans_here - 1]
    prev_rows = from_behind(last_rows, "seq", 1)
    previous = jnp.dot(prev_rows, wkv_flat, preferred_element_type=jnp.float32).astype(jnp.bfloat16)
    keyval_all = jnp.concatenate([previous[None], keyval], axis=0).reshape(
        groups, keys_per, heads_here, 2, head_dim
    )
    keys = keyval_all[:, :, :, 0]
    values = keyval_all[:, :, :, 1]
    position = lax.axis_index("seq")
    lens_pad = jnp.concatenate([jnp.ones((1, neigh), jnp.int32), neighbour_lengths], axis=0)
    lens = lax.dynamic_slice_in_dim(lens_pad, position * spans_here, groups, 0)
    key_mask = (jnp.arange(nlen, dtype=jnp.int32)[None, None, :] < lens[:, :, None]).reshape(
        groups, keys_per
    )
    valid = jnp.logical_or(jnp.arange(groups) > 0, position > 0).astype(jnp.float32)
    query = jnp.dot(whole_hidden, wq_flat, preferred_element_type=jnp.float32).astype(jnp.bfloat16)
    query_g = shift_rows(query, span_len).reshape(groups, span_len, heads_here, head_dim)
    scores = (
        jnp.einsum("gqhd,gkhd->ghqk", query_g, keys, preferred_element_type=jnp.float32) * scale
    )
    expo = jnp.where(key_mask[:, None, None, :], jnp.exp(scores), 0.0)
    prob = expo / jnp.sum(expo, axis=-1, keepdims=True) * valid[:, None, None, None]
    prob_low = prob.astype(jnp.bfloat16)
    attn = jnp.einsum(
        "ghqk,gkhd->gqhd", prob_low, values, preferred_element_type=jnp.float32
    ).astype(jnp.bfloat16)
    attn_flat = attn.reshape(groups * span_len, inner)[1 : tok_rows + 1]
    out_part = contract_heads(attn_flat, wo_flat)
    d_attn = jnp.dot(whole_cot, wo_flat, preferred_element_type=jnp.float32).astype(jnp.bfloat16)
    d_group = shift_rows(d_attn, span_len).reshape(groups, span_len, heads_here, head_dim)
    d_prob = jnp.einsum("gqhd,gkhd->ghqk", d_group, values, preferred_element_type=jnp.float32)
    delta = jnp.sum(prob * d_prob, axis=-1, keepdims=True)
    d_score = (prob * (d_prob - delta) * scale).astype(jnp.bfloat16)
    d_query = jnp.einsum(
        "ghqk,gkhd->gqhd", d_score, keys, preferred_element_type=jnp.float32
    ).astype(jnp.bfloat16)
    d_flat = d_query.reshape(groups * span_len, inner)[1 : tok_rows + 1]
    grad_part = contract_heads(d_flat, wq_flat)
    out_sum, grad_sum = (
        lax.psum_scatter(out_part, "mp", scatter_dimension=1, tiled=True),
        lax.psum_scatter(grad_part, "mp", scatter_dimension=1, tiled=True),
    )
    cca_out = out_sum.astype(jnp.bfloat16)
    hidden_grad = grad_sum.astype(jnp.bfloat16)
    return (cca_out, hidden_grad)


def solution(mesh):
    return jax.shard_map(
        per_device,
        mesh=mesh,
        in_specs=(
            P("seq", "mp"),
            P("seq", "mp"),
            P("seq", None, None),
            P(),
            P("mp", None),
            P("mp", None),
            P("mp", None),
            P("seq", "mp", None),
            P("seq", "mp", None, None),
            P("seq", "mp", None),
        ),
        out_specs=(P("seq", "mp"), P("seq", "mp")),
        check_vma=False,
    )
```

profile of v0, /device:TPU:0, one launch (start us, length us, event | category | flops | bytes accessed | tf_op | source)
XLA Modules:
  0.0 645.5 jit_solution(16285558834734861596)
XLA Ops:
  9.6 17.5 %gather_fusion = bf16[1024,896]{1,0:T(8,128)(2,1)S(1)} fusion(bf16[16000,896]{1,0:T(8,128)(2,1)} %param.14, s32[1024]{0:T(1024)S(1)} %broadcast_clamp_fusion), kind=kCustom, calls=%fused_computation | custom fusion | bytes 3674112 | tf_op jit(solution)/shard_map/jit(_take)/gather | solution.py:51
  29.0 32.6 %reduce-scatter.5.cloned.1.call-done = bf16[256,896]{1,0:T(8,128)(2,1)} async-done(((bf16[1024,896]{1,0:T(8,128)(2,1)}), bf16[256,896]{1,0:T(8,128)(2,1)}) %reduce-scatter.5.cloned.1.call-update) | async-done | bytes 458768 | tf_op jit(solution)/shard_map/reduce_scatter | solution.py:54
  61.7 22.7 %all-gather.8.cloned.1.call-done = bf16[1024,896]{1,0:T(8,128)(2,1)} async-done(((bf16[256,896]{1,0:T(8,128)(2,1)}), bf16[1024,896]{1,0:T(8,128)(2,1)}) %all-gather.8.cloned.1.call-update) | async-done | bytes 1835024 | tf_op jit(solution)/shard_map/all_gather | solution.py:58
  84.4 1.9 multiply_reduce_fusion
  86.4 7.8 %fusion.51 = f32[1024,896]{1,0:T(8,128)} fusion(bf16[896,896]{1,0:T(8,128)(2,1)S(1)} %copy-done, bf16[896,896]{1,0:T(8,128)(2,1)S(1)} %copy-done.7, f32[1024]{0:T(1024)S(1)} %add_rsqrt_fusion, bf16[1024,896]{1,0:T(8,128)(2,1)} %all-gather.8.cloned.1.call-done), kind=kOutput, calls=%fused_computation.52 | convolution fusion | flops 3299344384 | bytes 8720384 | tf_op jit(solution)/shard_map/dot_general | solution.py:80
  98.8 2.1 convert_element_type.57
  100.9 34.7 %reduce-scatter.7.cloned.1.call-done = f32[256,896]{1,0:T(8,128)} async-done(((f32[1024,896]{1,0:T(8,128)}), f32[256,896]{1,0:T(8,128)}) %reduce-scatter.7.cloned.1.call-update) | async-done | bytes 917520 | tf_op jit(solution)/shard_map/reduce_scatter | solution.py:83
  137.3 2.4 multiply_convert_fusion.5
  140.3 23.5 %all-gather.12.cloned.1.call-done = bf16[896,8,2,128]{3,1,2,0:T(8,128)(2,1)} async-done(((bf16[112,8,2,128]{3,1,2,0:T(8,128)(2,1)}), bf16[896,8,2,128]{3,1,2,0:T(8,128)(2,1)}) %all-gather.12.cloned.1.call-update) | async-done | bytes 3670032 | tf_op jit(solution)/shard_map/all_gather | solution.py:65
  163.8 6.4 copy.33
  170.2 16.1 %all-gather.14.cloned.1.call-done = bf16[256,4096]{1,0:T(8,128)(2,1)} async-done(((bf16[256,1024]{1,0:T(8,128)(2,1)}), bf16[256,4096]{1,0:T(8,128)(2,1)}) %all-gather.14.cloned.1.call-update) | async-done | bytes 2097168 | tf_op jit(solution)/shard_map/all_gather | solution.py:60
  186.3 126.5 %all-gather.16.cloned.1.call-done = bf16[4096,8,128]{2,1,0:T(8,128)(2,1)} async-done(((bf16[512,8,128]{2,1,0:T(8,128)(2,1)}), bf16[4096,8,128]{2,1,0:T(8,128)(2,1)}) %all-gather.16.cloned.1.call-update) | async-done | bytes 8388624 | tf_op jit(solution)/shard_map/all_gather | solution.py:64
  312.9 6.3 fusion.39
  319.2 15.9 %all-gather.20.cloned.1.call-done = bf16[256,4096]{1,0:T(8,128)(2,1)} async-done(((bf16[256,1024]{1,0:T(8,128)(2,1)}), bf16[256,4096]{1,0:T(8,128)(2,1)}) %all-gather.20.cloned.1.call-update) | async-done | bytes 2097168 | tf_op jit(solution)/shard_map/all_gather | solution.py:61
  335.1 126.7 %all-gather.18.cloned.1.call-done = bf16[4096,8,128]{2,1,0:T(8,128)(2,1)} async-done(((bf16[512,8,128]{2,1,0:T(8,128)(2,1)}), bf16[4096,8,128]{2,1,0:T(8,128)(2,1)}) %all-gather.18.cloned.1.call-update) | async-done | bytes 8388624 | tf_op jit(solution)/shard_map/all_gather | solution.py:66
  461.8 6.3 fusion.42
  469.9 13.2 %all-gather.10.cloned.1.call-done = bf16[1024,896]{1,0:T(8,128)(2,1)} async-done(((bf16[256,896]{1,0:T(8,128)(2,1)}), bf16[1024,896]{1,0:T(8,128)(2,1)}) %all-gather.10.cloned.1.call-update) | async-done | bytes 1835024 | tf_op jit(solution)/shard_map/all_gather | solution.py:87
  484.2 3.4 collective-permute-start
  487.6 9.1 %convolution_convert_fusion = bf16[1024,2048]{1,0:T(8,128)(2,1)} fusion(bf16[1024,896]{1,0:T(8,128)(2,1)} %all-gather.10.cloned.1.call-done, bf16[896,2048]{0,1:T(8,128)(2,1)} %bitcast.79), kind=kOutput, calls=%fused_computation.16 | convolution fusion | flops 3760193536 | bytes 9699328 | tf_op jit(solution)/shard_map/dot_general | solution.py:88
  496.7 7.7 %concatenate.18 = bf16[4,256,8,2,128]{4,3,2,1,0:T(2,128)(2,1)} reshape(bf16[1024,2048]{1,0:T(8,128)(2,1)} %convolution_convert_fusion) | data formatting | bytes 8388608 | tf_op jit(solution)/shard_map/concatenate | solution.py:93
  504.4 3.3 convolution_convert_fusion.1
  509.0 3.5 copy_dynamic-update-slice_fusion
  512.6 2.9 fusion.24
  515.6 2.5 fusion.28
  518.1 19.0 %fusion.48 = bf16[5,64,8,128]{3,1,2,0:T(8,128)(2,1)S(1)} fusion(bf16[5,256,8,2,128]{4,1,2,0,3:T(8,128)(2,1)} %copy-done.3, f32[5,8,64,256]{3,2,1,0:T(8,128)} %fusion.24, f32[5,8,64,256]{3,2,1,0:T(8,128)} %get-tuple-element.5, f32[5]{0:T(128)S(1)} %or_convert_fusion, f32[5,8,64]{2,1,0:T(8,128)S(1)} %get-tuple-element.4, ...), kind=kOutput, calls=%fused_computation.50 | convolution fusion | flops 176622336 | bytes 13808640 | tf_op jit(solution)/shard_map/ghqk,gkhd->gqhd/dot_general | solution.py:123
  537.7 7.8 %fusion.5 = f32[256,4096]{1,0:T(8,128)} fusion(bf16[512,8,8,128]{3,2,1,0:T(8,128)(2,1)} %bitcast.93, bf16[320,1024]{1,0:T(8,128)(2,1)S(1)} %bitcast.85), kind=kOutput, calls=%fused_computation.6 | convolution fusion | flops 2147483648 | bytes 13107200 | tf_op jit(solution)/shard_map/dot_general | solution.py:25
  545.8 3.4 fusion.45
  549.7 8.5 %fusion.3 = f32[256,4096]{1,0:T(8,128)} fusion(bf16[512,8,8,128]{3,2,1,0:T(8,128)(2,1)} %bitcast.91, bf16[320,1024]{1,0:T(8,128)(2,1)S(1)} %bitcast.86), kind=kOutput, calls=%fused_computation.4 | convolution fusion | flops 2147483648 | bytes 13107200 | tf_op jit(solution)/shard_map/dot_general | solution.py:25
  558.3 30.9 %reduce-scatter.11.cloned.1.call-done = f32[256,1024]{1,0:T(8,128)} async-done(((f32[256,4096]{1,0:T(8,128)}), f32[256,1024]{1,0:T(8,128)}) %reduce-scatter.11.cloned.1.call-update) | async-done | bytes 1048592 | tf_op jit(solution)/shard_map/reduce_scatter | solution.py:130
  589.2 2.1 convert_element_type.73
  591.3 45.0 %reduce-scatter.9.cloned.1.call-done = f32[256,1024]{1,0:T(8,128)} async-done(((f32[256,4096]{1,0:T(8,128)}), f32[256,1024]{1,0:T(8,128)}) %reduce-scatter.9.cloned.1.call-update) | async-done | bytes 1048592 | tf_op jit(solution)/shard_map/reduce_scatter | solution.py:129
  636.3 2.1 convert_element_type.68
  (69 shorter events, 15.8 us)
Async XLA Ops:
  8.0 78.4 %copy-start = (bf16[896,896]{1,0:T(8,128)(2,1)S(1)}, bf16[896,896]{1,0:T(8,128)(2,1)}, u32[]{:S(2)}) copy-start(bf16[896,896]{1,0:T(8,128)(2,1)} %param.16) | copy-start | bytes 4816900
  8.0 53.6 %reduce-scatter.5.cloned.1.call-start = ((), (), s32[]{:S(2)}) async-start(), calls=%async_computation.4 | async-start | bytes 2293760 | tf_op jit(solution)/shard_map/reduce_scatter | solution.py:54
  28.9 57.4 %copy-start.7 = (bf16[896,896]{1,0:T(8,128)(2,1)S(1)}, bf16[896,896]{1,0:T(8,128)(2,1)}, u32[]{:S(2)}) copy-start(bf16[896,896]{1,0:T(8,128)(2,1)} %param.15) | copy-start | bytes 4816900
  29.0 55.4 %all-gather.8.cloned.1.call-start = ((), (), s32[]{:S(2)}) async-start(), calls=%async_computation.5 | async-start | bytes 2293760 | tf_op jit(solution)/shard_map/all_gather | solution.py:58
  61.6 74.0 %reduce-scatter.7.cloned.1.call-start = ((), (), s32[]{:S(2)}) async-start(), calls=%async_computation.6 | async-start | bytes 4587520 | tf_op jit(solution)/shard_map/reduce_scatter | solution.py:83
  94.2 1.0 copy-start.5
  94.2 4.6 copy-start.2
  94.2 69.6 %all-gather.12.cloned.1.call-start = ((), (), s32[]{:S(2)}) async-start(), calls=%async_computation.8 | async-start | bytes 4128768 | tf_op jit(solution)/shard_map/all_gather | solution.py:65
  96.1 90.3 %all-gather.14.cloned.1.call-start = ((), (), s32[]{:S(2)}) async-start(), calls=%async_computation.9 | async-start | bytes 2621440 | tf_op jit(solution)/shard_map/all_gather | solution.py:60
  96.7 216.2 %all-gather.16.cloned.1.call-start = ((), (), s32[]{:S(2)}) async-start(), calls=%async_computation.10 | async-start | bytes 9437184 | tf_op jit(solution)/shard_map/all_gather | solution.py:64
  97.2 237.9 %all-gather.20.cloned.1.call-start = ((), (), s32[]{:S(2)}) async-start(), calls=%async_computation.13 | async-start | bytes 2621440 | tf_op jit(solution)/shard_map/all_gather | solution.py:61
  98.0 363.8 %all-gather.18.cloned.1.call-start = ((), (), s32[]{:S(2)}) async-start(), calls=%async_computation.11 | async-start | bytes 9437184 | tf_op jit(solution)/shard_map/all_gather | solution.py:66
  98.7 384.4 %all-gather.10.cloned.1.call-start = ((), (), s32[]{:S(2)}) async-start(), calls=%async_computation.7 | async-start | bytes 2293760 | tf_op jit(solution)/shard_map/all_gather | solution.py:87
  100.9 39.0 %copy-start.6 = (s32[32,2]{0,1:T(2,128)S(1)}, s32[32,2]{0,1:T(2,128)}, u32[]{:S(2)}) copy-start(s32[32,2]{0,1:T(2,128)} %param.13) | copy-start | bytes 772
  139.7 449.5 %reduce-scatter.11.cloned.1.call-start = ((), (), s32[]{:S(2)}) async-start(), calls=%async_computation.14 | async-start | bytes 5242880 | tf_op jit(solution)/shard_map/reduce_scatter | solution.py:130
  484.2 20.2 %collective-permute-start = (bf16[256,896]{1,0:T(8,128)(2,1)S(1)}, bf16[256,896]{1,0:T(8,128)(2,1)S(1)}, u32[]{:S(2)}, u32[]{:S(2)}) collective-permute-start(bf16[256,896]{1,0:T(8,128)(2,1)S(1)} %slice.23), channel_id=1, source_target_pairs={{0,4},{4,8},{8,12},{12,16},{16,20},{20,24},{24,28},{1,5},{5,9},{9,... | collective-permute-start | bytes 1376264 | tf_op jit(solution)/shard_map/ppermute | solution.py:10
  512.5 3.0 copy-start.3
  512.6 3.0 copy-start.4
  545.5 90.8 %reduce-scatter.9.cloned.1.call-start = ((), (), s32[]{:S(2)}) async-start(), calls=%async_computation.12 | async-start | bytes 5242880 | tf_op jit(solution)/shard_map/reduce_scatter | solution.py:129
  558.3 80.1 %copy-start.1 = (bf16[896,896]{1,0:T(8,128)(2,1)S(1)}, bf16[896,896]{1,0:T(8,128)(2,1)}, u32[]{:S(2)}) copy-start(bf16[896,896]{1,0:T(8,128)(2,1)} %param.16) | copy-start | bytes 4816900
Sparse Core Ops, SparseCore 0:
  29.1 32.4 reduce-scatter.4
  63.2 21.1 all-gather.7
  94.3 41.2 reduce-scatter.6
  545.6 43.5 reduce-scatter.10
  591.7 44.5 reduce-scatter.8
Sparse Core Ops, SparseCore 1:
  97.5 66.3 all-gather.11
  165.3 21.0 all-gather.13
  188.3 124.5 all-gather.15
  314.5 20.6 all-gather.19
  337.3 124.5 all-gather.17
  464.0 19.1 all-gather.9
where the time goes:
time: 646 us
  waiting for transfers between devices  490 us (76%)
  matrix products  77 us (12%)
  local copies, waits for them, and re-layouts  41.9 us (6%)
  other arithmetic  16.2 us (3%)
  between operations  15.6 us (2%)
    all_gather x1, waiting for transfers between devices, per_device(): lax.all_gather(w_out, 'seq', axis=0, tiled=True)  127 us
    all_gather x1, waiting for transfers between devices, per_device(): lax.all_gather(w_query, 'seq', axis=0, tiled=True)  127 us
    reduce_scatter x1, waiting for transfers between devices, per_device(): lax.psum_scatter(out_part, 'mp', scatter_dimension=1, tiled=True)  45 us
    reduce_scatter x1, waiting for transfers between devices, per_device(): share = lax.psum_scatter(ffn_part, 'mp', scatter_dimension=0, tiled=True)  34.7 us
    reduce_scatter x1, waiting for transfers between devices, per_device(): lax.psum_scatter(masked, 'mp', scatter_dimension=0, tiled=True)  32.6 us
    reduce_scatter x1, waiting for transfers between devices, per_device(): lax.psum_scatter(grad_part, 'mp', scatter_dimension=1, tiled=True)  30.9 us
    all_gather x1, waiting for transfers between devices, per_device(): lax.all_gather(w_keyval, 'seq', axis=0, tiled=True)  23.5 us
    all_gather x1, waiting for transfers between devices, per_device(): emb = lax.all_gather(emb_share, 'mp', axis=0, tiled=True)  22.7 us
  transfers between devices with their start and end apart: 12, of which 11 were waited for; matrix products, arithmetic and copies ran while one was open for 9% of the time, Pallas kernels for 0%

commit v1 on v0

v1 whole, which is shorter than its diff:
```python
import functools

import jax
import jax.numpy as jnp
from jax import lax
from jax.experimental import pallas as pl
from jax.experimental.pallas import tpu as pltpu
from jax.sharding import Mesh
from jax.sharding import PartitionSpec as P

SEQ = ("zh", "zl", "x")
GROUP = ("zl", "y", "c")
VMEM = 62 * 1024 * 1024
F32 = jnp.float32
BF16 = jnp.bfloat16


def flip(shard, axis):
    return lax.ppermute(shard, axis, [(0, 1), (1, 0)])


def onward(shard, axis):
    count = lax.axis_size(axis)
    return lax.ppermute(shard, axis, [(i, (i + 1) % count) for i in range(count)])


def tie(value, *earlier):
    return lax.optimization_barrier((value,) + earlier)[0]


def rms_rows(values):
    return values * lax.rsqrt(jnp.mean(values * values, axis=-1, keepdims=True) + 1e-06)


def dot(left, right):
    return jnp.dot(left, right, preferred_element_type=F32)


def dot_t(left, right):
    return lax.dot_general(left, right, (((1,), (1,)), ((), ())), preferred_element_type=F32)


def call(kernel, grid, prefetch, operands, outs, scratch):
    arrays = [o[0] for o in operands]
    return pl.pallas_call(
        kernel,
        grid_spec=pltpu.PrefetchScalarGridSpec(
            num_scalar_prefetch=1,
            grid=grid,
            in_specs=[pl.BlockSpec(block, index) for _, block, index in operands],
            out_specs=[pl.BlockSpec(block, index) for _, block, index in outs],
            scratch_shapes=scratch,
        ),
        out_shape=[o[0] for o in outs],
        compiler_params=pltpu.CompilerParams(vmem_limit_bytes=VMEM),
        cost_estimate=pl.CostEstimate(flops=1, bytes_accessed=1, transcendentals=0),
    )(prefetch, *arrays)


def shape(dims, dtype):
    return jax.ShapeDtypeStruct(dims, dtype)


def whole_block(ndim):
    return lambda *_: (0,) * ndim


def pack_kernel(
    at_ref, q_ref, kv_ref, o_ref, h_ref, c_ref,
    other_qkv_ref, other_out_ref, own_ref, own_q_ref, own_kv_ref, own_out_ref, states_ref,
    q, kv, o,
):
    rows, inner = own_out_ref.shape
    kv_rows, heads, _, head_dim = kv_ref.shape
    q[...] = q_ref[...].reshape(q.shape)
    o[...] = o_ref[...].reshape(o.shape)
    kv[...] = kv_ref[...].reshape(kv.shape)

    def cut(of, start, size):
        return of[:, pl.ds(pl.multiple_of(start, head_dim), size)]

    def copy(which, q_dst, kv_dst, out_dst):
        q_dst[...] = cut(q, which * inner, inner)
        out_dst[...] = cut(o, which * inner, inner)
        for h in range(heads // 2):
            for i in range(2):
                piece = cut(kv, ((which * (heads // 2) + h) * 2 + i) * head_dim, head_dim)
                kv_dst[i * kv_rows : (i + 1) * kv_rows, h * head_dim : (h + 1) * head_dim] = piece

    zl = at_ref[0]
    kv_end = rows + 2 * kv_rows
    copy(1 - zl, other_qkv_ref.at[:rows], other_qkv_ref.at[rows:], other_out_ref)
    copy(zl, own_ref.at[:rows], own_ref.at[rows:kv_end], own_ref.at[kv_end:])
    copy(zl, own_q_ref, own_kv_ref, own_out_ref)
    states_ref[0] = h_ref[...]
    states_ref[1] = c_ref[...]


def pack(zl, w_query, w_keyval, w_out, hidden, cotangent):
    rows, heads, head_dim = w_query.shape
    kv_rows, inner = w_keyval.shape[0], heads // 2 * head_dim
    sizes = [rows + 2 * kv_rows, rows, 2 * rows + 2 * kv_rows, rows, 2 * kv_rows, rows]
    outs = [(n, inner) for n in sizes] + [(2,) + hidden.shape]
    return call(
        pack_kernel,
        (1,),
        zl.reshape(1),
        [(a, a.shape, whole_block(a.ndim)) for a in (w_query, w_keyval, w_out, hidden, cotangent)],
        [(shape(dims, BF16), dims, whole_block(len(dims))) for dims in outs],
        [pltpu.VMEM(dims, BF16) for dims in ((rows, 2 * inner), (kv_rows, 4 * inner), (rows, 2 * inner))],
    )


def place_kernel(jobs, count, through, at_ref, *refs):
    sources, out_ref, sems = refs[:count], refs[count + through], refs[-1]
    stage = refs[-2] if through else out_ref

    def dst(ref, i, rows, plane):
        to = pl.ds(pl.multiple_of(at_ref[i] * rows, 16), rows)
        return ref.at[to] if plane is None else ref.at[plane, to]

    copies = []
    for i, (source, start, rows, plane) in enumerate(jobs):
        src = sources[source].at[pl.ds(start, rows)]
        to = stage.at[pl.ds(i * rows, rows)] if through else dst(stage, i, rows, plane)
        copies.append(pltpu.make_async_copy(src, to, sems.at[i]))
    for copy in copies:
        copy.start()
    for copy in copies:
        copy.wait()
    if through:
        copies = []
        for i, (_, _, rows, plane) in enumerate(jobs):
            src = stage.at[pl.ds(i * rows, rows)]
            copies.append(pltpu.make_async_copy(src, dst(out_ref, i, rows, plane), sems.at[i]))
        for copy in copies:
            copy.start()
        for copy in copies:
            copy.wait()


def place(pieces, dims, base=None):
    sources = []
    for piece in pieces:
        if not any(piece[1] is a for a in sources):
            sources.append(piece[1])
    index = [next(i for i, a in enumerate(sources) if a is piece[1]) for piece in pieces]
    jobs = [(i, p[2], p[3], p[4]) for i, p in zip(index, pieces)]
    if any(rows % 16 for _, _, rows, _ in jobs):
        whole = jnp.zeros(dims, BF16) if base is None else base
        for (at, block, start, rows, plane) in pieces:
            block = block[start : start + rows]
            if plane is None:
                whole = lax.dynamic_update_slice(whole, block, (at * rows, 0))
            else:
                whole = lax.dynamic_update_slice(whole, block[None], (plane, at * rows, 0))
        return whole
    through = base is not None
    arrays = sources + [base] if through else sources
    scratch = [pltpu.SemaphoreType.DMA((len(jobs),))]
    if through:
        scratch.insert(0, pltpu.VMEM((len(jobs) * jobs[0][2], dims[-1]), BF16))
    out_spec = pl.BlockSpec(memory_space=pl.ANY) if through else pl.BlockSpec(dims, whole_block(len(dims)))
    return pl.pallas_call(
        functools.partial(place_kernel, jobs, len(sources), int(through)),
        grid_spec=pltpu.PrefetchScalarGridSpec(
            num_scalar_prefetch=1,
            grid=(1,),
            in_specs=[pl.BlockSpec(memory_space=pl.ANY)] * len(arrays),
            out_specs=out_spec,
            scratch_shapes=scratch,
        ),
        out_shape=shape(dims, BF16),
        input_output_aliases={len(arrays): 0} if through else {},
        compiler_params=pltpu.CompilerParams(vmem_limit_bytes=VMEM),
        cost_estimate=pl.CostEstimate(flops=1, bytes_accessed=1, transcendentals=0),
    )(jnp.stack([p[0] for p in pieces]).astype(jnp.int32), *arrays)


def project_kernel(span, first, last, at_ref, own_ref, other_ref, w_ref, *rest):
    out_ref, acc = rest[-2:]
    step = pl.program_id(0)
    toks, cols = own_ref.shape[0], acc.shape[1]
    rows = jnp.concatenate([own_ref[...], other_ref[...]], axis=0)
    part = dot(rows, w_ref[...])

    @pl.when(step == 0)
    def _():
        acc[...] = part if first else part + rest[0][...]

    @pl.when(step > 0)
    def _():
        acc[...] += part

    @pl.when(step == pl.num_programs(0) - 1)
    def _():
        if not last:
            out_ref[...] = acc[...]
            return
        front, back = jnp.zeros((1, cols), F32), jnp.zeros((span - 1, cols), F32)
        for s in range(2):
            own = acc[s * toks : (s + 1) * toks, :]
            out_ref[s] = jnp.concatenate([front, own, back], axis=0).astype(BF16)


def project(at, states, which, w, wide, span, last, before=None):
    toks, wm = states[1].shape[1:]
    cols, steps, per = w.shape[1], at.shape[0], wm // wide
    operands = [
        (states[0], (None, None, toks, wide), lambda i, at: (at[i] // per, which, 0, lax.rem(at[i], per))),
        (states[1], (None, toks, wide), lambda i, at: (at[i] // per, 0, lax.rem(at[i], per))),
        (w, (wide, cols), lambda i, at: (at[i], 0)),
    ]
    total = (2 * toks, cols)
    if before is not None:
        operands.append((before, total, whole_block(2)))
    out = shape((2, toks + span, cols), BF16) if last else shape(total, F32)
    return call(
        functools.partial(project_kernel, span, before is None, last),
        (steps,),
        at,
        operands,
        [(out, out.shape, whole_block(len(out.shape)))],
        [pltpu.VMEM(total, F32)],
    )[0]


def keyval_kernel(at_ref, own_ref, other_ref, w_ref, k_ref, v_ref):
    for turn, rows_ref in enumerate((own_ref, other_ref)):

        @pl.when(pl.program_id(0) == turn)
        def _():
            rows = rows_ref[...]
            k_ref[...] = dot(rows, w_ref[0]).astype(BF16)
            v_ref[...] = dot(rows, w_ref[1]).astype(BF16)


def keyval(at, own, other, w):
    count, width = own.shape
    inner = w.shape[2]
    out = (shape((2 * count, inner), BF16), (count, inner), lambda i, at: (i, 0))
    operands = [(a, a.shape, whole_block(a.ndim)) for a in (own, other, w)]
    return call(keyval_kernel, (2,), at, operands, [out, out], [])


def encode_kernel(at_ref, emb_ref, up_ref, down_ref, up2_ref, down2_ref, ffn_ref, own_ref, normed, acc):
    step = pl.program_id(0)

    @pl.when(step == 0)
    def _():
        normed[...] = rms_rows(emb_ref[...].astype(F32)).astype(BF16)

    part = 0.0
    for up, down in ((up_ref, down_ref), (up2_ref, down2_ref)):
        act = jax.nn.gelu(dot_t(normed[...], up[...])).astype(BF16)
        part = part + dot(act, down[...])

    @pl.when(step == 0)
    def _():
        acc[...] = part

    @pl.when(step > 0)
    def _():
        acc[...] += part

    @pl.when(step == pl.num_programs(0) - 1)
    def _():
        share = own_ref.shape[0]
        ffn_ref[...] = acc[...].astype(BF16)
        mine = pl.ds(pl.multiple_of(at_ref[0] * share, share), share)
        own_ref[...] = acc[mine, :] + emb_ref[mine, :].astype(F32)


def encode(y, emb, weights, share, tiles):
    count, width = emb.shape
    hidden = weights[0].shape[0]
    tile = hidden // tiles
    return call(
        encode_kernel,
        (tiles,),
        y.reshape(1),
        [(emb, emb.shape, whole_block(2))]
        + [(w, (tile, width), lambda i, at: (i, 0)) for w in weights],
        [
            (shape((count, width), BF16), (count, width), whole_block(2)),
            (shape((share, width), F32), (share, width), whole_block(2)),
        ],
        [pltpu.VMEM((count, width), BF16), pltpu.VMEM((count, width), F32)],
    )


def span_rows(halves, g, cols):
    parts = [half[0, :, g, :, cols] for half in halves]
    parts = [p.reshape(p.shape[0] * p.shape[1], p.shape[2]) for p in parts]
    return jnp.concatenate(parts, axis=0)


def attend_kernel(span, head_dim, at_ref, q_ref, k_ref, v_ref, k2_ref, v2_ref, attn_ref, prob_ref, stage):
    turn = pl.program_id(0)
    _, blocks, groups, piece, inner = k_ref.shape
    heads, keys_per = inner // head_dim, 2 * blocks * piece
    nlen = keys_per // 2
    scale = head_dim ** (-0.5)
    toks = attn_ref.shape[1]
    lane = lax.broadcasted_iota(jnp.int32, (span, keys_per), 1)
    key = lane
    for i in range(2 * blocks):
        start = at_ref[2 * groups * 3 + i]
        here = jnp.logical_and(lane >= i * piece, lane < (i + 1) * piece)
        key = jnp.where(here, lane + (start - i * piece), key)
    for g in range(groups):
        rows = pl.ds(g * span, span)
        for h in range(heads):
            cols = pl.ds(h * head_dim, head_dim)
            prob_ref[0, h, rows, :] = dot_t(q_ref[0, rows, cols], span_rows((k_ref, k2_ref), g, cols))
    for g in range(groups):
        rows = pl.ds(g * span, span)
        base = (turn * groups + g) * 3
        first, second, live = at_ref[base], at_ref[base + 1], at_ref[base + 2]
        mask = jnp.logical_or(key < first, jnp.logical_and(key >= nlen, key < nlen + second))
        weight = live.astype(F32)
        for h in range(heads):
            cols = pl.ds(h * head_dim, head_dim)
            expo = jnp.where(mask, jnp.exp(prob_ref[0, h, rows, :] * scale), 0.0)
            prob = expo * (weight / jnp.sum(expo, axis=-1, keepdims=True))
            prob_ref[0, h, rows, :] = prob
            stage[rows, cols] = dot(prob.astype(BF16), span_rows((v_ref, v2_ref), g, cols))
    attn_ref[0] = stage[1 : toks + 1, :].astype(BF16)


def backward_kernel(
    span, head_dim, at_ref, prob_ref, d_ref, k_ref, v_ref, k2_ref, v2_ref, dq_ref, stage, d_prob
):
    groups, inner = k_ref.shape[2], k_ref.shape[4]
    heads = inner // head_dim
    scale = head_dim ** (-0.5)
    toks = dq_ref.shape[1]
    for g in range(groups):
        rows = pl.ds(g * span, span)
        for h in range(heads):
            cols = pl.ds(h * head_dim, head_dim)
            d_prob[h, rows, :] = dot_t(d_ref[0, rows, cols], span_rows((v_ref, v2_ref), g, cols))
    for g in range(groups):
        rows = pl.ds(g * span, span)
        for h in range(heads):
            cols = pl.ds(h * head_dim, head_dim)
            prob, slope = prob_ref[0, h, rows, :], d_prob[h, rows, :]
            delta = jnp.sum(prob * slope, axis=-1, keepdims=True)
            d_score = (prob * (slope - delta) * scale).astype(BF16)
            stage[rows, cols] = dot(d_score, span_rows((k_ref, k2_ref), g, cols))
    dq_ref[0] = stage[1 : toks + 1, :].astype(BF16)


def over_shards(kernel, at, padded, kv, span, head_dim, prob):
    shards, rows, inner = padded.shape
    toks = rows - span
    keys_per = 2 * kv[0].shape[1] * kv[0].shape[3]
    heads = inner // head_dim
    def by_turn(ndim):
        return lambda s, at: (s,) + (0,) * (ndim - 1)

    probs = shape((shards, heads, rows, keys_per), F32)
    prob_spec = ((1, heads, rows, keys_per), by_turn(4))
    operands = [(padded, (1, rows, inner), by_turn(3))]
    operands += [(a, (1,) + a.shape[1:], by_turn(5)) for a in kv]
    outs = [(shape((shards, toks, inner), BF16), (1, toks, inner), by_turn(3))]
    scratch = [pltpu.VMEM((rows, inner), F32)]
    if prob is None:
        outs.append((probs,) + prob_spec)
    else:
        operands.insert(0, (prob,) + prob_spec)
        scratch.append(pltpu.VMEM(probs.shape[1:], F32))
    return call(functools.partial(kernel, span, head_dim), (shards,), at, operands, outs, scratch)


def sent_kernel(at_ref, rows_ref, w_ref, out_ref):
    out_ref[0] = dot_t(rows_ref[...], w_ref[...]).astype(BF16)


def kept_kernel(at_ref, rows_ref, w_ref, add_ref, both_ref, y_ref, zl_ref, own_ref):
    total = dot_t(rows_ref[...], w_ref[...]) + add_ref[0].astype(F32)
    toks = own_ref.shape[0]

    @pl.when(pl.program_id(0) == 0)
    def _():
        y_ref[...] = total[:toks].astype(BF16)
        both_ref[...] = total[toks:].astype(BF16)

    @pl.when(pl.program_id(0) == 1)
    def _():
        own_ref[...] = total[:toks]
        zl_ref[...] = total[toks:].astype(BF16)


CUTS = 1


def columns(at, rows, w, wm, add=None):
    count, inner = rows.shape
    cut = wm // CUTS
    operands = [
        (rows, rows.shape, whole_block(2)),
        (w, (cut, inner), lambda i, j, at: (at[i] * CUTS + j, 0)),
    ]
    moved = (1, count, cut), lambda i, j, at: (i, 0, j)
    if add is None:
        out = shape((2, count, wm), BF16)
        return call(sent_kernel, (2, CUTS), at, operands, [(out,) + moved], [])[0]
    operands.append((add,) + moved)
    half = (count // 2, wm)
    block = (count // 2, cut)
    early = lambda i, j, at: (0, jnp.where(i == 0, j, CUTS - 1))
    late = lambda i, j, at: (0, jnp.where(i == 0, 0, j))
    outs = [(shape(half, BF16), block, early)] * 2
    outs += [(shape(half, BF16), block, late), (shape(half, F32), block, late)]
    return call(kept_kernel, (2, CUTS), at, operands, outs, [])


def core_sums(rows, w):
    y, c = lax.axis_index("y"), lax.axis_index("c")
    ny = lax.axis_size("y")
    wm = w.shape[0] // (2 * ny)
    if ny != 2:
        return None
    return columns(jnp.stack([(1 - y) * 2 + (1 - c), y * 2 + (1 - c)]), rows, w, wm)


def sum_heads(rows, w, sent):
    zl, y, c = (lax.axis_index(name) for name in GROUP)
    ny = lax.axis_size("y")
    wm = w.shape[0] // (2 * ny)
    count = rows.shape[0]
    if ny != 2:
        rows = jnp.roll(rows, zl * (count // 2), axis=0)
        blocks = dot_t(rows, w).astype(BF16).reshape(2, count // 2, ny, 2, wm)
        blocks = blocks.transpose(0, 2, 3, 1, 4).reshape(ny * 2 * count, wm)
        return lax.psum_scatter(blocks, GROUP, scatter_dimension=0, tiled=True).astype(BF16), ()
    at = jnp.stack([(1 - y) * 2 + c, y * 2 + c])
    to_both, to_y, to_zl, own = columns(at, rows, w, wm, flip(sent, "c"))
    over_both = lax.ppermute(to_both, ("zl", "y"), [(i, 3 - i) for i in range(4)])
    over_y, over_zl = flip(to_y, "y"), flip(to_zl, "zl")
    total = own + over_zl.astype(F32) + over_y.astype(F32) + over_both.astype(F32)
    return total.astype(BF16), (to_both, to_y, to_zl)


def per_device(
    hidden,
    cotangent,
    neighbour_ids,
    neighbour_lengths,
    embed_table,
    enc_up,
    enc_down,
    w_query,
    w_keyval,
    w_out,
):
    zh, zl, x = (lax.axis_index(name) for name in SEQ)
    y, c = lax.axis_index("y"), lax.axis_index("c")
    nzh, ny = lax.axis_size("zh"), lax.axis_size("y")
    spans_here, neigh, nlen = neighbour_ids.shape
    toks = hidden.shape[0]
    span = toks // spans_here
    keys_per = neigh * nlen
    groups = spans_here + 1
    rows_here, heads_here, head_dim = w_query.shape
    heads = heads_here // 2
    inner = heads * head_dim
    kv_rows, enc_width = w_keyval.shape[0], embed_table.shape[1]
    seqs = 4 * nzh
    piece = keys_per // (2 * ny)

    qkv_rows = rows_here + 2 * kv_rows

    def shard_at(hop, at_zl, at_x):
        return (lax.rem(zh + (nzh - hop), nzh) * 2 + at_zl) * 2 + at_x

    packed = pack(zl, w_query, w_keyval, w_out, hidden, cotangent)
    other_qkv, other_out, own, own_q, own_kv, own_out, states = packed
    up2, down2 = flip(enc_up, "c"), flip(enc_down, "c")
    beside_qkv = flip(other_qkv, "zl")
    own_x = flip(own, "x")
    hop_q = onward(own_q, "zh")

    def gather_states(rows):
        return lax.all_gather(rows, ("y", "c"), axis=0, tiled=False)

    own_states = gather_states(states)

    ids = neighbour_ids.reshape(spans_here, 2, ny, piece).transpose(1, 2, 0, 3).reshape(-1)
    vocab_here = embed_table.shape[0]
    local_ids = tie(ids, other_qkv) - (y * 2 + c) * vocab_here
    inside = jnp.logical_and(local_ids >= 0, local_ids < vocab_here)
    clipped = jnp.clip(local_ids, 0, vocab_here - 1)
    picked = tie(embed_table.at[clipped].get(mode="promise_in_bounds"), hop_q, beside_qkv, up2, down2)
    half_rows = ids.shape[0] // 2

    def half_emb(core):
        rows = lax.dynamic_slice_in_dim(picked, core * half_rows, half_rows, 0)
        live = lax.dynamic_slice_in_dim(inside, core * half_rows, half_rows, 0)
        return jnp.where(live[:, None], rows, jnp.zeros((), BF16))

    emb_other = half_emb(1 - c)
    emb = tie(half_emb(c), own_x) + flip(emb_other, "c")

    beside_qkv, other_out, hop_q = (tie(a, emb) for a in (beside_qkv, other_out, hop_q))
    beside_qkv_x, hop_q_x = flip(beside_qkv, "x"), flip(hop_q, "x")
    hop_q2 = onward(beside_qkv[:rows_here], "zh")
    beside_out = flip(other_out, "zl")
    emb = emb + flip(emb, "y") if ny == 2 else lax.psum(emb, "y")
    emb = tie(emb, beside_qkv_x, hop_q_x, hop_q2, beside_out, own_states)

    own_kv, beside_out, hidden = (tie(a, emb) for a in (own_kv, beside_out, hidden))
    hop_kv = onward(own_kv, "zh")
    beside_out_x = flip(beside_out, "x")
    other_hidden = flip(hidden, "zl")
    share_rows = half_rows // ny
    ffn, share = encode(y, emb, [enc_up, enc_down, up2, down2], share_rows, 2)
    ffn = tie(ffn, hop_kv)
    hop_kv2 = onward(tie(beside_qkv, ffn)[rows_here:], "zh")
    if ny == 2:
        sent = lax.dynamic_slice_in_dim(ffn, (1 - y) * share_rows, share_rows, 0)
        share = share + flip(sent, "y").astype(F32)
    else:
        share = lax.psum_scatter(ffn, "y", scatter_dimension=0, tiled=True).astype(F32)
        share = share + lax.dynamic_slice_in_dim(emb, y * share_rows, share_rows, 0).astype(F32)
    encoded = rms_rows(tie(share, beside_out_x, other_hidden)).astype(BF16)

    other_hidden = gather_states(tie(other_hidden, encoded))
    before = lax.ppermute(encoded[share_rows - piece :], SEQ, [(i, i + 1) for i in range(seqs - 1)])
    encoded = jnp.concatenate([tie(before, hop_kv2), encoded], axis=0)
    hop_qkv = jnp.concatenate([tie(hop_q2, encoded), hop_kv, hop_kv2], axis=0)
    hop_qkv_x = flip(hop_qkv, "x")
    hop_out = onward(jnp.concatenate([tie(own_out, encoded), beside_out], axis=0), "zh")

    if ny == 2:
        corner = lax.ppermute(encoded, ("zl", "y"), [(i, 3 - i) for i in range(4)])
        over_y, over_zl = flip(encoded, "y"), flip(encoded, "zl")
        over_y = tie(over_y, hop_qkv_x)
        own_rows, other_rows = [encoded, over_y], [over_zl, tie(corner, hop_out)]
        ys = [y, 1 - y]
    else:
        own_rows = [lax.all_gather(encoded, "y", axis=0, tiled=True)]
        other_rows, over_y = [flip(own_rows[0], "zl")], own_rows[0]
        ys = [jnp.int32(i) for i in range(ny)]

    q_pieces, kv_pieces, out_pieces = [], [], []

    def add_kv(at, block, start):
        kv_pieces.append((at, block, start, kv_rows, 0))
        kv_pieces.append((at, block, start + kv_rows, kv_rows, 1))

    here, here_x = shard_at(0, zl, x), shard_at(0, zl, 1 - x)
    there, there_x = shard_at(0, 1 - zl, x), shard_at(0, 1 - zl, 1 - x)
    for at, block, start in ((here, own_q, 0), (here_x, own_x, 0), (there, beside_qkv, 0), (there_x, beside_qkv_x, 0)):
        q_pieces.append((at, block, start, rows_here, None))
    for at, block, start in (
        (here, own_kv, 0),
        (here_x, own_x, rows_here),
        (there, beside_qkv, rows_here),
        (there_x, beside_qkv_x, rows_here),
    ):
        add_kv(at, block, start)
    for at, block, start in ((here, own_out, 0), (here_x, own_x, qkv_rows), (there, beside_out, 0), (there_x, beside_out_x, 0)):
        out_pieces.append((at, block, start, rows_here, None))
    for hop in range(1, nzh):
        if hop > 1:
            hop_q, hop_qkv = onward(hop_q, "zh"), onward(hop_qkv, "zh")
            hop_q_x, hop_qkv_x = flip(hop_q, "x"), flip(hop_qkv, "x")
        for at_x, at_q, at_qkv in ((x, hop_q, hop_qkv), (1 - x, hop_q_x, hop_qkv_x)):
            here, there = shard_at(hop, zl, at_x), shard_at(hop, 1 - zl, at_x)
            q_pieces += [(here, at_q, 0, rows_here, None), (there, at_qkv, 0, rows_here, None)]
            add_kv(here, at_qkv, rows_here)
            add_kv(there, at_qkv, qkv_rows)

    lens_pad = jnp.concatenate([jnp.ones((1, neigh), jnp.int32), neighbour_lengths], axis=0)
    at = []
    for turn in range(2):
        first = ((zh * 2 + lax.rem(zl + turn, 2)) * 2 + x) * spans_here
        rows = lax.dynamic_slice_in_dim(lens_pad, first, groups, 0)
        live = (first + jnp.arange(groups, dtype=jnp.int32) > 0).astype(jnp.int32)
        at.append(jnp.concatenate([rows, live[:, None]], axis=1).reshape(-1))
    starts = [(core * ny + at_y) * piece for core in (c, 1 - c) for at_y in ys]
    at = jnp.concatenate(at + [jnp.stack(starts).astype(jnp.int32)])

    w_dims = (seqs * rows_here, inner)
    q_pieces[0] = (q_pieces[0][0], tie(q_pieces[0][1], over_y)) + q_pieces[0][2:]
    kv_pieces[0] = (kv_pieces[0][0], tie(kv_pieces[0][1], over_y)) + kv_pieces[0][2:]
    wkv = place(kv_pieces, (2, enc_width, inner))
    own_rows = jnp.concatenate(own_rows, axis=0)
    own_rows2 = flip(own_rows, "c")
    other_rows = jnp.concatenate([tie(other_rows[0], wkv)] + other_rows[1:], axis=0)
    other_rows2 = flip(other_rows, "c")
    hop_out = tie(hop_out, other_rows)
    hop_out_x = flip(hop_out, "x")
    other_cot = flip(tie(cotangent, other_rows), "zl")
    wq = place(q_pieces, w_dims)
    every = jnp.arange(2 * ny, dtype=jnp.int32)
    kv_shape = (2, ny, groups, piece, inner)
    keys, values = keyval(at, own_rows, other_rows, wkv)
    other_cot = gather_states(tie(other_cot, keys))
    other_rows2 = tie(other_rows2, keys)
    keys2, values2 = keyval(at, own_rows2, other_rows2, wkv)
    query = project(every, (own_states, other_hidden), 0, tie(wq, keys2), hidden.shape[1], span, True)
    kv = [a.reshape(kv_shape) for a in (keys, values, keys2, values2)]
    attn, prob = over_shards(attend_kernel, at, query, kv, span, head_dim, None)
    attn = attn.reshape(2 * toks, inner)

    late = []
    for hop in range(1, nzh):
        if hop > 1:
            hop_out = onward(hop_out, "zh")
            hop_out_x = flip(hop_out, "x")
        for at_x, block in ((x, hop_out), (1 - x, hop_out_x)):
            late.append((shard_at(hop, zl, at_x), block, 0, rows_here, None))
            late.append((shard_at(hop, 1 - zl, at_x), block, rows_here, rows_here, None))

    def at_of(pieces):
        return jnp.stack([p[0] for p in pieces])

    states = (own_states, other_cot)
    wo = place(out_pieces, w_dims)
    some = project(at_of(out_pieces), states, 1, tie(wo, attn), rows_here, span, False)
    hop_out_x = tie(hop_out_x, some)
    late[-2:] = [(p[0], hop_out_x) + p[2:] for p in late[-2:]]
    wo = place(late, w_dims, wo)
    out_sent = core_sums(attn, wo)
    if out_sent is not None:
        some = tie(some, out_sent)
    d_attn = project(at_of(late), states, 1, wo, rows_here, span, True, some)
    cca_out, moved = sum_heads(tie(attn, d_attn), wo, out_sent)
    (d_query,) = over_shards(backward_kernel, at, tie(d_attn, *moved), kv, span, head_dim, prob)
    d_query = d_query.reshape(2 * toks, inner)
    hidden_grad, _ = sum_heads(d_query, wq, core_sums(d_query, wq))
    return (cca_out, hidden_grad)


def solution(mesh):
    ns, nm = mesh.shape["seq"], mesh.shape["mp"]
    fine = Mesh(mesh.devices.reshape(ns // 4, 2, 2, nm // 2, 2), ("zh", "zl", "x", "y", "c"))
    seq, mp = SEQ, ("y", "c")
    return jax.shard_map(
        per_device,
        mesh=fine,
        in_specs=(
            P(seq, mp),
            P(seq, mp),
            P(seq, None, None),
            P(),
            P(mp, None),
            P(mp, None),
            P(mp, None),
            P(seq, mp, None),
            P(seq, mp, None, None),
            P(seq, mp, None),
        ),
        out_specs=(P(seq, mp), P(seq, mp)),
        check_vma=False,
    )
```

time: 646 us -> 323 us (0.50)
  waiting for transfers between devices: 490 us -> 123 us
  Pallas kernels: 0 us -> 95.2 us
  matrix products: 77 us -> 0 us
  starting transfers between devices: 4.29 us -> 47 us
  local copies, waits for them, and re-layouts: 41.9 us -> 31.2 us
    all_gather x7 -> x3, waiting for transfers between devices: 345 us -> 0.01 us  [gather_states(): return lax.all_gather(rows, ('y', 'c'), axis=0, tiled=False)]
    reduce_scatter x4 -> x0, waiting for transfers between devices: 143 us -> none  [the longest x1 45 us: per_device(): lax.psum_scatter(out_part, 'mp', scatter_dimension=1, tiled=True)]
    ppermute x1 -> x34, waiting for transfers between devices: 0.01 us -> 123 us  [the longest x25 82.3 us: flip(): return lax.ppermute(shard, axis, [(0, 1), (1, 0)])]
    pallas_call x0 -> x17, Pallas kernels: none -> 95.2 us  [the longest x13 78.9 us: call(): pl.pallas_call(kernel, grid_spec=pltpu.PrefetchScalarGridSpec(num_scalar_...]
    dot_general x11 -> x0, matrix products: 77 us -> none  [the longest x1 19 us: per_device(): jnp.einsum('ghqk,gkhd->gqhd', d_score, keys, preferred_element_type=jnp.f...]
    ppermute x1 -> x34, starting transfers between devices: 3.4 us -> 46.9 us  [the longest x25 23.6 us: flip(): return lax.ppermute(shard, axis, [(0, 1), (1, 0)])]
    concatenate x5, local copies, waits for them, and re-layouts: 12.3 us -> 2.8 us  [the longest x1 1.92 us: per_device(): jnp.concatenate([tie(other_rows[0], wkv)] + other_rows[1:], axis=0)]
  transfers between devices with their start and end apart: 12 -> 37, of which waited for: 11 -> 22; matrix products, arithmetic and copies ran while one was open for 9% -> 12% of each run, Pallas kernels for 0% -> 21%
where the time goes in v1:
time: 323 us; the launch traced here: 322 us
  waiting for transfers between devices  123 us (38%)
  Pallas kernels  95.2 us (29%)
  starting transfers between devices  47 us (15%)
  local copies, waits for them, and re-layouts  31.2 us (10%)
  between operations  14.1 us (4%)
  other arithmetic  12.1 us (4%)
    ppermute x25, waiting for transfers between devices, flip(): return lax.ppermute(shard, axis, [(0, 1), (1, 0)])  82.3 us
    pallas_call x13, Pallas kernels, call(): pl.pallas_call(kernel, grid_spec=pltpu.PrefetchScalarGridSpec(num_scalar_...  78.9 us
    ppermute x25, starting transfers between devices, flip(): return lax.ppermute(shard, axis, [(0, 1), (1, 0)])  23.6 us
    gather x1, local copies, waits for them, and re-layouts, per_device(): embed_table.at[clipped].get(mode='promise_in_bounds')  18.9 us
    ppermute x5, waiting for transfers between devices, onward(): lax.ppermute(shard, axis, [(i, (i + 1) % count) for i in range(count)])  16.8 us
    pallas_call x4, Pallas kernels, place(): pl.pallas_call(functools.partial(place_kernel, jobs, len(sources), int(th...  16.3 us
    ppermute x5, starting transfers between devices, onward(): lax.ppermute(shard, axis, [(i, (i + 1) % count) for i in range(count)])  14.9 us
    ppermute x1, waiting for transfers between devices, per_device(): corner = lax.ppermute(encoded, ('zl', 'y'), [(i, 3 - i) for i in range(4)])  11.9 us
  transfers between devices with their start and end apart: 37, of which 22 were waited for; matrix products, arithmetic and copies ran while one was open for 12% of the time, Pallas kernels for 21%

profile of v1, /device:TPU:0, one launch (start us, length us, event | category | flops | bytes accessed | tf_op | source)
XLA Modules:
  0.0 322.5 jit_solution(319062307334198995)
XLA Ops:
  7.2 4.6 %shard_map.113 = (bf16[736,512]{1,0:T(8,128)(2,1)}, bf16[512,512]{1,0:T(8,128)(2,1)}, bf16[1248,512]{1,0:T(8,128)(2,1)}, bf16[512,512]{1,0:T(8,128)(2,1)}, bf16[...) custom-call(s32[1]{0:T(128)} %bitcast.6.at_ref, bf16[512,8,128]{2,1,0:T(8,128)(2,1)} %q_ref.1, ...), custom_call_target="tpu_custom_call" | custom-call | flops 1 | bytes 1 | tf_op jit(solution)/shard_map/pallas_call | solution.py:45
  19.7 18.9 %gather_fusion = bf16[1024,896]{1,0:T(8,128)(2,1)S(1)} fusion(bf16[16000,896]{1,0:T(8,128)(2,1)} %param.14, s32[1024]{0:T(1024)S(1)} %fusion), kind=kCustom, calls=%fused_computation | custom fusion | bytes 3674112 | tf_op jit(solution)/shard_map/gather | solution.py:495
  38.7 4.6 %collective-permute-done.refs_4_ = bf16[512,512]{1,0:T(8,128)(2,1)} collective-permute-done((bf16[512,512]{1,0:T(8,128)(2,1)}, bf16[512,512]{1,0:T(8,128)(2,1)}, u32[]{:S(2)}, u32[]{:S(2)}) %collective-permute-start) | collective-permute-done | bytes 524320 | tf_op jit(solution)/shard_map/ppermute | solution.py:24
  56.4 13.4 %collective-permute-done.6 = bf16[512,896]{1,0:T(8,128)(2,1)S(1)} collective-permute-done((bf16[512,896]{1,0:T(8,128)(2,1)S(1)}, bf16[512,896]{1,0:T(8,128)(2,1)S(1)}, u32[]{:S(2)}, u32[]{:S(2)}) %collective-permute-start.6) | collective-permute-done | bytes 917536 | tf_op jit(solution)/shard_map/ppermute | solution.py:19
  71.0 6.3 %collective-permute-done.9 = bf16[512,512]{1,0:T(8,128)(2,1)S(1)} collective-permute-done((bf16[512,512]{1,0:T(8,128)(2,1)S(1)}, bf16[512,512]{1,0:T(8,128)(2,1)S(1)}, u32[]{:S(2)}, u32[]{:S(2)}) %collective-permute-start.9) | collective-permute-done | bytes 524320 | tf_op jit(solution)/shard_map/ppermute | solution.py:24
  82.5 9.4 %shard_map.114 = (bf16[512,896]{1,0:T(8,128)(2,1)}, f32[256,896]{1,0:T(8,128)}) custom-call(s32[1]{0:T(128)} %bitcast.9.at_ref, bf16[512,896]{1,0:T(8,128)(2,1)} %add.215.emb_ref, bf16[896,896]{1,0:T(8,128)(2,1)} %up_ref.1, bf16[896,896]{1,0:T(8,128)(2,1)} %down_ref.1, bf16[896,896]{1,0:T(8,128)(2,1)} %collective-permute-done.2.up2_ref, ...), custom_call_target="tpu_custom_call" | custom-call | flops 1 | bytes 1 | tf_op jit(solution)/shard_map/pallas_call | solution.py:45
  96.8 7.4 %collective-permute-done.13 = bf16[256,896]{1,0:T(8,128)(2,1)S(1)} collective-permute-done((bf16[256,896]{1,0:T(8,128)(2,1)S(1)}, bf16[256,896]{1,0:T(8,128)(2,1)S(1)}, u32[]{:S(2)}, u32[]{:S(2)}) %collective-permute-start.13) | collective-permute-done | bytes 458784 | tf_op jit(solution)/shard_map/ppermute | solution.py:19
  112.8 3.6 %collective-permute-start.15 = (bf16[64,896]{1,0:T(8,128)(2,1)S(1)}, bf16[64,896]{1,0:T(8,128)(2,1)S(1)}, u32[]{:S(2)}, u32[]{:S(2)}) collective-permute-start(bf16[64,896]{1,0:T(8,128)(2,1)S(1)} %slice.14), channel_id=1, source_target_pairs={{0,4},{4,8},{8,12},{12,16},{16,20},{20,24},{24,28},{1,5},{5,9},{9,... | collective-permute-start | bytes 344072 | tf_op jit(solution)/shard_map/ppermute | solution.py:530
  116.4 5.6 %collective-permute-done.16 = bf16[224,512]{1,0:T(8,128)(2,1)S(1)} collective-permute-done((bf16[224,512]{1,0:T(8,128)(2,1)S(1)}, bf16[224,512]{1,0:T(8,128)(2,1)S(1)}, u32[]{:S(2)}, u32[]{:S(2)}) %collective-permute-start.16) | collective-permute-done | bytes 229408 | tf_op jit(solution)/shard_map/ppermute | solution.py:24
  126.7 4.3 %collective-permute-start.22 = (bf16[1024,512]{1,0:T(8,128)(2,1)}, bf16[1024,512]{1,0:T(8,128)(2,1)}, u32[]{:S(2)}, u32[]{:S(2)}) collective-permute-start(bf16[1024,512]{1,0:T(8,128)(2,1)} %pad_maximum_fusion.1), channel_id=1, source_target_pairs={{0,16},{16,0},{1,17},{17,1},{2,18},{18,2},{3,19},{19,3},{4,20},{20... | collective-permute-start | bytes 3145736 | tf_op jit(solution)/shard_map/ppermute | solution.py:24
  135.0 11.1 %collective-permute-done.17 = bf16[320,896]{1,0:T(8,128)(2,1)S(1)} collective-permute-done((bf16[320,896]{1,0:T(8,128)(2,1)}, bf16[320,896]{1,0:T(8,128)(2,1)S(1)}, u32[]{:S(2)}, u32[]{:S(2)}) %collective-permute-start.17) | collective-permute-done | bytes 573472 | tf_op jit(solution)/shard_map/ppermute | solution.py:19
  147.3 3.6 %shard_map.116.w_ref = bf16[2,896,512]{2,1,0:T(8,128)(2,1)} custom-call(s32[16]{0:T(128)} %stack.60.at_ref, bf16[224,512]{1,0:T(8,128)(2,1)} %get-tuple-element.83.refs_0_.refs_1_, bf16[224,512]{1,0:T(8,128)(2,1)} %get-tuple-element.83.refs_0_.refs_1_, bf16[1248,512]{1,0:T(8,128)(2,1)} %copy-done, bf16[736,512]{1,0:T(8,128)(2,1)} %collective-permute-done.1.refs_2_.refs_3_, ...), custom_call_target="tpu_custom_call" | custom-call | flops 1 | bytes 1 | tf_op jit(solution)/shard_map/pallas_call | solution.py:164
  150.9 16.2 %collective-permute-done.20 = bf16[320,896]{1,0:T(8,128)(2,1)} collective-permute-done((bf16[320,896]{1,0:T(8,128)(2,1)}, bf16[320,896]{1,0:T(8,128)(2,1)}, u32[]{:S(2)}, u32[]{:S(2)}) %collective-permute-start.20) | collective-permute-done | bytes 573472 | tf_op jit(solution)/shard_map/ppermute | solution.py:19
  169.1 11.9 %collective-permute-done.21 = bf16[320,896]{1,0:T(8,128)(2,1)} collective-permute-done((bf16[320,896]{1,0:T(8,128)(2,1)}, bf16[320,896]{1,0:T(8,128)(2,1)}, u32[]{:S(2)}, u32[]{:S(2)}) %collective-permute-start.21) | collective-permute-done | bytes 573472 | tf_op jit(solution)/shard_map/ppermute | solution.py:537
  185.6 7.2 %shard_map.117 = (bf16[1280,512]{1,0:T(8,128)(2,1)}, bf16[1280,512]{1,0:T(8,128)(2,1)}) custom-call(s32[34]{0:T(128)} %concatenate.31.at_ref, bf16[640,896]{1,0:T(8,128)(2,1)} %pad_maximum_fusion.own_ref, bf16[640,896]{1,0:T(8,128)(2,1)} %constant_dynamic-update-slice_fusion.3.other_ref, bf16[2,896,512]{2,1,0:T(8,128)(2,1)} %shard_map.116.w_ref), custom_call_target="tpu_custom_call" | custom-call | flops 1 | bytes 1 | tf_op jit(solution)/shard_map/pallas_call | solution.py:45
  199.5 4.4 %shard_map.121.w_ref.refs_2_ = bf16[4096,512]{1,0:T(8,128)(2,1)} custom-call(s32[4]{0:T(128)} %pad_add_fusion.4.at_ref, bf16[512,512]{1,0:T(8,128)(2,1)} %get-tuple-element.86.refs_0_, bf16[1248,512]{1,0:T(8,128)(2,1)} %copy-done, bf16[512,512]{1,0:T(8,128)(2,1)} %copy-done.4, bf16[512,512]{1,0:T(8,128)(2,1)} %copy-done.9), custom_call_target="tpu_custom_call" | custom-call | flops 1 | bytes 1 | tf_op jit(solution)/shard_map/pallas_call | solution.py:164
  203.8 4.9 %shard_map.115.w_ref = bf16[4096,512]{1,0:T(8,128)(2,1)} custom-call(s32[8]{0:T(128)} %stack.59.at_ref, bf16[512,512]{1,0:T(8,128)(2,1)} %get-tuple-element.82.refs_0_, bf16[1248,512]{1,0:T(8,128)(2,1)} %copy-done, bf16[736,512]{1,0:T(8,128)(2,1)} %collective-permute-done.1.refs_2_.refs_3_, bf16[736,512]{1,0:T(8,128)(2,1)} %collective-permute-done.7.refs_3_.refs_4_, ...), custom_call_target="tpu_custom_call" | custom-call | flops 1 | bytes 1 | tf_op jit(solution)/shard_map/pallas_call | solution.py:164
  208.7 7.0 %shard_map.118 = (bf16[1280,512]{1,0:T(8,128)(2,1)}, bf16[1280,512]{1,0:T(8,128)(2,1)}) custom-call(s32[34]{0:T(128)} %concatenate.31.at_ref, bf16[640,896]{1,0:T(8,128)(2,1)} %collective-permute-done.19.own_ref, bf16[640,896]{1,0:T(8,128)(2,1)} %collective-permute-done.23.other_ref, bf16[2,896,512]{2,1,0:T(8,128)(2,1)} %shard_map.116.w_ref), custom_call_target="tpu_custom_call" | custom-call | flops 1 | bytes 1 | tf_op jit(solution)/shard_map/pallas_call | solution.py:45
  216.3 7.3 %shard_map.119.q_ref = bf16[2,320,512]{2,1,0:T(8,128)(2,1)} custom-call(s32[4]{0:T(128)} %iota.13.at_ref, bf16[4,2,256,1024]{3,2,1,0:T(8,128)(2,1)} %bitcast.30, bf16[4,256,1024]{2,1,0:T(8,128)(2,1)} %bitcast.45, bf16[4096,512]{1,0:T(8,128)(2,1)} %shard_map.115.w_ref), custom_call_target="tpu_custom_call" | custom-call | flops 1 | bytes 1 | tf_op jit(solution)/shard_map/pallas_call | solution.py:45
  223.6 5.4 %shard_map.120 = (bf16[2,256,512]{2,1,0:T(8,128)(2,1)}, f32[2,4,320,256]{3,2,1,0:T(8,128)}) custom-call(s32[34]{0:T(128)} %concatenate.31.at_ref, bf16[2,320,512]{2,1,0:T(8,128)(2,1)} %shard_map.119.q_ref, bf16[2,2,5,64,512]{4,3,2,1,0:T(8,128)(2,1)} %bitcast.35, bf16[2,2,5,64,512]{4,3,2,1,0:T(8,128)(2,1)} %bitcast.37, bf16[2,2,5,64,512]{4,3,2,1,0:T(8,128)(2,1)} %bitcast.39, ...), custom_call_target="tpu_custom_call" | custom-call | flops 1 | bytes 1 | tf_op jit(solution)/shard_map/pallas_call | solution.py:45
  229.0 5.9 %shard_map.122.rest_0_ = f32[512,512]{1,0:T(8,128)} custom-call(s32[4]{0:T(128)} %pad_add_fusion.4.at_ref, bf16[4,2,256,1024]{3,2,1,0:T(8,128)(2,1)} %bitcast.31, bf16[4,256,1024]{2,1,0:T(8,128)(2,1)} %bitcast.33, bf16[4096,512]{1,0:T(8,128)(2,1)} %shard_map.121.w_ref.refs_2_), custom_call_target="tpu_custom_call" | custom-call | flops 1 | bytes 1 | tf_op jit(solution)/shard_map/pallas_call | solution.py:45
  234.9 3.5 %shard_map.123.w_ref = bf16[4096,512]{1,0:T(8,128)(2,1)} custom-call(s32[4]{0:T(128)} %pad_add_fusion.3.at_ref, bf16[1024,512]{1,0:T(8,128)(2,1)} %collective-permute-done.22.refs_0_, bf16[1024,512]{1,0:T(8,128)(2,1)} %collective-permute-done.25.refs_1_, bf16[4096,512]{1,0:T(8,128)(2,1)} %shard_map.121.w_ref.refs_2_), custom_call_target="tpu_custom_call", output_to_operand_aliasing={{}: (3, {})} | custom-call | flops 1 | bytes 1 | tf_op jit(solution)/shard_map/pallas_call | solution.py:164
  238.5 4.5 %shard_map.124 = bf16[2,512,1024]{2,1,0:T(8,128)(2,1)} custom-call(s32[2]{0:T(128)} %pad_add_fusion.5.at_ref, bf16[512,512]{1,0:T(8,128)(2,1)} %bitcast.46, bf16[4096,512]{1,0:T(8,128)(2,1)} %shard_map.123.w_ref), custom_call_target="tpu_custom_call" | custom-call | flops 1 | bytes 1 | tf_op jit(solution)/shard_map/pallas_call | solution.py:45
  243.6 6.2 %shard_map.125.d_ref = bf16[2,320,512]{2,1,0:T(8,128)(2,1)} custom-call(s32[4]{0:T(128)} %pad_add_fusion.3.at_ref, bf16[4,2,256,1024]{3,2,1,0:T(8,128)(2,1)} %bitcast.32, bf16[4,256,1024]{2,1,0:T(8,128)(2,1)} %bitcast.34, bf16[4096,512]{1,0:T(8,128)(2,1)} %shard_map.123.w_ref, f32[512,512]{1,0:T(8,128)} %shard_map.122.rest_0_), custom_call_target="tpu_custom_call" | custom-call | flops 1 | bytes 1 | tf_op jit(solution)/shard_map/pallas_call | solution.py:45
  249.8 5.6 %shard_map.126 = (bf16[256,1024]{1,0:T(8,128)(2,1)}, bf16[256,1024]{1,0:T(8,128)(2,1)}, bf16[256,1024]{1,0:T(8,128)(2,1)}, f32[256,1024]{1,0:T(8,128)}) custom-call(s32[2]{0:T(128)} %pad_add_fusion.2.at_ref, bf16[512,512]{1,0:T(8,128)(2,1)} %bitcast.47, bf16[4096,512]{1,0:T(8,128)(2,1)} %shard_map.123.w_ref, ...), custom_call_target="tpu_custom_call" | custom-call | flops 1 | bytes 1 | tf_op jit(solution)/shard_map/pallas_call | solution.py:45
  255.4 5.6 %shard_map.127 = bf16[2,256,512]{2,1,0:T(8,128)(2,1)} custom-call(s32[34]{0:T(128)} %concatenate.31.at_ref, f32[2,4,320,256]{3,2,1,0:T(8,128)} %get-tuple-element.106.prob_ref, bf16[2,320,512]{2,1,0:T(8,128)(2,1)} %shard_map.125.d_ref, bf16[2,2,5,64,512]{4,3,2,1,0:T(8,128)(2,1)} %bitcast.36, bf16[2,2,5,64,512]{4,3,2,1,0:T(8,128)(2,1)} %bitcast.38, ...), custom_call_target="tpu_custom_call" | custom-call | flops 1 | bytes 1 | tf_op jit(solution)/shard_map/pallas_call | solution.py:45
  261.1 4.5 %shard_map.128 = bf16[2,512,1024]{2,1,0:T(8,128)(2,1)} custom-call(s32[2]{0:T(128)} %pad_add_fusion.5.at_ref, bf16[512,512]{1,0:T(8,128)(2,1)} %bitcast.43, bf16[4096,512]{1,0:T(8,128)(2,1)} %shard_map.115.w_ref), custom_call_target="tpu_custom_call" | custom-call | flops 1 | bytes 1 | tf_op jit(solution)/shard_map/pallas_call | solution.py:45
  270.3 5.6 %shard_map.129 = (bf16[256,1024]{1,0:T(8,128)(2,1)}, bf16[256,1024]{1,0:T(8,128)(2,1)}, bf16[256,1024]{1,0:T(8,128)(2,1)}, f32[256,1024]{1,0:T(8,128)}) custom-call(s32[2]{0:T(128)} %pad_add_fusion.2.at_ref, bf16[512,512]{1,0:T(8,128)(2,1)} %bitcast.44, bf16[4096,512]{1,0:T(8,128)(2,1)} %shard_map.115.w_ref, ...), custom_call_target="tpu_custom_call" | custom-call | flops 1 | bytes 1 | tf_op jit(solution)/shard_map/pallas_call | solution.py:45
  277.6 3.6 %collective-permute-done.27 = bf16[256,1024]{1,0:T(8,128)(2,1)S(1)} collective-permute-done((bf16[256,1024]{1,0:T(8,128)(2,1)}, bf16[256,1024]{1,0:T(8,128)(2,1)S(1)}, u32[]{:S(2)}, u32[]{:S(2)}) %collective-permute-start.27) | collective-permute-done | bytes 524320 | tf_op jit(solution)/shard_map/ppermute | solution.py:19
  282.3 10.5 %collective-permute-done.28 = bf16[256,1024]{1,0:T(8,128)(2,1)} collective-permute-done((bf16[256,1024]{1,0:T(8,128)(2,1)}, bf16[256,1024]{1,0:T(8,128)(2,1)}, u32[]{:S(2)}, u32[]{:S(2)}) %collective-permute-start.28) | collective-permute-done | bytes 524320 | tf_op jit(solution)/shard_map/ppermute | solution.py:19
  295.7 8.0 %collective-permute-done.31 = bf16[256,1024]{1,0:T(8,128)(2,1)S(1)} collective-permute-done((bf16[256,1024]{1,0:T(8,128)(2,1)}, bf16[256,1024]{1,0:T(8,128)(2,1)S(1)}, u32[]{:S(2)}, u32[]{:S(2)}) %collective-permute-start.31) | collective-permute-done | bytes 524320 | tf_op jit(solution)/shard_map/ppermute | solution.py:19
  303.7 11.1 %collective-permute-done.33 = bf16[256,1024]{1,0:T(8,128)(2,1)S(1)} collective-permute-done((bf16[256,1024]{1,0:T(8,128)(2,1)}, bf16[256,1024]{1,0:T(8,128)(2,1)S(1)}, u32[]{:S(2)}, u32[]{:S(2)}) %collective-permute-start.33) | collective-permute-done | bytes 524320 | tf_op jit(solution)/shard_map/ppermute | solution.py:440
  (150 shorter events, 76.7 us)
Async XLA Ops:
  7.2 72.8 %all-gather.7.cloned.1.call-start = ((), (), s32[]{:S(2)}) async-start(), calls=%async_computation | async-start | bytes 5242880 | tf_op jit(solution)/shard_map/all_gather | solution.py:486
  11.8 203.9 %all-gather.9.cloned.1.call-start = ((), (), s32[]{:S(2)}) async-start(), calls=%async_computation.1 | async-start | bytes 2621440 | tf_op jit(solution)/shard_map/all_gather | solution.py:486
  11.9 32.2 %collective-permute-start.2 = (bf16[896,896]{1,0:T(8,128)(2,1)}, bf16[896,896]{1,0:T(8,128)(2,1)}, u32[]{:S(2)}, u32[]{:S(2)}) collective-permute-start(bf16[896,896]{1,0:T(8,128)(2,1)} %up_ref.1), channel_id=1, source_target_pairs={{0,1},{1,0},{2,3},{3,2},{4,5},{5,4},{6,7},{7,6},{8,9},{9,8},{10,11... | collective-permute-start | bytes 4816904 | tf_op jit(solution)/shard_map/ppermute | solution.py:19
  12.4 31.7 %collective-permute-start.3 = (bf16[896,896]{1,0:T(8,128)(2,1)}, bf16[896,896]{1,0:T(8,128)(2,1)}, u32[]{:S(2)}, u32[]{:S(2)}) collective-permute-start(bf16[896,896]{1,0:T(8,128)(2,1)} %down_ref.1), channel_id=1, source_target_pairs={{0,1},{1,0},{2,3},{3,2},{4,5},{5,4},{6,7},{7,6},{8,9},{9,8},{10,11... | collective-permute-start | bytes 4816904 | tf_op jit(solution)/shard_map/ppermute | solution.py:19
  12.5 31.6 %collective-permute-start.1 = (bf16[736,512]{1,0:T(8,128)(2,1)}, bf16[736,512]{1,0:T(8,128)(2,1)}, u32[]{:S(2)}, u32[]{:S(2)}) collective-permute-start(bf16[736,512]{1,0:T(8,128)(2,1)} %get-tuple-element.58), channel_id=1, source_target_pairs={{0,8},{8,0},{1,9},{9,1},{2,10},{10,2},{3,11},{11,3},{4,12},{12,4},... | collective-permute-start | bytes 2261000 | tf_op jit(solution)/shard_map/ppermute | solution.py:19
  15.5 27.9 %collective-permute-start = (bf16[512,512]{1,0:T(8,128)(2,1)}, bf16[512,512]{1,0:T(8,128)(2,1)}, u32[]{:S(2)}, u32[]{:S(2)}) collective-permute-start(bf16[512,512]{1,0:T(8,128)(2,1)} %get-tuple-element.82.refs_0_), channel_id=1, source_target_pairs={{0,16},{16,0},{1,17},{17,1},{2,18},{18,2},{3,19},{19,3},{4,20},{20... | collective-permute-start | bytes 1572872 | tf_op jit(solution)/shard_map/ppermute | solution.py:24
  18.1 29.7 %collective-permute-start.4 = (bf16[1248,512]{1,0:T(8,128)(2,1)}, bf16[1248,512]{1,0:T(8,128)(2,1)S(1)}, u32[]{:S(2)}, u32[]{:S(2)}) collective-permute-start(bf16[1248,512]{1,0:T(8,128)(2,1)} %get-tuple-element.62), channel_id=1, source_target_pairs={{0,4},{4,0},{1,5},{5,1},{2,6},{6,2},{3,7},{7,3},{8,12},{12,8},{9,1... | collective-permute-start | bytes 3833864 | tf_op jit(solution)/shard_map/ppermute | solution.py:19
  48.0 21.8 %collective-permute-start.6 = (bf16[512,896]{1,0:T(8,128)(2,1)S(1)}, bf16[512,896]{1,0:T(8,128)(2,1)S(1)}, u32[]{:S(2)}, u32[]{:S(2)}) collective-permute-start(bf16[512,896]{1,0:T(8,128)(2,1)S(1)} %add.214), channel_id=1, source_target_pairs={{0,2},{2,0},{1,3},{3,1},{4,6},{6,4},{5,7},{7,5},{8,10},{10,8},{9,1... | collective-permute-start | bytes 2752520 | tf_op jit(solution)/shard_map/ppermute | solution.py:19
  49.6 30.3 %collective-permute-start.7 = (bf16[736,512]{1,0:T(8,128)(2,1)}, bf16[736,512]{1,0:T(8,128)(2,1)}, u32[]{:S(2)}, u32[]{:S(2)}) collective-permute-start(bf16[736,512]{1,0:T(8,128)(2,1)} %collective-permute-done.1.refs_2_.refs_3_), channel_id=1, source_target_pairs={{0,4},{4,0},{1,5},{5,1},{2,6},{6,2},{3,7},{7,3},{8,12},{12,8},{9,1... | collective-permute-start | bytes 2261000 | tf_op jit(solution)/shard_map/ppermute | solution.py:19
  52.2 25.0 %collective-permute-start.9 = (bf16[512,512]{1,0:T(8,128)(2,1)S(1)}, bf16[512,512]{1,0:T(8,128)(2,1)S(1)}, u32[]{:S(2)}, u32[]{:S(2)}) collective-permute-start(bf16[512,512]{1,0:T(8,128)(2,1)S(1)} %slice.9), channel_id=1, source_target_pairs={{0,16},{16,0},{1,17},{17,1},{2,18},{18,2},{3,19},{19,3},{4,20},{20... | collective-permute-start | bytes 1572872 | tf_op jit(solution)/shard_map/ppermute | solution.py:24
  54.2 24.9 %collective-permute-start.8 = (bf16[512,512]{1,0:T(8,128)(2,1)}, bf16[512,512]{1,0:T(8,128)(2,1)S(1)}, u32[]{:S(2)}, u32[]{:S(2)}) collective-permute-start(bf16[512,512]{1,0:T(8,128)(2,1)} %collective-permute-done.refs_4_), channel_id=1, source_target_pairs={{0,4},{4,0},{1,5},{5,1},{2,6},{6,2},{3,7},{7,3},{8,12},{12,8},{9,1... | collective-permute-start | bytes 1572872 | tf_op jit(solution)/shard_map/ppermute | solution.py:19
  54.8 24.3 %collective-permute-start.10 = (bf16[512,512]{1,0:T(8,128)(2,1)S(1)}, bf16[512,512]{1,0:T(8,128)(2,1)S(1)}, u32[]{:S(2)}, u32[]{:S(2)}) collective-permute-start(bf16[512,512]{1,0:T(8,128)(2,1)S(1)} %copy-done.21), channel_id=1, source_target_pairs={{0,8},{8,0},{1,9},{9,1},{2,10},{10,2},{3,11},{11,3},{4,12},{12,4},... | collective-permute-start | bytes 1572872 | tf_op jit(solution)/shard_map/ppermute | solution.py:19
  79.9 12.2 %collective-permute-start.12 = (bf16[224,512]{1,0:T(8,128)(2,1)S(1)}, bf16[224,512]{1,0:T(8,128)(2,1)S(1)}, u32[]{:S(2)}, u32[]{:S(2)}) collective-permute-start(bf16[224,512]{1,0:T(8,128)(2,1)S(1)} %copy-done.8), channel_id=1, source_target_pairs={{0,16},{16,0},{1,17},{17,1},{2,18},{18,2},{3,19},{19,3},{4,20},{20... | collective-permute-start | bytes 688136 | tf_op jit(solution)/shard_map/ppermute | solution.py:24
  93.9 12.5 %collective-permute-start.11 = (bf16[256,1024]{1,0:T(8,128)(2,1)S(1)}, bf16[256,1024]{1,0:T(8,128)(2,1)S(1)}, u32[]{:S(2)}, u32[]{:S(2)}) collective-permute-start(bf16[256,1024]{1,0:T(8,128)(2,1)S(1)} %copy-done.12), channel_id=1, source_target_pairs={{0,8},{8,0},{1,9},{9,1},{2,10},{10,2},{3,11},{11,3},{4,12},{12,4},... | collective-permute-start | bytes 1572872 | tf_op jit(solution)/shard_map/ppermute | solution.py:19
  95.3 12.6 %collective-permute-start.14 = (bf16[512,512]{1,0:T(8,128)(2,1)S(1)}, bf16[512,512]{1,0:T(8,128)(2,1)S(1)}, u32[]{:S(2)}, u32[]{:S(2)}) collective-permute-start(bf16[512,512]{1,0:T(8,128)(2,1)S(1)} %collective-permute-done.10.refs_2_), channel_id=1, source_target_pairs={{0,4},{4,0},{1,5},{5,1},{2,6},{6,2},{3,7},{7,3},{8,12},{12,8},{9,1... | collective-permute-start | bytes 1572872 | tf_op jit(solution)/shard_map/ppermute | solution.py:19
  108.2 120.8 %all-gather.11.cloned.1.call-start = ((), (), s32[]{:S(2)}) async-start(), calls=%async_computation.2 | async-start | bytes 2621440 | tf_op jit(solution)/shard_map/all_gather | solution.py:486
  109.3 12.7 %collective-permute-start.16 = (bf16[224,512]{1,0:T(8,128)(2,1)S(1)}, bf16[224,512]{1,0:T(8,128)(2,1)S(1)}, u32[]{:S(2)}, u32[]{:S(2)}) collective-permute-start(bf16[224,512]{1,0:T(8,128)(2,1)S(1)} %slice.11), channel_id=1, source_target_pairs={{0,16},{16,0},{1,17},{17,1},{2,18},{18,2},{3,19},{19,3},{4,20},{20... | collective-permute-start | bytes 688136 | tf_op jit(solution)/shard_map/ppermute | solution.py:24
  124.0 23.3 %collective-permute-start.18 = (bf16[960,512]{1,0:T(8,128)(2,1)S(1)}, bf16[960,512]{1,0:T(8,128)(2,1)}, u32[]{:S(2)}, u32[]{:S(2)}) collective-permute-start(bf16[960,512]{1,0:T(8,128)(2,1)S(1)} %constant_dynamic-update-slice_fusion.refs_5_), channel_id=1, source_target_pairs={{0,4},{4,0},{1,5},{5,1},{2,6},{6,2},{3,7},{7,3},{8,12},{12,8},{9,1... | collective-permute-start | bytes 2949128 | tf_op jit(solution)/shard_map/ppermute | solution.py:19
  126.7 54.3 %collective-permute-start.22 = (bf16[1024,512]{1,0:T(8,128)(2,1)}, bf16[1024,512]{1,0:T(8,128)(2,1)}, u32[]{:S(2)}, u32[]{:S(2)}) collective-permute-start(bf16[1024,512]{1,0:T(8,128)(2,1)} %pad_maximum_fusion.1), channel_id=1, source_target_pairs={{0,16},{16,0},{1,17},{17,1},{2,18},{18,2},{3,19},{19,3},{4,20},{20... | collective-permute-start | bytes 3145736 | tf_op jit(solution)/shard_map/ppermute | solution.py:24
  130.9 15.2 %collective-permute-start.17 = (bf16[320,896]{1,0:T(8,128)(2,1)}, bf16[320,896]{1,0:T(8,128)(2,1)S(1)}, u32[]{:S(2)}, u32[]{:S(2)}) collective-permute-start(bf16[320,896]{1,0:T(8,128)(2,1)} %pad_maximum_fusion.2), channel_id=1, source_target_pairs={{0,2},{2,0},{1,3},{3,1},{4,6},{6,4},{5,7},{7,5},{8,10},{10,8},{9,1... | collective-permute-start | bytes 1720328 | tf_op jit(solution)/shard_map/ppermute | solution.py:19
  132.5 34.7 %collective-permute-start.20 = (bf16[320,896]{1,0:T(8,128)(2,1)}, bf16[320,896]{1,0:T(8,128)(2,1)}, u32[]{:S(2)}, u32[]{:S(2)}) collective-permute-start(bf16[320,896]{1,0:T(8,128)(2,1)} %pad_maximum_fusion.2), channel_id=1, source_target_pairs={{0,8},{8,0},{1,9},{9,1},{2,10},{10,2},{3,11},{11,3},{4,12},{12,4},... | collective-permute-start | bytes 1720328 | tf_op jit(solution)/shard_map/ppermute | solution.py:19
  132.5 48.5 %collective-permute-start.21 = (bf16[320,896]{1,0:T(8,128)(2,1)}, bf16[320,896]{1,0:T(8,128)(2,1)}, u32[]{:S(2)}, u32[]{:S(2)}) collective-permute-start(bf16[320,896]{1,0:T(8,128)(2,1)} %pad_maximum_fusion.2), channel_id=1, source_target_pairs={{0,10},{2,8},{8,2},{10,0},{1,11},{3,9},{9,3},{11,1},{4,14},{6,12},... | collective-permute-start | bytes 1720328 | tf_op jit(solution)/shard_map/ppermute | solution.py:537
  182.9 12.0 %collective-permute-start.24 = (bf16[256,1024]{1,0:T(8,128)(2,1)S(1)}, bf16[256,1024]{1,0:T(8,128)(2,1)}, u32[]{:S(2)}, u32[]{:S(2)}) collective-permute-start(bf16[256,1024]{1,0:T(8,128)(2,1)S(1)} %copy-done.13), channel_id=1, source_target_pairs={{0,8},{8,0},{1,9},{9,1},{2,10},{10,2},{3,11},{11,3},{4,12},{12,4},... | collective-permute-start | bytes 1572872 | tf_op jit(solution)/shard_map/ppermute | solution.py:19
  194.9 13.8 %collective-permute-start.23 = (bf16[640,896]{1,0:T(8,128)(2,1)}, bf16[640,896]{1,0:T(8,128)(2,1)}, u32[]{:S(2)}, u32[]{:S(2)}) collective-permute-start(bf16[640,896]{1,0:T(8,128)(2,1)} %constant_dynamic-update-slice_fusion.3.other_ref), channel_id=1, source_target_pairs={{0,1},{1,0},{2,3},{3,2},{4,5},{5,4},{6,7},{7,6},{8,9},{9,8},{10,11... | collective-permute-start | bytes 3440648 | tf_op jit(solution)/shard_map/ppermute | solution.py:19
  195.0 13.7 %collective-permute-start.19 = (bf16[640,896]{1,0:T(8,128)(2,1)S(1)}, bf16[640,896]{1,0:T(8,128)(2,1)}, u32[]{:S(2)}, u32[]{:S(2)}) collective-permute-start(bf16[640,896]{1,0:T(8,128)(2,1)S(1)} %copy-done.2), channel_id=1, source_target_pairs={{0,1},{1,0},{2,3},{3,2},{4,5},{5,4},{6,7},{7,6},{8,9},{9,8},{10,11... | collective-permute-start | bytes 3440648 | tf_op jit(solution)/shard_map/ppermute | solution.py:19
  195.5 39.4 %collective-permute-start.25 = (bf16[1024,512]{1,0:T(8,128)(2,1)}, bf16[1024,512]{1,0:T(8,128)(2,1)}, u32[]{:S(2)}, u32[]{:S(2)}) collective-permute-start(bf16[1024,512]{1,0:T(8,128)(2,1)} %collective-permute-done.22.refs_0_), channel_id=1, source_target_pairs={{0,4},{4,0},{1,5},{5,1},{2,6},{6,2},{3,7},{7,3},{8,12},{12,8},{9,1... | collective-permute-start | bytes 3145736 | tf_op jit(solution)/shard_map/ppermute | solution.py:19
  266.1 15.0 %collective-permute-start.27 = (bf16[256,1024]{1,0:T(8,128)(2,1)}, bf16[256,1024]{1,0:T(8,128)(2,1)S(1)}, u32[]{:S(2)}, u32[]{:S(2)}) collective-permute-start(bf16[256,1024]{1,0:T(8,128)(2,1)} %get-tuple-element.103), channel_id=1, source_target_pairs={{0,8},{8,0},{1,9},{9,1},{2,10},{10,2},{3,11},{11,3},{4,12},{12,4},... | collective-permute-start | bytes 1572872 | tf_op jit(solution)/shard_map/ppermute | solution.py:19
  266.9 25.9 %collective-permute-start.28 = (bf16[256,1024]{1,0:T(8,128)(2,1)}, bf16[256,1024]{1,0:T(8,128)(2,1)}, u32[]{:S(2)}, u32[]{:S(2)}) collective-permute-start(bf16[256,1024]{1,0:T(8,128)(2,1)} %get-tuple-element.104), channel_id=1, source_target_pairs={{0,2},{2,0},{1,3},{3,1},{4,6},{6,4},{5,7},{7,5},{8,10},{10,8},{9,1... | collective-permute-start | bytes 1572872 | tf_op jit(solution)/shard_map/ppermute | solution.py:19
  267.9 25.5 %collective-permute-start.29 = (bf16[256,1024]{1,0:T(8,128)(2,1)}, bf16[256,1024]{1,0:T(8,128)(2,1)}, u32[]{:S(2)}, u32[]{:S(2)}) collective-permute-start(bf16[256,1024]{1,0:T(8,128)(2,1)} %get-tuple-element.105), channel_id=1, source_target_pairs={{0,10},{2,8},{8,2},{10,0},{1,11},{3,9},{9,3},{11,1},{4,14},{6,12},... | collective-permute-start | bytes 1572872 | tf_op jit(solution)/shard_map/ppermute | solution.py:440
  275.8 27.8 %collective-permute-start.31 = (bf16[256,1024]{1,0:T(8,128)(2,1)}, bf16[256,1024]{1,0:T(8,128)(2,1)S(1)}, u32[]{:S(2)}, u32[]{:S(2)}) collective-permute-start(bf16[256,1024]{1,0:T(8,128)(2,1)} %get-tuple-element.109), channel_id=1, source_target_pairs={{0,8},{8,0},{1,9},{9,1},{2,10},{10,2},{3,11},{11,3},{4,12},{12,4},... | collective-permute-start | bytes 1572872 | tf_op jit(solution)/shard_map/ppermute | solution.py:19
  276.6 27.1 %collective-permute-start.32 = (bf16[256,1024]{1,0:T(8,128)(2,1)}, bf16[256,1024]{1,0:T(8,128)(2,1)S(1)}, u32[]{:S(2)}, u32[]{:S(2)}) collective-permute-start(bf16[256,1024]{1,0:T(8,128)(2,1)} %get-tuple-element.110), channel_id=1, source_target_pairs={{0,2},{2,0},{1,3},{3,1},{4,6},{6,4},{5,7},{7,5},{8,10},{10,8},{9,1... | collective-permute-start | bytes 1572872 | tf_op jit(solution)/shard_map/ppermute | solution.py:19
  281.2 33.7 %collective-permute-start.33 = (bf16[256,1024]{1,0:T(8,128)(2,1)}, bf16[256,1024]{1,0:T(8,128)(2,1)S(1)}, u32[]{:S(2)}, u32[]{:S(2)}) collective-permute-start(bf16[256,1024]{1,0:T(8,128)(2,1)} %get-tuple-element.111), channel_id=1, source_target_pairs={{0,10},{2,8},{8,2},{10,0},{1,11},{3,9},{9,3},{11,1},{4,14},{6,12},... | collective-permute-start | bytes 1572872 | tf_op jit(solution)/shard_map/ppermute | solution.py:440
  (27 other events, 401.6 us)
Sparse Core Ops, SparseCore 0:
  11.9 37.1 all-gather.6
  108.3 23.8 all-gather.8
  195.1 20.8 all-gather.10

commit v2 on v1

--- a/solution.py
+++ b/solution.py
@@ -53,7 +53,7 @@
         ),
         out_shape=[o[0] for o in outs],
         compiler_params=pltpu.CompilerParams(vmem_limit_bytes=VMEM),
-        cost_estimate=pl.CostEstimate(flops=1, bytes_accessed=1, transcendentals=0),
+        cost_estimate=pl.CostEstimate(flops=20000000000, bytes_accessed=1, transcendentals=0),
     )(prefetch, *arrays)
 
 
@@ -173,7 +173,7 @@
         out_shape=shape(dims, BF16),
         input_output_aliases={len(arrays): 0} if through else {},
         compiler_params=pltpu.CompilerParams(vmem_limit_bytes=VMEM),
-        cost_estimate=pl.CostEstimate(flops=1, bytes_accessed=1, transcendentals=0),
+        cost_estimate=pl.CostEstimate(flops=20000000000, bytes_accessed=1, transcendentals=0),
     )(jnp.stack([p[0] for p in pieces]).astype(jnp.int32), *arrays)
 
 
@@ -204,11 +204,13 @@
 
 
 def project(at, states, which, w, wide, span, last, before=None):
-    toks, wm = states[1].shape[1:]
+    toks, wm = states[0].shape[2:]
     cols, steps, per = w.shape[1], at.shape[0], wm // wide
     operands = [
-        (states[0], (None, None, toks, wide), lambda i, at: (at[i] // per, which, 0, lax.rem(at[i], per))),
-        (states[1], (None, toks, wide), lambda i, at: (at[i] // per, 0, lax.rem(at[i], per))),
+        (a, (None, None, toks, wide), lambda i, at: (at[i] // per, which, 0, lax.rem(at[i], per)))
+        for a in states
+    ]
+    operands += [
         (w, (wide, cols), lambda i, at: (at[i], 0)),
     ]
     total = (2 * toks, cols)
@@ -225,22 +227,16 @@
     )[0]
 
 
-def keyval_kernel(at_ref, own_ref, other_ref, w_ref, k_ref, v_ref):
-    for turn, rows_ref in enumerate((own_ref, other_ref)):
-
-        @pl.when(pl.program_id(0) == turn)
-        def _():
-            rows = rows_ref[...]
-            k_ref[...] = dot(rows, w_ref[0]).astype(BF16)
-            v_ref[...] = dot(rows, w_ref[1]).astype(BF16)
-
-
-def keyval(at, own, other, w):
-    count, width = own.shape
-    inner = w.shape[2]
-    out = (shape((2 * count, inner), BF16), (count, inner), lambda i, at: (i, 0))
-    operands = [(a, a.shape, whole_block(a.ndim)) for a in (own, other, w)]
-    return call(keyval_kernel, (2,), at, operands, [out, out], [])
+def keyval_kernel(at_ref, rows_ref, w_ref, k_ref, v_ref):
+    rows = rows_ref[...]
+    k_ref[...] = dot(rows, w_ref[0]).astype(BF16)
+    v_ref[...] = dot(rows, w_ref[1]).astype(BF16)
+
+
+def keyval(at, rows, w):
+    out = shape((rows.shape[0], w.shape[2]), BF16)
+    operands = [(a, a.shape, whole_block(a.ndim)) for a in (rows, w)]
+    return call(keyval_kernel, (1,), at, operands, [(out, out.shape, whole_block(2))] * 2, [])
 
 
 def encode_kernel(at_ref, emb_ref, up_ref, down_ref, up2_ref, down2_ref, ffn_ref, own_ref, normed, acc):
@@ -290,18 +286,17 @@
 
 
 def span_rows(halves, g, cols):
-    parts = [half[0, :, g, :, cols] for half in halves]
+    parts = [half[:, g, :, cols] for half in halves]
     parts = [p.reshape(p.shape[0] * p.shape[1], p.shape[2]) for p in parts]
     return jnp.concatenate(parts, axis=0)
 
 
-def attend_kernel(span, head_dim, at_ref, q_ref, k_ref, v_ref, k2_ref, v2_ref, attn_ref, prob_ref, stage):
-    turn = pl.program_id(0)
-    _, blocks, groups, piece, inner = k_ref.shape
+def attend_kernel(span, head_dim, turn, at_ref, q_ref, k_ref, v_ref, k2_ref, v2_ref, attn_ref, prob_ref, stage):
+    blocks, groups, piece, inner = k_ref.shape
     heads, keys_per = inner // head_dim, 2 * blocks * piece
     nlen = keys_per // 2
     scale = head_dim ** (-0.5)
-    toks = attn_ref.shape[1]
+    toks = attn_ref.shape[0]
     lane = lax.broadcasted_iota(jnp.int32, (span, keys_per), 1)
     key = lane
     for i in range(2 * blocks):
@@ -312,7 +307,7 @@
         rows = pl.ds(g * span, span)
         for h in range(heads):
             cols = pl.ds(h * head_dim, head_dim)
-            prob_ref[0, h, rows, :] = dot_t(q_ref[0, rows, cols], span_rows((k_ref, k2_ref), g, cols))
+            prob_ref[h, rows, :] = dot_t(q_ref[0, rows, cols], span_rows((k_ref, k2_ref), g, cols))
     for g in range(groups):
         rows = pl.ds(g * span, span)
         base = (turn * groups + g) * 3
@@ -321,20 +316,20 @@
         weight = live.astype(F32)
         for h in range(heads):
             cols = pl.ds(h * head_dim, head_dim)
-            expo = jnp.where(mask, jnp.exp(prob_ref[0, h, rows, :] * scale), 0.0)
+            expo = jnp.where(mask, jnp.exp(prob_ref[h, rows, :] * scale), 0.0)
             prob = expo * (weight / jnp.sum(expo, axis=-1, keepdims=True))
-            prob_ref[0, h, rows, :] = prob
+            prob_ref[h, rows, :] = prob
             stage[rows, cols] = dot(prob.astype(BF16), span_rows((v_ref, v2_ref), g, cols))
-    attn_ref[0] = stage[1 : toks + 1, :].astype(BF16)
+    attn_ref[...] = stage[1 : toks + 1, :].astype(BF16)
 
 
 def backward_kernel(
-    span, head_dim, at_ref, prob_ref, d_ref, k_ref, v_ref, k2_ref, v2_ref, dq_ref, stage, d_prob
+    span, head_dim, turn, at_ref, prob_ref, d_ref, k_ref, v_ref, k2_ref, v2_ref, dq_ref, stage, d_prob
 ):
-    groups, inner = k_ref.shape[2], k_ref.shape[4]
+    groups, inner = k_ref.shape[1], k_ref.shape[3]
     heads = inner // head_dim
     scale = head_dim ** (-0.5)
-    toks = dq_ref.shape[1]
+    toks = dq_ref.shape[0]
     for g in range(groups):
         rows = pl.ds(g * span, span)
         for h in range(heads):
@@ -344,76 +339,61 @@
         rows = pl.ds(g * span, span)
         for h in range(heads):
             cols = pl.ds(h * head_dim, head_dim)
-            prob, slope = prob_ref[0, h, rows, :], d_prob[h, rows, :]
+            prob, slope = prob_ref[h, rows, :], d_prob[h, rows, :]
             delta = jnp.sum(prob * slope, axis=-1, keepdims=True)
             d_score = (prob * (slope - delta) * scale).astype(BF16)
             stage[rows, cols] = dot(d_score, span_rows((k_ref, k2_ref), g, cols))
-    dq_ref[0] = stage[1 : toks + 1, :].astype(BF16)
-
-
-def over_shards(kernel, at, padded, kv, span, head_dim, prob):
-    shards, rows, inner = padded.shape
-    toks = rows - span
-    keys_per = 2 * kv[0].shape[1] * kv[0].shape[3]
-    heads = inner // head_dim
-    def by_turn(ndim):
-        return lambda s, at: (s,) + (0,) * (ndim - 1)
-
-    probs = shape((shards, heads, rows, keys_per), F32)
-    prob_spec = ((1, heads, rows, keys_per), by_turn(4))
-    operands = [(padded, (1, rows, inner), by_turn(3))]
-    operands += [(a, (1,) + a.shape[1:], by_turn(5)) for a in kv]
-    outs = [(shape((shards, toks, inner), BF16), (1, toks, inner), by_turn(3))]
+    dq_ref[...] = stage[1 : toks + 1, :].astype(BF16)
+
+
+def over_shard(kernel, turn, at, padded, kv, span, head_dim, prob):
+    _, rows, inner = padded.shape
+    toks, heads = rows - span, inner // head_dim
+    probs = shape((heads, rows, 2 * kv[0].shape[0] * kv[0].shape[2]), F32)
+    operands = [(padded, (1, rows, inner), lambda i, at: (turn, 0, 0))]
+    operands += [(a, a.shape, whole_block(4)) for a in kv]
+    outs = [(shape((toks, inner), BF16), (toks, inner), whole_block(2))]
     scratch = [pltpu.VMEM((rows, inner), F32)]
     if prob is None:
-        outs.append((probs,) + prob_spec)
+        outs.append((probs, probs.shape, whole_block(3)))
     else:
-        operands.insert(0, (prob,) + prob_spec)
-        scratch.append(pltpu.VMEM(probs.shape[1:], F32))
-    return call(functools.partial(kernel, span, head_dim), (shards,), at, operands, outs, scratch)
-
-
-def sent_kernel(at_ref, rows_ref, w_ref, out_ref):
-    out_ref[0] = dot_t(rows_ref[...], w_ref[...]).astype(BF16)
-
-
-def kept_kernel(at_ref, rows_ref, w_ref, add_ref, both_ref, y_ref, zl_ref, own_ref):
-    total = dot_t(rows_ref[...], w_ref[...]) + add_ref[0].astype(F32)
-    toks = own_ref.shape[0]
+        operands.insert(0, (prob, prob.shape, whole_block(3)))
+        scratch.append(pltpu.VMEM(probs.shape, F32))
+    return call(functools.partial(kernel, span, head_dim, turn), (1,), at, operands, outs, scratch)
+
+
+def sent_kernel(at_ref, own_ref, other_ref, w_ref, out_ref):
+    rows = jnp.concatenate([own_ref[...], other_ref[...]], axis=0)
+    out_ref[0] = dot_t(rows, w_ref[...]).astype(BF16)
+
+
+def kept_kernel(at_ref, own_rows_ref, other_rows_ref, w_ref, add_ref, both_ref, y_ref, zl_ref, own_ref):
+    def total(rows_ref, start):
+        add = add_ref[0, start : start + rows_ref.shape[0], :]
+        return dot_t(rows_ref[...], w_ref[...]) + add.astype(F32)
 
     @pl.when(pl.program_id(0) == 0)
     def _():
-        y_ref[...] = total[:toks].astype(BF16)
-        both_ref[...] = total[toks:].astype(BF16)
+        y_ref[...] = total(own_rows_ref, 0).astype(BF16)
+        both_ref[...] = total(other_rows_ref, own_ref.shape[0]).astype(BF16)
 
     @pl.when(pl.program_id(0) == 1)
     def _():
-        own_ref[...] = total[:toks]
-        zl_ref[...] = total[toks:].astype(BF16)
-
-
-CUTS = 1
+        own_ref[...] = total(own_rows_ref, 0)
+        zl_ref[...] = total(other_rows_ref, own_ref.shape[0]).astype(BF16)
 
 
 def columns(at, rows, w, wm, add=None):
-    count, inner = rows.shape
-    cut = wm // CUTS
-    operands = [
-        (rows, rows.shape, whole_block(2)),
-        (w, (cut, inner), lambda i, j, at: (at[i] * CUTS + j, 0)),
-    ]
-    moved = (1, count, cut), lambda i, j, at: (i, 0, j)
+    toks, inner = rows[0].shape
+    operands = [(a, a.shape, whole_block(2)) for a in rows]
+    operands.append((w, (wm, inner), lambda i, at: (at[i], 0)))
+    moved = (1, 2 * toks, wm), lambda i, at: (i, 0, 0)
     if add is None:
-        out = shape((2, count, wm), BF16)
-        return call(sent_kernel, (2, CUTS), at, operands, [(out,) + moved], [])[0]
+        out = shape((2, 2 * toks, wm), BF16)
+        return call(sent_kernel, (2,), at, operands, [(out,) + moved], [])[0]
     operands.append((add,) + moved)
-    half = (count // 2, wm)
-    block = (count // 2, cut)
-    early = lambda i, j, at: (0, jnp.where(i == 0, j, CUTS - 1))
-    late = lambda i, j, at: (0, jnp.where(i == 0, 0, j))
-    outs = [(shape(half, BF16), block, early)] * 2
-    outs += [(shape(half, BF16), block, late), (shape(half, F32), block, late)]
-    return call(kept_kernel, (2, CUTS), at, operands, outs, [])
+    outs = [(shape((toks, wm), dtype), (toks, wm), whole_block(2)) for dtype in (BF16, BF16, BF16, F32)]
+    return call(kept_kernel, (2,), at, operands, outs, [])
 
 
 def core_sums(rows, w):
@@ -429,18 +409,19 @@
     zl, y, c = (lax.axis_index(name) for name in GROUP)
     ny = lax.axis_size("y")
     wm = w.shape[0] // (2 * ny)
-    count = rows.shape[0]
     if ny != 2:
+        rows = jnp.concatenate(rows, axis=0)
+        count = rows.shape[0]
         rows = jnp.roll(rows, zl * (count // 2), axis=0)
         blocks = dot_t(rows, w).astype(BF16).reshape(2, count // 2, ny, 2, wm)
         blocks = blocks.transpose(0, 2, 3, 1, 4).reshape(ny * 2 * count, wm)
-        return lax.psum_scatter(blocks, GROUP, scatter_dimension=0, tiled=True).astype(BF16), ()
+        return lax.psum_scatter(blocks, GROUP, scatter_dimension=0, tiled=True).astype(BF16), (), ()
     at = jnp.stack([(1 - y) * 2 + c, y * 2 + c])
     to_both, to_y, to_zl, own = columns(at, rows, w, wm, flip(sent, "c"))
     over_both = lax.ppermute(to_both, ("zl", "y"), [(i, 3 - i) for i in range(4)])
     over_y, over_zl = flip(to_y, "y"), flip(to_zl, "zl")
     total = own + over_zl.astype(F32) + over_y.astype(F32) + over_both.astype(F32)
-    return total.astype(BF16), (to_both, to_y, to_zl)
+    return total.astype(BF16), (to_both, to_y, to_zl), (over_both, over_y, over_zl)
 
 
 def per_device(
@@ -510,10 +491,10 @@
     emb = emb + flip(emb, "y") if ny == 2 else lax.psum(emb, "y")
     emb = tie(emb, beside_qkv_x, hop_q_x, hop_q2, beside_out, own_states)
 
-    own_kv, beside_out, hidden = (tie(a, emb) for a in (own_kv, beside_out, hidden))
+    own_kv, beside_out, states = (tie(a, emb) for a in (own_kv, beside_out, states))
     hop_kv = onward(own_kv, "zh")
     beside_out_x = flip(beside_out, "x")
-    other_hidden = flip(hidden, "zl")
+    other_states = flip(states, "zl")
     share_rows = half_rows // ny
     ffn, share = encode(y, emb, [enc_up, enc_down, up2, down2], share_rows, 2)
     ffn = tie(ffn, hop_kv)
@@ -524,11 +505,11 @@
     else:
         share = lax.psum_scatter(ffn, "y", scatter_dimension=0, tiled=True).astype(F32)
         share = share + lax.dynamic_slice_in_dim(emb, y * share_rows, share_rows, 0).astype(F32)
-    encoded = rms_rows(tie(share, beside_out_x, other_hidden)).astype(BF16)
-
-    other_hidden = gather_states(tie(other_hidden, encoded))
+    encoded = rms_rows(tie(share, beside_out_x, other_states, hop_kv2)).astype(BF16)
+
+    other_states = gather_states(tie(other_states, encoded))
     before = lax.ppermute(encoded[share_rows - piece :], SEQ, [(i, i + 1) for i in range(seqs - 1)])
-    encoded = jnp.concatenate([tie(before, hop_kv2), encoded], axis=0)
+    encoded = jnp.concatenate([before, encoded], axis=0)
     hop_qkv = jnp.concatenate([tie(hop_q2, encoded), hop_kv, hop_kv2], axis=0)
     hop_qkv_x = flip(hop_qkv, "x")
     hop_out = onward(jnp.concatenate([tie(own_out, encoded), beside_out], axis=0), "zh")
@@ -537,7 +518,7 @@
         corner = lax.ppermute(encoded, ("zl", "y"), [(i, 3 - i) for i in range(4)])
         over_y, over_zl = flip(encoded, "y"), flip(encoded, "zl")
         over_y = tie(over_y, hop_qkv_x)
-        own_rows, other_rows = [encoded, over_y], [over_zl, tie(corner, hop_out)]
+        own_rows, other_rows = [encoded, over_y], [over_zl, corner]
         ys = [y, 1 - y]
     else:
         own_rows = [lax.all_gather(encoded, "y", axis=0, tiled=True)]
@@ -587,24 +568,34 @@
     q_pieces[0] = (q_pieces[0][0], tie(q_pieces[0][1], over_y)) + q_pieces[0][2:]
     kv_pieces[0] = (kv_pieces[0][0], tie(kv_pieces[0][1], over_y)) + kv_pieces[0][2:]
     wkv = place(kv_pieces, (2, enc_width, inner))
+    wq, wo = place(q_pieces, w_dims), place(out_pieces, w_dims)
+    every = jnp.arange(2 * ny, dtype=jnp.int32)
+    kv_shape = (ny, groups, piece, inner)
+    states = (own_states, other_states)
+
+    def at_of(pieces):
+        return jnp.stack([p[0] for p in pieces])
+
+    def keys_values(rows, rows2):
+        near = keyval(at, rows, wkv)
+        far = keyval(at, tie(rows2, *near), wkv)
+        return [a.reshape(kv_shape) for a in (*near, *far)]
+
+    def attend(turn, kv, query):
+        return over_shard(attend_kernel, turn, at, query, kv, span, head_dim, None)
+
     own_rows = jnp.concatenate(own_rows, axis=0)
     own_rows2 = flip(own_rows, "c")
-    other_rows = jnp.concatenate([tie(other_rows[0], wkv)] + other_rows[1:], axis=0)
+    kv = keys_values(own_rows, own_rows2)
+    query = project(every, states, 0, tie(wq, wo, *kv), hidden.shape[1], span, True)
+    attn, prob = attend(0, kv, query)
+    other_rows = jnp.concatenate(lax.optimization_barrier((*other_rows, attn))[:-1], axis=0)
     other_rows2 = flip(other_rows, "c")
-    hop_out = tie(hop_out, other_rows)
+    hop_out = tie(hop_out, attn)
     hop_out_x = flip(hop_out, "x")
-    other_cot = flip(tie(cotangent, other_rows), "zl")
-    wq = place(q_pieces, w_dims)
-    every = jnp.arange(2 * ny, dtype=jnp.int32)
-    kv_shape = (2, ny, groups, piece, inner)
-    keys, values = keyval(at, own_rows, other_rows, wkv)
-    other_cot = gather_states(tie(other_cot, keys))
-    other_rows2 = tie(other_rows2, keys)
-    keys2, values2 = keyval(at, own_rows2, other_rows2, wkv)
-    query = project(every, (own_states, other_hidden), 0, tie(wq, keys2), hidden.shape[1], span, True)
-    kv = [a.reshape(kv_shape) for a in (keys, values, keys2, values2)]
-    attn, prob = over_shards(attend_kernel, at, query, kv, span, head_dim, None)
-    attn = attn.reshape(2 * toks, inner)
+    kv2 = keys_values(other_rows, other_rows2)
+    attn2, prob2 = attend(1, kv2, query)
+    some = project(at_of(out_pieces), states, 1, tie(wo, attn2), rows_here, span, False)
 
     late = []
     for hop in range(1, nzh):
@@ -615,23 +606,24 @@
             late.append((shard_at(hop, zl, at_x), block, 0, rows_here, None))
             late.append((shard_at(hop, 1 - zl, at_x), block, rows_here, rows_here, None))
 
-    def at_of(pieces):
-        return jnp.stack([p[0] for p in pieces])
-
-    states = (own_states, other_cot)
-    wo = place(out_pieces, w_dims)
-    some = project(at_of(out_pieces), states, 1, tie(wo, attn), rows_here, span, False)
     hop_out_x = tie(hop_out_x, some)
     late[-2:] = [(p[0], hop_out_x) + p[2:] for p in late[-2:]]
     wo = place(late, w_dims, wo)
+    attn = (attn, attn2)
     out_sent = core_sums(attn, wo)
     if out_sent is not None:
         some = tie(some, out_sent)
     d_attn = project(at_of(late), states, 1, wo, rows_here, span, True, some)
-    cca_out, moved = sum_heads(tie(attn, d_attn), wo, out_sent)
-    (d_query,) = over_shards(backward_kernel, at, tie(d_attn, *moved), kv, span, head_dim, prob)
-    d_query = d_query.reshape(2 * toks, inner)
-    hidden_grad, _ = sum_heads(d_query, wq, core_sums(d_query, wq))
+    cca_out, moved, arrived = sum_heads((attn[0], tie(attn[1], d_attn)), wo, out_sent)
+    d_attn = tie(d_attn, *moved)
+    d_query = [
+        over_shard(backward_kernel, turn, at, d_attn, kv_here, span, head_dim, prob_here)[0]
+        for turn, kv_here, prob_here in ((0, kv, prob), (1, kv2, prob2))
+    ]
+    grad_sent = core_sums(d_query, wq)
+    if arrived:
+        grad_sent = tie(grad_sent, *arrived)
+    hidden_grad, _, _ = sum_heads(d_query, wq, grad_sent)
     return (cca_out, hidden_grad)
 
 

time: 323 us -> 307 us (0.950)
  waiting for transfers between devices: 123 us -> 95.3 us
  Pallas kernels: 95.2 us -> 107 us
  starting transfers between devices: 47 us -> 42.6 us
    ppermute x25 -> x24, waiting for transfers between devices: 82.3 us -> 69.1 us  [flip(): return lax.ppermute(shard, axis, [(0, 1), (1, 0)])]
    ppermute x1, waiting for transfers between devices: 11.9 us -> 0.01 us  [per_device(): corner = lax.ppermute(encoded, ('zl', 'y'), [(i, 3 - i) for i in range(4)])]
    ppermute x2, waiting for transfers between devices: 11.7 us -> 0.01 us  [sum_heads(): lax.ppermute(to_both, ('zl', 'y'), [(i, 3 - i) for i in range(4)])]
    pallas_call x13 -> x17, Pallas kernels: 78.9 us -> 90.4 us  [call(): pl.pallas_call(kernel, grid_spec=pltpu.PrefetchScalarGridSpec(num_scalar_...]
    all_gather x3 -> x2, waiting for transfers between devices: 0.01 us -> 7.05 us  [gather_states(): return lax.all_gather(rows, ('y', 'c'), axis=0, tiled=False)]
    ppermute x5, starting transfers between devices: 14.9 us -> 10.1 us  [onward(): lax.ppermute(shard, axis, [(i, (i + 1) % count) for i in range(count)])]
    ppermute x25 -> x24, starting transfers between devices: 23.6 us -> 22.1 us  [flip(): return lax.ppermute(shard, axis, [(0, 1), (1, 0)])]
  transfers between devices with their start and end apart: 37 -> 35, of which waited for: 22 -> 17; matrix products, arithmetic and copies ran while one was open for 12% -> 13% of each run, Pallas kernels for 21% -> 27%
where the time goes in v2:
time: 307 us; the launch traced here: 305 us
  Pallas kernels  107 us (35%)
  waiting for transfers between devices  95.3 us (31%)
  starting transfers between devices  42.6 us (14%)
  local copies, waits for them, and re-layouts  33.2 us (11%)
  between operations  14.3 us (5%)
  other arithmetic  13.1 us (4%)
    pallas_call x17, Pallas kernels, call(): pl.pallas_call(kernel, grid_spec=pltpu.PrefetchScalarGridSpec(num_scalar_...  90.4 us
    ppermute x24, waiting for transfers between devices, flip(): return lax.ppermute(shard, axis, [(0, 1), (1, 0)])  69.1 us
    ppermute x24, starting transfers between devices, flip(): return lax.ppermute(shard, axis, [(0, 1), (1, 0)])  22.1 us
    ppermute x5, waiting for transfers between devices, onward(): lax.ppermute(shard, axis, [(i, (i + 1) % count) for i in range(count)])  19.1 us
    gather x1, local copies, waits for them, and re-layouts, per_device(): embed_table.at[clipped].get(mode='promise_in_bounds')  18.9 us
    pallas_call x4, Pallas kernels, place(): pl.pallas_call(functools.partial(place_kernel, jobs, len(sources), int(th...  16.3 us
    ppermute x5, starting transfers between devices, onward(): lax.ppermute(shard, axis, [(i, (i + 1) % count) for i in range(count)])  10.1 us
    all_gather x2, waiting for transfers between devices, gather_states(): return lax.all_gather(rows, ('y', 'c'), axis=0, tiled=False)  7.05 us
  transfers between devices with their start and end apart: 35, of which 17 were waited for; matrix products, arithmetic and copies ran while one was open for 13% of the time, Pallas kernels for 27%

profile of v2, /device:TPU:0, one launch (start us, length us, event | category | flops | bytes accessed | tf_op | source)
XLA Modules:
  0.0 305.3 jit_solution(2871405193199003554)
XLA Ops:
  7.2 4.6 %shard_map.113 = (bf16[736,512]{1,0:T(8,128)(2,1)}, bf16[512,512]{1,0:T(8,128)(2,1)}, bf16[1248,512]{1,0:T(8,128)(2,1)}, bf16[512,512]{1,0:T(8,128)(2,1)}, bf16[...) custom-call(s32[1]{0:T(128)} %bitcast.6.at_ref, bf16[512,8,128]{2,1,0:T(8,128)(2,1)} %q_ref.1, ...), custom_call_target="tpu_custom_call" | custom-call | flops 20000000000 | bytes 1 | tf_op jit(solution)/shard_map/pallas_call | solution.py:45
  19.8 18.9 %gather_fusion = bf16[1024,896]{1,0:T(8,128)(2,1)S(1)} fusion(bf16[16000,896]{1,0:T(8,128)(2,1)} %param.14, s32[1024]{0:T(1024)S(1)} %fusion), kind=kCustom, calls=%fused_computation | custom fusion | bytes 3674112 | tf_op jit(solution)/shard_map/gather | solution.py:476
  38.8 4.6 %collective-permute-done.refs_4_ = bf16[512,512]{1,0:T(8,128)(2,1)} collective-permute-done((bf16[512,512]{1,0:T(8,128)(2,1)}, bf16[512,512]{1,0:T(8,128)(2,1)}, u32[]{:S(2)}, u32[]{:S(2)}) %collective-permute-start) | collective-permute-done | bytes 524320 | tf_op jit(solution)/shard_map/ppermute | solution.py:24
  57.1 12.8 %collective-permute-done.6 = bf16[512,896]{1,0:T(8,128)(2,1)S(1)} collective-permute-done((bf16[512,896]{1,0:T(8,128)(2,1)S(1)}, bf16[512,896]{1,0:T(8,128)(2,1)S(1)}, u32[]{:S(2)}, u32[]{:S(2)}) %collective-permute-start.6) | collective-permute-done | bytes 917536 | tf_op jit(solution)/shard_map/ppermute | solution.py:19
  71.1 7.1 %collective-permute-done.9 = bf16[512,512]{1,0:T(8,128)(2,1)S(1)} collective-permute-done((bf16[512,512]{1,0:T(8,128)(2,1)}, bf16[512,512]{1,0:T(8,128)(2,1)S(1)}, u32[]{:S(2)}, u32[]{:S(2)}) %collective-permute-start.9) | collective-permute-done | bytes 524320 | tf_op jit(solution)/shard_map/ppermute | solution.py:24
  83.4 9.3 %shard_map.114 = (bf16[512,896]{1,0:T(8,128)(2,1)}, f32[256,896]{1,0:T(8,128)}) custom-call(s32[1]{0:T(128)} %bitcast.9.at_ref, bf16[512,896]{1,0:T(8,128)(2,1)} %add.215.emb_ref, bf16[896,896]{1,0:T(8,128)(2,1)} %up_ref.1, bf16[896,896]{1,0:T(8,128)(2,1)} %down_ref.1, bf16[896,896]{1,0:T(8,128)(2,1)} %collective-permute-done.2.up2_ref, ...), custom_call_target="tpu_custom_call" | custom-call | flops 20000000000 | bytes 1 | tf_op jit(solution)/shard_map/pallas_call | solution.py:45
  99.1 5.8 %collective-permute-done.13 = bf16[256,896]{1,0:T(8,128)(2,1)} collective-permute-done((bf16[256,896]{1,0:T(8,128)(2,1)S(1)}, bf16[256,896]{1,0:T(8,128)(2,1)}, u32[]{:S(2)}, u32[]{:S(2)}) %collective-permute-start.13) | collective-permute-done | bytes 458784 | tf_op jit(solution)/shard_map/ppermute | solution.py:19
  106.1 7.4 %collective-permute-done.15 = bf16[224,512]{1,0:T(8,128)(2,1)} collective-permute-done((bf16[224,512]{1,0:T(8,128)(2,1)S(1)}, bf16[224,512]{1,0:T(8,128)(2,1)}, u32[]{:S(2)}, u32[]{:S(2)}) %collective-permute-start.15) | collective-permute-done | bytes 229408 | tf_op jit(solution)/shard_map/ppermute | solution.py:24
  114.6 3.6 %collective-permute-start.16 = (bf16[64,896]{1,0:T(8,128)(2,1)S(1)}, bf16[64,896]{1,0:T(8,128)(2,1)S(1)}, u32[]{:S(2)}, u32[]{:S(2)}) collective-permute-start(bf16[64,896]{1,0:T(8,128)(2,1)S(1)} %slice.14), channel_id=1, source_target_pairs={{0,4},{4,8},{8,12},{12,16},{16,20},{20,24},{24,28},{1,5},{5,9},{9,... | collective-permute-start | bytes 344072 | tf_op jit(solution)/shard_map/ppermute | solution.py:511
  128.9 4.3 %shard_map.116.w_ref.refs_2_ = bf16[4096,512]{1,0:T(8,128)(2,1)} custom-call(s32[4]{0:T(128)} %pad_add_fusion.3.at_ref, bf16[512,512]{1,0:T(8,128)(2,1)} %get-tuple-element.104.refs_0_, bf16[1248,512]{1,0:T(8,128)(2,1)} %collective-permute-done.4.refs_1_.refs_2_, bf16[512,512]{1,0:T(8,128)(2,1)} %collective-permute-done.10.refs_2_, ...), custom_call_target="tpu_custom_call" | custom-call | flops 20000000000 | bytes 1 | tf_op jit(solution)/shard_map/pallas_call | solution.py:164
  141.4 7.3 %collective-permute-done.18.refs_7_.refs_6_ = bf16[960,512]{1,0:T(8,128)(2,1)} collective-permute-done((bf16[960,512]{1,0:T(8,128)(2,1)}, bf16[960,512]{1,0:T(8,128)(2,1)}, u32[]{:S(2)}, u32[]{:S(2)}) %collective-permute-start.18) | collective-permute-done | bytes 983072 | tf_op jit(solution)/shard_map/ppermute | solution.py:19
  153.5 4.9 %shard_map.118 = (bf16[640,512]{1,0:T(8,128)(2,1)}, bf16[640,512]{1,0:T(8,128)(2,1)}) custom-call(s32[34]{0:T(128)} %concatenate.31.at_ref, bf16[640,896]{1,0:T(8,128)(2,1)} %copy-done, bf16[2,896,512]{2,1,0:T(8,128)(2,1)} %shard_map.117.w_ref), custom_call_target="tpu_custom_call" | custom-call | flops 20000000000 | bytes 1 | tf_op jit(solution)/shard_map/pallas_call | solution.py:45
  158.5 4.9 %shard_map.115.w_ref = bf16[4096,512]{1,0:T(8,128)(2,1)} custom-call(s32[8]{0:T(128)} %stack.59.at_ref, bf16[512,512]{1,0:T(8,128)(2,1)} %get-tuple-element.86.refs_0_, bf16[1248,512]{1,0:T(8,128)(2,1)} %collective-permute-done.4.refs_1_.refs_2_, bf16[736,512]{1,0:T(8,128)(2,1)} %copy-done.5, bf16[736,512]{1,0:T(8,128)(2,1)} %collective-permute-done.7.refs_3_.refs_4_, ...), custom_call_target="tpu_custom_call" | custom-call | flops 20000000000 | bytes 1 | tf_op jit(solution)/shard_map/pallas_call | solution.py:164
  163.4 4.9 %shard_map.119 = (bf16[640,512]{1,0:T(8,128)(2,1)}, bf16[640,512]{1,0:T(8,128)(2,1)}) custom-call(s32[34]{0:T(128)} %concatenate.31.at_ref, bf16[640,896]{1,0:T(8,128)(2,1)} %collective-permute-done.19.rows_ref, bf16[2,896,512]{2,1,0:T(8,128)(2,1)} %shard_map.117.w_ref), custom_call_target="tpu_custom_call" | custom-call | flops 20000000000 | bytes 1 | tf_op jit(solution)/shard_map/pallas_call | solution.py:45
  168.3 7.0 %all-gather.7.cloned.1.call-done = bf16[8,256,1024]{2,1,0:T(8,128)(2,1)} async-done(((bf16[2,256,1024]{2,1,0:T(8,128)(2,1)}), bf16[8,256,1024]{2,1,0:T(8,128)(2,1)}) %all-gather.7.cloned.1.call-update) | async-done | bytes 4194320 | tf_op jit(solution)/shard_map/all_gather | solution.py:467
  175.8 7.3 %shard_map.120.q_ref = bf16[2,320,512]{2,1,0:T(8,128)(2,1)} custom-call(s32[4]{0:T(128)} %iota.13.at_ref, bf16[4,2,256,1024]{3,2,1,0:T(8,128)(2,1)} %bitcast.32, bf16[4,2,256,1024]{3,2,1,0:T(8,128)(2,1)} %bitcast.35, bf16[4096,512]{1,0:T(8,128)(2,1)} %shard_map.115.w_ref), custom_call_target="tpu_custom_call" | custom-call | flops 20000000000 | bytes 1 | tf_op jit(solution)/shard_map/pallas_call | solution.py:45
  183.1 4.5 %shard_map.121 = (bf16[256,512]{1,0:T(8,128)(2,1)}, f32[4,320,256]{2,1,0:T(8,128)}) custom-call(s32[34]{0:T(128)} %concatenate.31.at_ref, bf16[2,320,512]{2,1,0:T(8,128)(2,1)} %shard_map.120.q_ref, bf16[2,5,64,512]{3,2,1,0:T(8,128)(2,1)} %bitcast.38, bf16[2,5,64,512]{3,2,1,0:T(8,128)(2,1)} %bitcast.40, bf16[2,5,64,512]{3,2,1,0:T(8,128)(2,1)} %bitcast.42, ...), custom_call_target="tpu_custom_call" | custom-call | flops 20000000000 | bytes 1 | tf_op jit(solution)/shard_map/pallas_call | solution.py:45
  192.3 4.9 %shard_map.122 = (bf16[640,512]{1,0:T(8,128)(2,1)}, bf16[640,512]{1,0:T(8,128)(2,1)}) custom-call(s32[34]{0:T(128)} %concatenate.31.at_ref, bf16[640,896]{1,0:T(8,128)(2,1)} %copy-done.10, bf16[2,896,512]{2,1,0:T(8,128)(2,1)} %shard_map.117.w_ref), custom_call_target="tpu_custom_call" | custom-call | flops 20000000000 | bytes 1 | tf_op jit(solution)/shard_map/pallas_call | solution.py:45
  197.2 4.9 %shard_map.123 = (bf16[640,512]{1,0:T(8,128)(2,1)}, bf16[640,512]{1,0:T(8,128)(2,1)}) custom-call(s32[34]{0:T(128)} %concatenate.31.at_ref, bf16[640,896]{1,0:T(8,128)(2,1)} %collective-permute-done.22.rows_ref, bf16[2,896,512]{2,1,0:T(8,128)(2,1)} %shard_map.117.w_ref), custom_call_target="tpu_custom_call" | custom-call | flops 20000000000 | bytes 1 | tf_op jit(solution)/shard_map/pallas_call | solution.py:45
  202.1 4.4 %shard_map.124 = (bf16[256,512]{1,0:T(8,128)(2,1)}, f32[4,320,256]{2,1,0:T(8,128)}) custom-call(s32[34]{0:T(128)} %concatenate.31.at_ref, bf16[2,320,512]{2,1,0:T(8,128)(2,1)} %shard_map.120.q_ref, bf16[2,5,64,512]{3,2,1,0:T(8,128)(2,1)} %bitcast.46, bf16[2,5,64,512]{3,2,1,0:T(8,128)(2,1)} %bitcast.48, bf16[2,5,64,512]{3,2,1,0:T(8,128)(2,1)} %bitcast.50, ...), custom_call_target="tpu_custom_call" | custom-call | flops 20000000000 | bytes 1 | tf_op jit(solution)/shard_map/pallas_call | solution.py:45
  206.5 5.9 %shard_map.125.rest_0_ = f32[512,512]{1,0:T(8,128)} custom-call(s32[4]{0:T(128)} %pad_add_fusion.3.at_ref, bf16[4,2,256,1024]{3,2,1,0:T(8,128)(2,1)} %bitcast.33, bf16[4,2,256,1024]{3,2,1,0:T(8,128)(2,1)} %bitcast.36, bf16[4096,512]{1,0:T(8,128)(2,1)} %shard_map.116.w_ref.refs_2_), custom_call_target="tpu_custom_call" | custom-call | flops 20000000000 | bytes 1 | tf_op jit(solution)/shard_map/pallas_call | solution.py:45
  217.9 4.5 %shard_map.127 = bf16[2,512,1024]{2,1,0:T(8,128)(2,1)} custom-call(s32[2]{0:T(128)} %pad_add_fusion.5.at_ref, bf16[256,512]{1,0:T(8,128)(2,1)} %get-tuple-element.95.own_ref.own_rows_ref, bf16[256,512]{1,0:T(8,128)(2,1)} %get-tuple-element.109.other_ref.other_rows_ref, bf16[4096,512]{1,0:T(8,128)(2,1)} %shard_map.126.w_ref), custom_call_target="tpu_custom_call" | custom-call | flops 20000000000 | bytes 1 | tf_op jit(solution)/shard_map/pallas_call | solution.py:45
  223.0 6.2 %shard_map.128.d_ref = bf16[2,320,512]{2,1,0:T(8,128)(2,1)} custom-call(s32[4]{0:T(128)} %pad_add_fusion.4.at_ref, bf16[4,2,256,1024]{3,2,1,0:T(8,128)(2,1)} %bitcast.34, bf16[4,2,256,1024]{3,2,1,0:T(8,128)(2,1)} %bitcast.37, bf16[4096,512]{1,0:T(8,128)(2,1)} %shard_map.126.w_ref, f32[512,512]{1,0:T(8,128)} %shard_map.125.rest_0_), custom_call_target="tpu_custom_call" | custom-call | flops 20000000000 | bytes 1 | tf_op jit(solution)/shard_map/pallas_call | solution.py:45
  229.3 5.4 %shard_map.129 = (bf16[256,1024]{1,0:T(8,128)(2,1)}, bf16[256,1024]{1,0:T(8,128)(2,1)}, bf16[256,1024]{1,0:T(8,128)(2,1)}, f32[256,1024]{1,0:T(8,128)}) custom-call(s32[2]{0:T(128)} %pad_add_fusion.2.at_ref, bf16[256,512]{1,0:T(8,128)(2,1)} %get-tuple-element.95.own_ref.own_rows_ref, bf16[256,512]{1,0:T(8,128)(2,1)} %get-tuple-element.109.other_ref.other_rows_ref, ...), custom_call_target="tpu_custom_call" | custom-call | flops 20000000000 | bytes 1 | tf_op jit(solution)/shard_map/pallas_call | solution.py:45
  238.1 4.4 %shard_map.131.other_ref.other_rows_ref = bf16[256,512]{1,0:T(8,128)(2,1)} custom-call(s32[34]{0:T(128)} %concatenate.31.at_ref, f32[4,320,256]{2,1,0:T(8,128)} %get-tuple-element.116.prob_ref, bf16[2,320,512]{2,1,0:T(8,128)(2,1)} %shard_map.128.d_ref, bf16[2,5,64,512]{3,2,1,0:T(8,128)(2,1)} %bitcast.47, bf16[2,5,64,512]{3,2,1,0:T(8,128)(2,1)} %bitcast.49, ...), custom_call_target="tpu_custom_call" | custom-call | flops 20000000000 | bytes 1 | tf_op jit(solution)/shard_map/pallas_call | solution.py:45
  242.5 4.4 %shard_map.130.own_ref.own_rows_ref = bf16[256,512]{1,0:T(8,128)(2,1)} custom-call(s32[34]{0:T(128)} %concatenate.31.at_ref, f32[4,320,256]{2,1,0:T(8,128)} %get-tuple-element.114.prob_ref, bf16[2,320,512]{2,1,0:T(8,128)(2,1)} %shard_map.128.d_ref, bf16[2,5,64,512]{3,2,1,0:T(8,128)(2,1)} %bitcast.39, bf16[2,5,64,512]{3,2,1,0:T(8,128)(2,1)} %bitcast.41, ...), custom_call_target="tpu_custom_call" | custom-call | flops 20000000000 | bytes 1 | tf_op jit(solution)/shard_map/pallas_call | solution.py:45
  246.9 4.5 %shard_map.132 = bf16[2,512,1024]{2,1,0:T(8,128)(2,1)} custom-call(s32[2]{0:T(128)} %pad_add_fusion.5.at_ref, bf16[256,512]{1,0:T(8,128)(2,1)} %shard_map.130.own_ref.own_rows_ref, bf16[256,512]{1,0:T(8,128)(2,1)} %shard_map.131.other_ref.other_rows_ref, bf16[4096,512]{1,0:T(8,128)(2,1)} %shard_map.115.w_ref), custom_call_target="tpu_custom_call" | custom-call | flops 20000000000 | bytes 1 | tf_op jit(solution)/shard_map/pallas_call | solution.py:45
  251.4 9.1 %collective-permute-done.27 = bf16[256,1024]{1,0:T(8,128)(2,1)} collective-permute-done((bf16[256,1024]{1,0:T(8,128)(2,1)}, bf16[256,1024]{1,0:T(8,128)(2,1)}, u32[]{:S(2)}, u32[]{:S(2)}) %collective-permute-start.27) | collective-permute-done | bytes 524320 | tf_op jit(solution)/shard_map/ppermute | solution.py:19
  260.6 4.5 %collective-permute-done.29.add_ref = bf16[2,512,1024]{2,1,0:T(8,128)(2,1)} collective-permute-done((bf16[2,512,1024]{2,1,0:T(8,128)(2,1)}, bf16[2,512,1024]{2,1,0:T(8,128)(2,1)}, u32[]{:S(2)}, u32[]{:S(2)}) %collective-permute-start.29) | collective-permute-done | bytes 2097184 | tf_op jit(solution)/shard_map/ppermute | solution.py:19
  265.1 5.4 %shard_map.133 = (bf16[256,1024]{1,0:T(8,128)(2,1)}, bf16[256,1024]{1,0:T(8,128)(2,1)}, bf16[256,1024]{1,0:T(8,128)(2,1)}, f32[256,1024]{1,0:T(8,128)}) custom-call(s32[2]{0:T(128)} %pad_add_fusion.2.at_ref, bf16[256,512]{1,0:T(8,128)(2,1)} %shard_map.130.own_ref.own_rows_ref, bf16[256,512]{1,0:T(8,128)(2,1)} %shard_map.131.other_ref.other_rows_ref, ...), custom_call_target="tpu_custom_call" | custom-call | flops 20000000000 | bytes 1 | tf_op jit(solution)/shard_map/pallas_call | solution.py:45
  276.2 9.2 %collective-permute-done.30 = bf16[256,1024]{1,0:T(8,128)(2,1)S(1)} collective-permute-done((bf16[256,1024]{1,0:T(8,128)(2,1)}, bf16[256,1024]{1,0:T(8,128)(2,1)S(1)}, u32[]{:S(2)}, u32[]{:S(2)}) %collective-permute-start.30) | collective-permute-done | bytes 524320 | tf_op jit(solution)/shard_map/ppermute | solution.py:19
  285.4 11.9 %collective-permute-done.31 = bf16[256,1024]{1,0:T(8,128)(2,1)S(1)} collective-permute-done((bf16[256,1024]{1,0:T(8,128)(2,1)}, bf16[256,1024]{1,0:T(8,128)(2,1)S(1)}, u32[]{:S(2)}, u32[]{:S(2)}) %collective-permute-start.31) | collective-permute-done | bytes 524320 | tf_op jit(solution)/shard_map/ppermute | solution.py:19
  (135 shorter events, 82.2 us)
Async XLA Ops:
  7.2 72.0 %all-gather.5.cloned.1.call-start = ((), (), s32[]{:S(2)}) async-start(), calls=%async_computation | async-start | bytes 5242880 | tf_op jit(solution)/shard_map/all_gather | solution.py:467
  11.8 163.5 %all-gather.7.cloned.1.call-start = ((), (), s32[]{:S(2)}) async-start(), calls=%async_computation.1 | async-start | bytes 5242880 | tf_op jit(solution)/shard_map/all_gather | solution.py:467
  11.9 32.1 %collective-permute-start.2 = (bf16[896,896]{1,0:T(8,128)(2,1)}, bf16[896,896]{1,0:T(8,128)(2,1)}, u32[]{:S(2)}, u32[]{:S(2)}) collective-permute-start(bf16[896,896]{1,0:T(8,128)(2,1)} %up_ref.1), channel_id=1, source_target_pairs={{0,1},{1,0},{2,3},{3,2},{4,5},{5,4},{6,7},{7,6},{8,9},{9,8},{10,11... | collective-permute-start | bytes 4816904 | tf_op jit(solution)/shard_map/ppermute | solution.py:19
  12.4 31.6 %collective-permute-start.3 = (bf16[896,896]{1,0:T(8,128)(2,1)}, bf16[896,896]{1,0:T(8,128)(2,1)}, u32[]{:S(2)}, u32[]{:S(2)}) collective-permute-start(bf16[896,896]{1,0:T(8,128)(2,1)} %down_ref.1), channel_id=1, source_target_pairs={{0,1},{1,0},{2,3},{3,2},{4,5},{5,4},{6,7},{7,6},{8,9},{9,8},{10,11... | collective-permute-start | bytes 4816904 | tf_op jit(solution)/shard_map/ppermute | solution.py:19
  12.5 31.5 %collective-permute-start.1 = (bf16[736,512]{1,0:T(8,128)(2,1)}, bf16[736,512]{1,0:T(8,128)(2,1)S(1)}, u32[]{:S(2)}, u32[]{:S(2)}) collective-permute-start(bf16[736,512]{1,0:T(8,128)(2,1)} %get-tuple-element.63), channel_id=1, source_target_pairs={{0,8},{8,0},{1,9},{9,1},{2,10},{10,2},{3,11},{11,3},{4,12},{12,4},... | collective-permute-start | bytes 2261000 | tf_op jit(solution)/shard_map/ppermute | solution.py:19
  15.5 27.9 %collective-permute-start = (bf16[512,512]{1,0:T(8,128)(2,1)}, bf16[512,512]{1,0:T(8,128)(2,1)}, u32[]{:S(2)}, u32[]{:S(2)}) collective-permute-start(bf16[512,512]{1,0:T(8,128)(2,1)} %get-tuple-element.86.refs_0_), channel_id=1, source_target_pairs={{0,16},{16,0},{1,17},{17,1},{2,18},{18,2},{3,19},{19,3},{4,20},{20... | collective-permute-start | bytes 1572872 | tf_op jit(solution)/shard_map/ppermute | solution.py:24
  18.1 29.8 %collective-permute-start.4 = (bf16[1248,512]{1,0:T(8,128)(2,1)}, bf16[1248,512]{1,0:T(8,128)(2,1)}, u32[]{:S(2)}, u32[]{:S(2)}) collective-permute-start(bf16[1248,512]{1,0:T(8,128)(2,1)} %get-tuple-element.67), channel_id=1, source_target_pairs={{0,4},{4,0},{1,5},{5,1},{2,6},{6,2},{3,7},{7,3},{8,12},{12,8},{9,1... | collective-permute-start | bytes 3833864 | tf_op jit(solution)/shard_map/ppermute | solution.py:19
  48.1 21.7 %collective-permute-start.6 = (bf16[512,896]{1,0:T(8,128)(2,1)S(1)}, bf16[512,896]{1,0:T(8,128)(2,1)S(1)}, u32[]{:S(2)}, u32[]{:S(2)}) collective-permute-start(bf16[512,896]{1,0:T(8,128)(2,1)S(1)} %add.214), channel_id=1, source_target_pairs={{0,2},{2,0},{1,3},{3,1},{4,6},{6,4},{5,7},{7,5},{8,10},{10,8},{9,1... | collective-permute-start | bytes 2752520 | tf_op jit(solution)/shard_map/ppermute | solution.py:19
  49.7 29.4 %collective-permute-start.7 = (bf16[736,512]{1,0:T(8,128)(2,1)}, bf16[736,512]{1,0:T(8,128)(2,1)}, u32[]{:S(2)}, u32[]{:S(2)}) collective-permute-start(bf16[736,512]{1,0:T(8,128)(2,1)} %copy-done.5), channel_id=1, source_target_pairs={{0,4},{4,0},{1,5},{5,1},{2,6},{6,2},{3,7},{7,3},{8,12},{12,8},{9,1... | collective-permute-start | bytes 2261000 | tf_op jit(solution)/shard_map/ppermute | solution.py:19
  53.1 25.0 %collective-permute-start.9 = (bf16[512,512]{1,0:T(8,128)(2,1)}, bf16[512,512]{1,0:T(8,128)(2,1)S(1)}, u32[]{:S(2)}, u32[]{:S(2)}) collective-permute-start(bf16[512,512]{1,0:T(8,128)(2,1)} %slice.9), channel_id=1, source_target_pairs={{0,16},{16,0},{1,17},{17,1},{2,18},{18,2},{3,19},{19,3},{4,20},{20... | collective-permute-start | bytes 1572872 | tf_op jit(solution)/shard_map/ppermute | solution.py:24
  55.0 24.1 %collective-permute-start.8 = (bf16[512,512]{1,0:T(8,128)(2,1)}, bf16[512,512]{1,0:T(8,128)(2,1)}, u32[]{:S(2)}, u32[]{:S(2)}) collective-permute-start(bf16[512,512]{1,0:T(8,128)(2,1)} %collective-permute-done.refs_4_), channel_id=1, source_target_pairs={{0,4},{4,0},{1,5},{5,1},{2,6},{6,2},{3,7},{7,3},{8,12},{12,8},{9,1... | collective-permute-start | bytes 1572872 | tf_op jit(solution)/shard_map/ppermute | solution.py:19
  55.5 23.6 %collective-permute-start.10 = (bf16[512,512]{1,0:T(8,128)(2,1)}, bf16[512,512]{1,0:T(8,128)(2,1)}, u32[]{:S(2)}, u32[]{:S(2)}) collective-permute-start(bf16[512,512]{1,0:T(8,128)(2,1)} %get-tuple-element.72), channel_id=1, source_target_pairs={{0,8},{8,0},{1,9},{9,1},{2,10},{10,2},{3,11},{11,3},{4,12},{12,4},... | collective-permute-start | bytes 1572872 | tf_op jit(solution)/shard_map/ppermute | solution.py:19
  79.1 13.6 %collective-permute-start.12 = (bf16[224,512]{1,0:T(8,128)(2,1)}, bf16[224,512]{1,0:T(8,128)(2,1)S(1)}, u32[]{:S(2)}, u32[]{:S(2)}) collective-permute-start(bf16[224,512]{1,0:T(8,128)(2,1)} %get-tuple-element.88.refs_0_.refs_1_), channel_id=1, source_target_pairs={{0,16},{16,0},{1,17},{17,1},{2,18},{18,2},{3,19},{19,3},{4,20},{20... | collective-permute-start | bytes 688136 | tf_op jit(solution)/shard_map/ppermute | solution.py:24
  81.8 32.5 %collective-permute-start.11 = (bf16[2,256,1024]{2,1,0:T(8,128)(2,1)S(1)}, bf16[2,256,1024]{2,1,0:T(8,128)(2,1)}, u32[]{:S(2)}, u32[]{:S(2)}) collective-permute-start(bf16[2,256,1024]{2,1,0:T(8,128)(2,1)S(1)} %copy-done.3), channel_id=1, source_target_pairs={{0,8},{8,0},{1,9},{9,1},{2,10},{10,2},{3,11},{11,3},{4,12},{12,4},... | collective-permute-start | bytes 3145736 | tf_op jit(solution)/shard_map/ppermute | solution.py:19
  93.9 11.0 %collective-permute-start.13 = (bf16[256,896]{1,0:T(8,128)(2,1)S(1)}, bf16[256,896]{1,0:T(8,128)(2,1)}, u32[]{:S(2)}, u32[]{:S(2)}) collective-permute-start(bf16[256,896]{1,0:T(8,128)(2,1)S(1)} %constant_dynamic-slice_fusion), channel_id=1, source_target_pairs={{0,2},{2,0},{1,3},{3,1},{4,6},{6,4},{5,7},{7,5},{8,10},{10,8},{9,1... | collective-permute-start | bytes 1376264 | tf_op jit(solution)/shard_map/ppermute | solution.py:19
  94.6 18.9 %collective-permute-start.14 = (bf16[512,512]{1,0:T(8,128)(2,1)}, bf16[512,512]{1,0:T(8,128)(2,1)}, u32[]{:S(2)}, u32[]{:S(2)}) collective-permute-start(bf16[512,512]{1,0:T(8,128)(2,1)} %collective-permute-done.10.refs_2_), channel_id=1, source_target_pairs={{0,4},{4,0},{1,5},{5,1},{2,6},{6,2},{3,7},{7,3},{8,12},{12,8},{9,1... | collective-permute-start | bytes 1572872 | tf_op jit(solution)/shard_map/ppermute | solution.py:19
  97.6 15.8 %collective-permute-start.15 = (bf16[224,512]{1,0:T(8,128)(2,1)S(1)}, bf16[224,512]{1,0:T(8,128)(2,1)}, u32[]{:S(2)}, u32[]{:S(2)}) collective-permute-start(bf16[224,512]{1,0:T(8,128)(2,1)S(1)} %slice.10), channel_id=1, source_target_pairs={{0,16},{16,0},{1,17},{17,1},{2,18},{18,2},{3,19},{19,3},{4,20},{20... | collective-permute-start | bytes 688136 | tf_op jit(solution)/shard_map/ppermute | solution.py:24
  114.6 7.0 %collective-permute-start.16 = (bf16[64,896]{1,0:T(8,128)(2,1)S(1)}, bf16[64,896]{1,0:T(8,128)(2,1)S(1)}, u32[]{:S(2)}, u32[]{:S(2)}) collective-permute-start(bf16[64,896]{1,0:T(8,128)(2,1)S(1)} %slice.14), channel_id=1, source_target_pairs={{0,4},{4,8},{8,12},{12,16},{16,20},{20,24},{24,28},{1,5},{5,9},{9,... | collective-permute-start | bytes 344072 | tf_op jit(solution)/shard_map/ppermute | solution.py:511
  122.4 18.2 %collective-permute-start.17 = (bf16[320,896]{1,0:T(8,128)(2,1)}, bf16[320,896]{1,0:T(8,128)(2,1)S(1)}, u32[]{:S(2)}, u32[]{:S(2)}) collective-permute-start(bf16[320,896]{1,0:T(8,128)(2,1)} %pad_maximum_fusion.2), channel_id=1, source_target_pairs={{0,2},{2,0},{1,3},{3,1},{4,6},{6,4},{5,7},{7,5},{8,10},{10,8},{9,1... | collective-permute-start | bytes 1720328 | tf_op jit(solution)/shard_map/ppermute | solution.py:19
  126.1 22.5 %collective-permute-start.18 = (bf16[960,512]{1,0:T(8,128)(2,1)}, bf16[960,512]{1,0:T(8,128)(2,1)}, u32[]{:S(2)}, u32[]{:S(2)}) collective-permute-start(bf16[960,512]{1,0:T(8,128)(2,1)} %constant_dynamic-update-slice_fusion.refs_5_), channel_id=1, source_target_pairs={{0,4},{4,0},{1,5},{5,1},{2,6},{6,2},{3,7},{7,3},{8,12},{12,8},{9,1... | collective-permute-start | bytes 2949128 | tf_op jit(solution)/shard_map/ppermute | solution.py:19
  133.2 54.4 %collective-permute-start.21 = (bf16[320,896]{1,0:T(8,128)(2,1)}, bf16[320,896]{1,0:T(8,128)(2,1)}, u32[]{:S(2)}, u32[]{:S(2)}) collective-permute-start(bf16[320,896]{1,0:T(8,128)(2,1)} %pad_maximum_fusion.2), channel_id=1, source_target_pairs={{0,10},{2,8},{8,2},{10,0},{1,11},{3,9},{9,3},{11,1},{4,14},{6,12},... | collective-permute-start | bytes 1720328 | tf_op jit(solution)/shard_map/ppermute | solution.py:518
  135.4 52.1 %collective-permute-start.20 = (bf16[320,896]{1,0:T(8,128)(2,1)}, bf16[320,896]{1,0:T(8,128)(2,1)}, u32[]{:S(2)}, u32[]{:S(2)}) collective-permute-start(bf16[320,896]{1,0:T(8,128)(2,1)} %pad_maximum_fusion.2), channel_id=1, source_target_pairs={{0,8},{8,0},{1,9},{9,1},{2,10},{10,2},{3,11},{11,3},{4,12},{12,4},... | collective-permute-start | bytes 1720328 | tf_op jit(solution)/shard_map/ppermute | solution.py:19
  138.4 49.2 %collective-permute-start.23 = (bf16[1024,512]{1,0:T(8,128)(2,1)}, bf16[1024,512]{1,0:T(8,128)(2,1)}, u32[]{:S(2)}, u32[]{:S(2)}) collective-permute-start(bf16[1024,512]{1,0:T(8,128)(2,1)} %pad_maximum_fusion.1), channel_id=1, source_target_pairs={{0,16},{16,0},{1,17},{17,1},{2,18},{18,2},{3,19},{19,3},{4,20},{20... | collective-permute-start | bytes 3145736 | tf_op jit(solution)/shard_map/ppermute | solution.py:24
  149.9 13.5 %collective-permute-start.19 = (bf16[640,896]{1,0:T(8,128)(2,1)S(1)}, bf16[640,896]{1,0:T(8,128)(2,1)}, u32[]{:S(2)}, u32[]{:S(2)}) collective-permute-start(bf16[640,896]{1,0:T(8,128)(2,1)S(1)} %pad_maximum_fusion.rows_ref), channel_id=1, source_target_pairs={{0,1},{1,0},{2,3},{3,2},{4,5},{5,4},{6,7},{7,6},{8,9},{9,8},{10,11... | collective-permute-start | bytes 3440648 | tf_op jit(solution)/shard_map/ppermute | solution.py:19
  188.7 25.7 %collective-permute-start.24 = (bf16[1024,512]{1,0:T(8,128)(2,1)}, bf16[1024,512]{1,0:T(8,128)(2,1)}, u32[]{:S(2)}, u32[]{:S(2)}) collective-permute-start(bf16[1024,512]{1,0:T(8,128)(2,1)} %collective-permute-done.23.refs_0_), channel_id=1, source_target_pairs={{0,4},{4,0},{1,5},{5,1},{2,6},{6,2},{3,7},{7,3},{8,12},{12,8},{9,1... | collective-permute-start | bytes 3145736 | tf_op jit(solution)/shard_map/ppermute | solution.py:19
  222.4 6.8 %collective-permute-start.25 = (bf16[2,512,1024]{2,1,0:T(8,128)(2,1)}, bf16[2,512,1024]{2,1,0:T(8,128)(2,1)}, u32[]{:S(2)}, u32[]{:S(2)}) collective-permute-start(bf16[2,512,1024]{2,1,0:T(8,128)(2,1)} %shard_map.127), channel_id=1, source_target_pairs={{0,1},{1,0},{2,3},{3,2},{4,5},{5,4},{6,7},{7,6},{8,9},{9,8},{10,11... | collective-permute-start | bytes 6291464 | tf_op jit(solution)/shard_map/ppermute | solution.py:19
  234.7 16.8 %collective-permute-start.26 = (bf16[256,1024]{1,0:T(8,128)(2,1)}, bf16[256,1024]{1,0:T(8,128)(2,1)S(1)}, u32[]{:S(2)}, u32[]{:S(2)}) collective-permute-start(bf16[256,1024]{1,0:T(8,128)(2,1)} %get-tuple-element.111), channel_id=1, source_target_pairs={{0,8},{8,0},{1,9},{9,1},{2,10},{10,2},{3,11},{11,3},{4,12},{12,4},... | collective-permute-start | bytes 1572872 | tf_op jit(solution)/shard_map/ppermute | solution.py:19
  234.7 25.9 %collective-permute-start.27 = (bf16[256,1024]{1,0:T(8,128)(2,1)}, bf16[256,1024]{1,0:T(8,128)(2,1)}, u32[]{:S(2)}, u32[]{:S(2)}) collective-permute-start(bf16[256,1024]{1,0:T(8,128)(2,1)} %get-tuple-element.112), channel_id=1, source_target_pairs={{0,2},{2,0},{1,3},{3,1},{4,6},{6,4},{5,7},{7,5},{8,10},{10,8},{9,1... | collective-permute-start | bytes 1572872 | tf_op jit(solution)/shard_map/ppermute | solution.py:19
  235.0 25.6 %collective-permute-start.28 = (bf16[256,1024]{1,0:T(8,128)(2,1)}, bf16[256,1024]{1,0:T(8,128)(2,1)}, u32[]{:S(2)}, u32[]{:S(2)}) collective-permute-start(bf16[256,1024]{1,0:T(8,128)(2,1)} %get-tuple-element.113), channel_id=1, source_target_pairs={{0,10},{2,8},{8,2},{10,0},{1,11},{3,9},{9,3},{11,1},{4,14},{6,12},... | collective-permute-start | bytes 1572872 | tf_op jit(solution)/shard_map/ppermute | solution.py:421
  270.4 15.0 %collective-permute-start.30 = (bf16[256,1024]{1,0:T(8,128)(2,1)}, bf16[256,1024]{1,0:T(8,128)(2,1)S(1)}, u32[]{:S(2)}, u32[]{:S(2)}) collective-permute-start(bf16[256,1024]{1,0:T(8,128)(2,1)} %get-tuple-element.119), channel_id=1, source_target_pairs={{0,8},{8,0},{1,9},{9,1},{2,10},{10,2},{3,11},{11,3},{4,12},{12,4},... | collective-permute-start | bytes 1572872 | tf_op jit(solution)/shard_map/ppermute | solution.py:19
  272.2 25.1 %collective-permute-start.31 = (bf16[256,1024]{1,0:T(8,128)(2,1)}, bf16[256,1024]{1,0:T(8,128)(2,1)S(1)}, u32[]{:S(2)}, u32[]{:S(2)}) collective-permute-start(bf16[256,1024]{1,0:T(8,128)(2,1)} %get-tuple-element.120), channel_id=1, source_target_pairs={{0,2},{2,0},{1,3},{3,1},{4,6},{6,4},{5,7},{7,5},{8,10},{10,8},{9,1... | collective-permute-start | bytes 1572872 | tf_op jit(solution)/shard_map/ppermute | solution.py:19
  272.5 24.8 %collective-permute-start.32 = (bf16[256,1024]{1,0:T(8,128)(2,1)}, bf16[256,1024]{1,0:T(8,128)(2,1)S(1)}, u32[]{:S(2)}, u32[]{:S(2)}) collective-permute-start(bf16[256,1024]{1,0:T(8,128)(2,1)} %get-tuple-element.121), channel_id=1, source_target_pairs={{0,10},{2,8},{8,2},{10,0},{1,11},{3,9},{9,3},{11,1},{4,14},{6,12},... | collective-permute-start | bytes 1572872 | tf_op jit(solution)/shard_map/ppermute | solution.py:421
  (18 other events, 184.9 us)
Sparse Core Ops, SparseCore 0:
  12.0 37.1 all-gather.4
  133.3 41.9 all-gather.6

commit v3 on v2

--- a/solution.py
+++ b/solution.py
@@ -622,7 +622,7 @@
     ]
     grad_sent = core_sums(d_query, wq)
     if arrived:
-        grad_sent = tie(grad_sent, *arrived)
+        grad_sent = tie(grad_sent, *arrived[1:])
     hidden_grad, _, _ = sum_heads(d_query, wq, grad_sent)
     return (cca_out, hidden_grad)
 

time: 307 us -> 297 us (0.967)
  waiting for transfers between devices: 95.3 us -> 86.1 us
    ppermute x24, waiting for transfers between devices: 69.1 us -> 46.5 us  [flip(): return lax.ppermute(shard, axis, [(0, 1), (1, 0)])]
    ppermute x2, waiting for transfers between devices: 0.01 us -> 13.4 us  [sum_heads(): lax.ppermute(to_both, ('zl', 'y'), [(i, 3 - i) for i in range(4)])]
  transfers between devices with their start and end apart: 35 -> 35, of which waited for: 17 -> 20; matrix products, arithmetic and copies ran while one was open for 13% -> 14% of each run, Pallas kernels for 27% -> 30%
where the time goes in v3:
time: 297 us; the launch traced here: 295 us
  Pallas kernels  107 us (36%)
  waiting for transfers between devices  86.1 us (29%)
  starting transfers between devices  41.7 us (14%)
  local copies, waits for them, and re-layouts  33.2 us (11%)
  between operations  14.3 us (5%)
  other arithmetic  13.1 us (4%)
    pallas_call x17, Pallas kernels, call(): pl.pallas_call(kernel, grid_spec=pltpu.PrefetchScalarGridSpec(num_scalar_...  90.4 us
    ppermute x24, waiting for transfers between devices, flip(): return lax.ppermute(shard, axis, [(0, 1), (1, 0)])  46.5 us
    ppermute x24, starting transfers between devices, flip(): return lax.ppermute(shard, axis, [(0, 1), (1, 0)])  22.8 us
    ppermute x5, waiting for transfers between devices, onward(): lax.ppermute(shard, axis, [(i, (i + 1) % count) for i in range(count)])  19.1 us
    gather x1, local copies, waits for them, and re-layouts, per_device(): embed_table.at[clipped].get(mode='promise_in_bounds')  18.9 us
    pallas_call x4, Pallas kernels, place(): pl.pallas_call(functools.partial(place_kernel, jobs, len(sources), int(th...  16.3 us
    ppermute x2, waiting for transfers between devices, sum_heads(): lax.ppermute(to_both, ('zl', 'y'), [(i, 3 - i) for i in range(4)])  13.4 us
    ppermute x5, starting transfers between devices, onward(): lax.ppermute(shard, axis, [(i, (i + 1) % count) for i in range(count)])  10.1 us
  transfers between devices with their start and end apart: 35, of which 20 were waited for; matrix products, arithmetic and copies ran while one was open for 14% of the time, Pallas kernels for 30%

profile of v3, /device:TPU:0, one launch (start us, length us, event | category | flops | bytes accessed | tf_op | source)
XLA Modules:
  0.0 295.2 jit_solution(11860902126048901547)
XLA Ops:
  7.2 4.6 %shard_map.113 = (bf16[736,512]{1,0:T(8,128)(2,1)}, bf16[512,512]{1,0:T(8,128)(2,1)}, bf16[1248,512]{1,0:T(8,128)(2,1)}, bf16[512,512]{1,0:T(8,128)(2,1)}, bf16[...) custom-call(s32[1]{0:T(128)} %bitcast.6.at_ref, bf16[512,8,128]{2,1,0:T(8,128)(2,1)} %q_ref.1, ...), custom_call_target="tpu_custom_call" | custom-call | flops 20000000000 | bytes 1 | tf_op jit(solution)/shard_map/pallas_call | solution.py:45
  19.8 18.9 %gather_fusion = bf16[1024,896]{1,0:T(8,128)(2,1)S(1)} fusion(bf16[16000,896]{1,0:T(8,128)(2,1)} %param.14, s32[1024]{0:T(1024)S(1)} %fusion), kind=kCustom, calls=%fused_computation | custom fusion | bytes 3674112 | tf_op jit(solution)/shard_map/gather | solution.py:476
  38.8 4.6 %collective-permute-done.refs_4_ = bf16[512,512]{1,0:T(8,128)(2,1)} collective-permute-done((bf16[512,512]{1,0:T(8,128)(2,1)}, bf16[512,512]{1,0:T(8,128)(2,1)}, u32[]{:S(2)}, u32[]{:S(2)}) %collective-permute-start) | collective-permute-done | bytes 524320 | tf_op jit(solution)/shard_map/ppermute | solution.py:24
  57.1 12.8 %collective-permute-done.6 = bf16[512,896]{1,0:T(8,128)(2,1)S(1)} collective-permute-done((bf16[512,896]{1,0:T(8,128)(2,1)S(1)}, bf16[512,896]{1,0:T(8,128)(2,1)S(1)}, u32[]{:S(2)}, u32[]{:S(2)}) %collective-permute-start.6) | collective-permute-done | bytes 917536 | tf_op jit(solution)/shard_map/ppermute | solution.py:19
  71.1 7.1 %collective-permute-done.9 = bf16[512,512]{1,0:T(8,128)(2,1)S(1)} collective-permute-done((bf16[512,512]{1,0:T(8,128)(2,1)}, bf16[512,512]{1,0:T(8,128)(2,1)S(1)}, u32[]{:S(2)}, u32[]{:S(2)}) %collective-permute-start.9) | collective-permute-done | bytes 524320 | tf_op jit(solution)/shard_map/ppermute | solution.py:24
  83.4 9.3 %shard_map.114 = (bf16[512,896]{1,0:T(8,128)(2,1)}, f32[256,896]{1,0:T(8,128)}) custom-call(s32[1]{0:T(128)} %bitcast.9.at_ref, bf16[512,896]{1,0:T(8,128)(2,1)} %add.215.emb_ref, bf16[896,896]{1,0:T(8,128)(2,1)} %up_ref.1, bf16[896,896]{1,0:T(8,128)(2,1)} %down_ref.1, bf16[896,896]{1,0:T(8,128)(2,1)} %collective-permute-done.2.up2_ref, ...), custom_call_target="tpu_custom_call" | custom-call | flops 20000000000 | bytes 1 | tf_op jit(solution)/shard_map/pallas_call | solution.py:45
  99.1 5.8 %collective-permute-done.13 = bf16[256,896]{1,0:T(8,128)(2,1)} collective-permute-done((bf16[256,896]{1,0:T(8,128)(2,1)S(1)}, bf16[256,896]{1,0:T(8,128)(2,1)}, u32[]{:S(2)}, u32[]{:S(2)}) %collective-permute-start.13) | collective-permute-done | bytes 458784 | tf_op jit(solution)/shard_map/ppermute | solution.py:19
  106.1 7.4 %collective-permute-done.15 = bf16[224,512]{1,0:T(8,128)(2,1)} collective-permute-done((bf16[224,512]{1,0:T(8,128)(2,1)S(1)}, bf16[224,512]{1,0:T(8,128)(2,1)}, u32[]{:S(2)}, u32[]{:S(2)}) %collective-permute-start.15) | collective-permute-done | bytes 229408 | tf_op jit(solution)/shard_map/ppermute | solution.py:24
  114.6 3.6 %collective-permute-start.16 = (bf16[64,896]{1,0:T(8,128)(2,1)S(1)}, bf16[64,896]{1,0:T(8,128)(2,1)S(1)}, u32[]{:S(2)}, u32[]{:S(2)}) collective-permute-start(bf16[64,896]{1,0:T(8,128)(2,1)S(1)} %slice.14), channel_id=1, source_target_pairs={{0,4},{4,8},{8,12},{12,16},{16,20},{20,24},{24,28},{1,5},{5,9},{9,... | collective-permute-start | bytes 344072 | tf_op jit(solution)/shard_map/ppermute | solution.py:511
  128.9 4.3 %shard_map.116.w_ref.refs_2_ = bf16[4096,512]{1,0:T(8,128)(2,1)} custom-call(s32[4]{0:T(128)} %pad_add_fusion.3.at_ref, bf16[512,512]{1,0:T(8,128)(2,1)} %get-tuple-element.104.refs_0_, bf16[1248,512]{1,0:T(8,128)(2,1)} %collective-permute-done.4.refs_1_.refs_2_, bf16[512,512]{1,0:T(8,128)(2,1)} %collective-permute-done.10.refs_2_, ...), custom_call_target="tpu_custom_call" | custom-call | flops 20000000000 | bytes 1 | tf_op jit(solution)/shard_map/pallas_call | solution.py:164
  141.4 7.3 %collective-permute-done.18.refs_7_.refs_6_ = bf16[960,512]{1,0:T(8,128)(2,1)} collective-permute-done((bf16[960,512]{1,0:T(8,128)(2,1)}, bf16[960,512]{1,0:T(8,128)(2,1)}, u32[]{:S(2)}, u32[]{:S(2)}) %collective-permute-start.18) | collective-permute-done | bytes 983072 | tf_op jit(solution)/shard_map/ppermute | solution.py:19
  149.9 3.6 %shard_map.117.w_ref = bf16[2,896,512]{2,1,0:T(8,128)(2,1)} custom-call(s32[16]{0:T(128)} %stack.61.at_ref, bf16[224,512]{1,0:T(8,128)(2,1)} %get-tuple-element.88.refs_0_.refs_1_, bf16[224,512]{1,0:T(8,128)(2,1)} %get-tuple-element.88.refs_0_.refs_1_, bf16[1248,512]{1,0:T(8,128)(2,1)} %collective-permute-done.4.refs_1_.refs_2_, bf16[736,512]{1,0:T(8,128)(2,1)} %copy-done.5, ...), custom_call_target="tpu_custom_call" | custom-call | flops 20000000000 | bytes 1 | tf_op jit(solution)/shard_map/pallas_call | solution.py:164
  153.5 4.9 %shard_map.118 = (bf16[640,512]{1,0:T(8,128)(2,1)}, bf16[640,512]{1,0:T(8,128)(2,1)}) custom-call(s32[34]{0:T(128)} %concatenate.31.at_ref, bf16[640,896]{1,0:T(8,128)(2,1)} %copy-done, bf16[2,896,512]{2,1,0:T(8,128)(2,1)} %shard_map.117.w_ref), custom_call_target="tpu_custom_call" | custom-call | flops 20000000000 | bytes 1 | tf_op jit(solution)/shard_map/pallas_call | solution.py:45
  158.5 4.9 %shard_map.115.w_ref = bf16[4096,512]{1,0:T(8,128)(2,1)} custom-call(s32[8]{0:T(128)} %stack.59.at_ref, bf16[512,512]{1,0:T(8,128)(2,1)} %get-tuple-element.86.refs_0_, bf16[1248,512]{1,0:T(8,128)(2,1)} %collective-permute-done.4.refs_1_.refs_2_, bf16[736,512]{1,0:T(8,128)(2,1)} %copy-done.5, bf16[736,512]{1,0:T(8,128)(2,1)} %collective-permute-done.7.refs_3_.refs_4_, ...), custom_call_target="tpu_custom_call" | custom-call | flops 20000000000 | bytes 1 | tf_op jit(solution)/shard_map/pallas_call | solution.py:164
  163.4 4.9 %shard_map.119 = (bf16[640,512]{1,0:T(8,128)(2,1)}, bf16[640,512]{1,0:T(8,128)(2,1)}) custom-call(s32[34]{0:T(128)} %concatenate.31.at_ref, bf16[640,896]{1,0:T(8,128)(2,1)} %collective-permute-done.19.rows_ref, bf16[2,896,512]{2,1,0:T(8,128)(2,1)} %shard_map.117.w_ref), custom_call_target="tpu_custom_call" | custom-call | flops 20000000000 | bytes 1 | tf_op jit(solution)/shard_map/pallas_call | solution.py:45
  168.3 7.0 %all-gather.7.cloned.1.call-done = bf16[8,256,1024]{2,1,0:T(8,128)(2,1)} async-done(((bf16[2,256,1024]{2,1,0:T(8,128)(2,1)}), bf16[8,256,1024]{2,1,0:T(8,128)(2,1)}) %all-gather.7.cloned.1.call-update) | async-done | bytes 4194320 | tf_op jit(solution)/shard_map/all_gather | solution.py:467
  175.8 7.3 %shard_map.120.q_ref = bf16[2,320,512]{2,1,0:T(8,128)(2,1)} custom-call(s32[4]{0:T(128)} %iota.13.at_ref, bf16[4,2,256,1024]{3,2,1,0:T(8,128)(2,1)} %bitcast.32, bf16[4,2,256,1024]{3,2,1,0:T(8,128)(2,1)} %bitcast.35, bf16[4096,512]{1,0:T(8,128)(2,1)} %shard_map.115.w_ref), custom_call_target="tpu_custom_call" | custom-call | flops 20000000000 | bytes 1 | tf_op jit(solution)/shard_map/pallas_call | solution.py:45
  183.1 4.5 %shard_map.121 = (bf16[256,512]{1,0:T(8,128)(2,1)}, f32[4,320,256]{2,1,0:T(8,128)}) custom-call(s32[34]{0:T(128)} %concatenate.31.at_ref, bf16[2,320,512]{2,1,0:T(8,128)(2,1)} %shard_map.120.q_ref, bf16[2,5,64,512]{3,2,1,0:T(8,128)(2,1)} %bitcast.38, bf16[2,5,64,512]{3,2,1,0:T(8,128)(2,1)} %bitcast.40, bf16[2,5,64,512]{3,2,1,0:T(8,128)(2,1)} %bitcast.42, ...), custom_call_target="tpu_custom_call" | custom-call | flops 20000000000 | bytes 1 | tf_op jit(solution)/shard_map/pallas_call | solution.py:45
  192.3 4.9 %shard_map.122 = (bf16[640,512]{1,0:T(8,128)(2,1)}, bf16[640,512]{1,0:T(8,128)(2,1)}) custom-call(s32[34]{0:T(128)} %concatenate.31.at_ref, bf16[640,896]{1,0:T(8,128)(2,1)} %copy-done.10, bf16[2,896,512]{2,1,0:T(8,128)(2,1)} %shard_map.117.w_ref), custom_call_target="tpu_custom_call" | custom-call | flops 20000000000 | bytes 1 | tf_op jit(solution)/shard_map/pallas_call | solution.py:45
  197.2 4.9 %shard_map.123 = (bf16[640,512]{1,0:T(8,128)(2,1)}, bf16[640,512]{1,0:T(8,128)(2,1)}) custom-call(s32[34]{0:T(128)} %concatenate.31.at_ref, bf16[640,896]{1,0:T(8,128)(2,1)} %collective-permute-done.22.rows_ref, bf16[2,896,512]{2,1,0:T(8,128)(2,1)} %shard_map.117.w_ref), custom_call_target="tpu_custom_call" | custom-call | flops 20000000000 | bytes 1 | tf_op jit(solution)/shard_map/pallas_call | solution.py:45
  202.1 4.4 %shard_map.124 = (bf16[256,512]{1,0:T(8,128)(2,1)}, f32[4,320,256]{2,1,0:T(8,128)}) custom-call(s32[34]{0:T(128)} %concatenate.31.at_ref, bf16[2,320,512]{2,1,0:T(8,128)(2,1)} %shard_map.120.q_ref, bf16[2,5,64,512]{3,2,1,0:T(8,128)(2,1)} %bitcast.46, bf16[2,5,64,512]{3,2,1,0:T(8,128)(2,1)} %bitcast.48, bf16[2,5,64,512]{3,2,1,0:T(8,128)(2,1)} %bitcast.50, ...), custom_call_target="tpu_custom_call" | custom-call | flops 20000000000 | bytes 1 | tf_op jit(solution)/shard_map/pallas_call | solution.py:45
  206.5 5.9 %shard_map.125.rest_0_ = f32[512,512]{1,0:T(8,128)} custom-call(s32[4]{0:T(128)} %pad_add_fusion.3.at_ref, bf16[4,2,256,1024]{3,2,1,0:T(8,128)(2,1)} %bitcast.33, bf16[4,2,256,1024]{3,2,1,0:T(8,128)(2,1)} %bitcast.36, bf16[4096,512]{1,0:T(8,128)(2,1)} %shard_map.116.w_ref.refs_2_), custom_call_target="tpu_custom_call" | custom-call | flops 20000000000 | bytes 1 | tf_op jit(solution)/shard_map/pallas_call | solution.py:45
  214.4 3.5 %shard_map.126.w_ref = bf16[4096,512]{1,0:T(8,128)(2,1)} custom-call(s32[4]{0:T(128)} %pad_add_fusion.4.at_ref, bf16[1024,512]{1,0:T(8,128)(2,1)} %collective-permute-done.23.refs_0_, bf16[1024,512]{1,0:T(8,128)(2,1)} %collective-permute-done.24.refs_1_, bf16[4096,512]{1,0:T(8,128)(2,1)} %shard_map.116.w_ref.refs_2_), custom_call_target="tpu_custom_call", output_to_operand_aliasing={{}: (3, {})} | custom-call | flops 20000000000 | bytes 1 | tf_op jit(solution)/shard_map/pallas_call | solution.py:164
  217.9 4.5 %shard_map.127 = bf16[2,512,1024]{2,1,0:T(8,128)(2,1)} custom-call(s32[2]{0:T(128)} %pad_add_fusion.5.at_ref, bf16[256,512]{1,0:T(8,128)(2,1)} %get-tuple-element.95.own_ref.own_rows_ref, bf16[256,512]{1,0:T(8,128)(2,1)} %get-tuple-element.109.other_ref.other_rows_ref, bf16[4096,512]{1,0:T(8,128)(2,1)} %shard_map.126.w_ref), custom_call_target="tpu_custom_call" | custom-call | flops 20000000000 | bytes 1 | tf_op jit(solution)/shard_map/pallas_call | solution.py:45
  223.0 6.2 %shard_map.128.d_ref = bf16[2,320,512]{2,1,0:T(8,128)(2,1)} custom-call(s32[4]{0:T(128)} %pad_add_fusion.4.at_ref, bf16[4,2,256,1024]{3,2,1,0:T(8,128)(2,1)} %bitcast.34, bf16[4,2,256,1024]{3,2,1,0:T(8,128)(2,1)} %bitcast.37, bf16[4096,512]{1,0:T(8,128)(2,1)} %shard_map.126.w_ref, f32[512,512]{1,0:T(8,128)} %shard_map.125.rest_0_), custom_call_target="tpu_custom_call" | custom-call | flops 20000000000 | bytes 1 | tf_op jit(solution)/shard_map/pallas_call | solution.py:45
  229.3 5.4 %shard_map.129 = (bf16[256,1024]{1,0:T(8,128)(2,1)}, bf16[256,1024]{1,0:T(8,128)(2,1)}, bf16[256,1024]{1,0:T(8,128)(2,1)}, f32[256,1024]{1,0:T(8,128)}) custom-call(s32[2]{0:T(128)} %pad_add_fusion.2.at_ref, bf16[256,512]{1,0:T(8,128)(2,1)} %get-tuple-element.95.own_ref.own_rows_ref, bf16[256,512]{1,0:T(8,128)(2,1)} %get-tuple-element.109.other_ref.other_rows_ref, ...), custom_call_target="tpu_custom_call" | custom-call | flops 20000000000 | bytes 1 | tf_op jit(solution)/shard_map/pallas_call | solution.py:45
  235.0 4.4 %shard_map.131.other_ref.other_rows_ref = bf16[256,512]{1,0:T(8,128)(2,1)} custom-call(s32[34]{0:T(128)} %concatenate.31.at_ref, f32[4,320,256]{2,1,0:T(8,128)} %get-tuple-element.116.prob_ref, bf16[2,320,512]{2,1,0:T(8,128)(2,1)} %shard_map.128.d_ref, bf16[2,5,64,512]{3,2,1,0:T(8,128)(2,1)} %bitcast.47, bf16[2,5,64,512]{3,2,1,0:T(8,128)(2,1)} %bitcast.49, ...), custom_call_target="tpu_custom_call" | custom-call | flops 20000000000 | bytes 1 | tf_op jit(solution)/shard_map/pallas_call | solution.py:45
  239.4 4.4 %shard_map.130.own_ref.own_rows_ref = bf16[256,512]{1,0:T(8,128)(2,1)} custom-call(s32[34]{0:T(128)} %concatenate.31.at_ref, f32[4,320,256]{2,1,0:T(8,128)} %get-tuple-element.114.prob_ref, bf16[2,320,512]{2,1,0:T(8,128)(2,1)} %shard_map.128.d_ref, bf16[2,5,64,512]{3,2,1,0:T(8,128)(2,1)} %bitcast.39, bf16[2,5,64,512]{3,2,1,0:T(8,128)(2,1)} %bitcast.41, ...), custom_call_target="tpu_custom_call" | custom-call | flops 20000000000 | bytes 1 | tf_op jit(solution)/shard_map/pallas_call | solution.py:45
  243.7 4.5 %shard_map.132 = bf16[2,512,1024]{2,1,0:T(8,128)(2,1)} custom-call(s32[2]{0:T(128)} %pad_add_fusion.5.at_ref, bf16[256,512]{1,0:T(8,128)(2,1)} %shard_map.130.own_ref.own_rows_ref, bf16[256,512]{1,0:T(8,128)(2,1)} %shard_map.131.other_ref.other_rows_ref, bf16[4096,512]{1,0:T(8,128)(2,1)} %shard_map.115.w_ref), custom_call_target="tpu_custom_call" | custom-call | flops 20000000000 | bytes 1 | tf_op jit(solution)/shard_map/pallas_call | solution.py:45
  253.8 5.4 %shard_map.133 = (bf16[256,1024]{1,0:T(8,128)(2,1)}, bf16[256,1024]{1,0:T(8,128)(2,1)}, bf16[256,1024]{1,0:T(8,128)(2,1)}, f32[256,1024]{1,0:T(8,128)}) custom-call(s32[2]{0:T(128)} %pad_add_fusion.2.at_ref, bf16[256,512]{1,0:T(8,128)(2,1)} %shard_map.130.own_ref.own_rows_ref, bf16[256,512]{1,0:T(8,128)(2,1)} %shard_map.131.other_ref.other_rows_ref, ...), custom_call_target="tpu_custom_call" | custom-call | flops 20000000000 | bytes 1 | tf_op jit(solution)/shard_map/pallas_call | solution.py:45
  267.6 8.3 %collective-permute-done.30 = bf16[256,1024]{1,0:T(8,128)(2,1)S(1)} collective-permute-done((bf16[256,1024]{1,0:T(8,128)(2,1)}, bf16[256,1024]{1,0:T(8,128)(2,1)S(1)}, u32[]{:S(2)}, u32[]{:S(2)}) %collective-permute-start.30) | collective-permute-done | bytes 524320 | tf_op jit(solution)/shard_map/ppermute | solution.py:19
  276.4 10.9 %collective-permute-done.32 = bf16[256,1024]{1,0:T(8,128)(2,1)S(1)} collective-permute-done((bf16[256,1024]{1,0:T(8,128)(2,1)}, bf16[256,1024]{1,0:T(8,128)(2,1)S(1)}, u32[]{:S(2)}, u32[]{:S(2)}) %collective-permute-start.32) | collective-permute-done | bytes 524320 | tf_op jit(solution)/shard_map/ppermute | solution.py:421
  (135 shorter events, 80.5 us)
Async XLA Ops:
  7.2 72.0 %all-gather.5.cloned.1.call-start = ((), (), s32[]{:S(2)}) async-start(), calls=%async_computation | async-start | bytes 5242880 | tf_op jit(solution)/shard_map/all_gather | solution.py:467
  11.8 163.5 %all-gather.7.cloned.1.call-start = ((), (), s32[]{:S(2)}) async-start(), calls=%async_computation.1 | async-start | bytes 5242880 | tf_op jit(solution)/shard_map/all_gather | solution.py:467
  11.9 32.1 %collective-permute-start.2 = (bf16[896,896]{1,0:T(8,128)(2,1)}, bf16[896,896]{1,0:T(8,128)(2,1)}, u32[]{:S(2)}, u32[]{:S(2)}) collective-permute-start(bf16[896,896]{1,0:T(8,128)(2,1)} %up_ref.1), channel_id=1, source_target_pairs={{0,1},{1,0},{2,3},{3,2},{4,5},{5,4},{6,7},{7,6},{8,9},{9,8},{10,11... | collective-permute-start | bytes 4816904 | tf_op jit(solution)/shard_map/ppermute | solution.py:19
  12.4 31.6 %collective-permute-start.3 = (bf16[896,896]{1,0:T(8,128)(2,1)}, bf16[896,896]{1,0:T(8,128)(2,1)}, u32[]{:S(2)}, u32[]{:S(2)}) collective-permute-start(bf16[896,896]{1,0:T(8,128)(2,1)} %down_ref.1), channel_id=1, source_target_pairs={{0,1},{1,0},{2,3},{3,2},{4,5},{5,4},{6,7},{7,6},{8,9},{9,8},{10,11... | collective-permute-start | bytes 4816904 | tf_op jit(solution)/shard_map/ppermute | solution.py:19
  12.5 31.5 %collective-permute-start.1 = (bf16[736,512]{1,0:T(8,128)(2,1)}, bf16[736,512]{1,0:T(8,128)(2,1)S(1)}, u32[]{:S(2)}, u32[]{:S(2)}) collective-permute-start(bf16[736,512]{1,0:T(8,128)(2,1)} %get-tuple-element.63), channel_id=1, source_target_pairs={{0,8},{8,0},{1,9},{9,1},{2,10},{10,2},{3,11},{11,3},{4,12},{12,4},... | collective-permute-start | bytes 2261000 | tf_op jit(solution)/shard_map/ppermute | solution.py:19
  15.5 27.9 %collective-permute-start = (bf16[512,512]{1,0:T(8,128)(2,1)}, bf16[512,512]{1,0:T(8,128)(2,1)}, u32[]{:S(2)}, u32[]{:S(2)}) collective-permute-start(bf16[512,512]{1,0:T(8,128)(2,1)} %get-tuple-element.86.refs_0_), channel_id=1, source_target_pairs={{0,16},{16,0},{1,17},{17,1},{2,18},{18,2},{3,19},{19,3},{4,20},{20... | collective-permute-start | bytes 1572872 | tf_op jit(solution)/shard_map/ppermute | solution.py:24
  18.1 29.8 %collective-permute-start.4 = (bf16[1248,512]{1,0:T(8,128)(2,1)}, bf16[1248,512]{1,0:T(8,128)(2,1)}, u32[]{:S(2)}, u32[]{:S(2)}) collective-permute-start(bf16[1248,512]{1,0:T(8,128)(2,1)} %get-tuple-element.67), channel_id=1, source_target_pairs={{0,4},{4,0},{1,5},{5,1},{2,6},{6,2},{3,7},{7,3},{8,12},{12,8},{9,1... | collective-permute-start | bytes 3833864 | tf_op jit(solution)/shard_map/ppermute | solution.py:19
  48.1 21.7 %collective-permute-start.6 = (bf16[512,896]{1,0:T(8,128)(2,1)S(1)}, bf16[512,896]{1,0:T(8,128)(2,1)S(1)}, u32[]{:S(2)}, u32[]{:S(2)}) collective-permute-start(bf16[512,896]{1,0:T(8,128)(2,1)S(1)} %add.214), channel_id=1, source_target_pairs={{0,2},{2,0},{1,3},{3,1},{4,6},{6,4},{5,7},{7,5},{8,10},{10,8},{9,1... | collective-permute-start | bytes 2752520 | tf_op jit(solution)/shard_map/ppermute | solution.py:19
  49.7 29.4 %collective-permute-start.7 = (bf16[736,512]{1,0:T(8,128)(2,1)}, bf16[736,512]{1,0:T(8,128)(2,1)}, u32[]{:S(2)}, u32[]{:S(2)}) collective-permute-start(bf16[736,512]{1,0:T(8,128)(2,1)} %copy-done.5), channel_id=1, source_target_pairs={{0,4},{4,0},{1,5},{5,1},{2,6},{6,2},{3,7},{7,3},{8,12},{12,8},{9,1... | collective-permute-start | bytes 2261000 | tf_op jit(solution)/shard_map/ppermute | solution.py:19
  53.1 25.0 %collective-permute-start.9 = (bf16[512,512]{1,0:T(8,128)(2,1)}, bf16[512,512]{1,0:T(8,128)(2,1)S(1)}, u32[]{:S(2)}, u32[]{:S(2)}) collective-permute-start(bf16[512,512]{1,0:T(8,128)(2,1)} %slice.9), channel_id=1, source_target_pairs={{0,16},{16,0},{1,17},{17,1},{2,18},{18,2},{3,19},{19,3},{4,20},{20... | collective-permute-start | bytes 1572872 | tf_op jit(solution)/shard_map/ppermute | solution.py:24
  55.0 24.1 %collective-permute-start.8 = (bf16[512,512]{1,0:T(8,128)(2,1)}, bf16[512,512]{1,0:T(8,128)(2,1)}, u32[]{:S(2)}, u32[]{:S(2)}) collective-permute-start(bf16[512,512]{1,0:T(8,128)(2,1)} %collective-permute-done.refs_4_), channel_id=1, source_target_pairs={{0,4},{4,0},{1,5},{5,1},{2,6},{6,2},{3,7},{7,3},{8,12},{12,8},{9,1... | collective-permute-start | bytes 1572872 | tf_op jit(solution)/shard_map/ppermute | solution.py:19
  55.5 23.6 %collective-permute-start.10 = (bf16[512,512]{1,0:T(8,128)(2,1)}, bf16[512,512]{1,0:T(8,128)(2,1)}, u32[]{:S(2)}, u32[]{:S(2)}) collective-permute-start(bf16[512,512]{1,0:T(8,128)(2,1)} %get-tuple-element.72), channel_id=1, source_target_pairs={{0,8},{8,0},{1,9},{9,1},{2,10},{10,2},{3,11},{11,3},{4,12},{12,4},... | collective-permute-start | bytes 1572872 | tf_op jit(solution)/shard_map/ppermute | solution.py:19
  79.1 13.6 %collective-permute-start.12 = (bf16[224,512]{1,0:T(8,128)(2,1)}, bf16[224,512]{1,0:T(8,128)(2,1)S(1)}, u32[]{:S(2)}, u32[]{:S(2)}) collective-permute-start(bf16[224,512]{1,0:T(8,128)(2,1)} %get-tuple-element.88.refs_0_.refs_1_), channel_id=1, source_target_pairs={{0,16},{16,0},{1,17},{17,1},{2,18},{18,2},{3,19},{19,3},{4,20},{20... | collective-permute-start | bytes 688136 | tf_op jit(solution)/shard_map/ppermute | solution.py:24
  81.8 32.5 %collective-permute-start.11 = (bf16[2,256,1024]{2,1,0:T(8,128)(2,1)S(1)}, bf16[2,256,1024]{2,1,0:T(8,128)(2,1)}, u32[]{:S(2)}, u32[]{:S(2)}) collective-permute-start(bf16[2,256,1024]{2,1,0:T(8,128)(2,1)S(1)} %copy-done.3), channel_id=1, source_target_pairs={{0,8},{8,0},{1,9},{9,1},{2,10},{10,2},{3,11},{11,3},{4,12},{12,4},... | collective-permute-start | bytes 3145736 | tf_op jit(solution)/shard_map/ppermute | solution.py:19
  93.9 11.0 %collective-permute-start.13 = (bf16[256,896]{1,0:T(8,128)(2,1)S(1)}, bf16[256,896]{1,0:T(8,128)(2,1)}, u32[]{:S(2)}, u32[]{:S(2)}) collective-permute-start(bf16[256,896]{1,0:T(8,128)(2,1)S(1)} %constant_dynamic-slice_fusion), channel_id=1, source_target_pairs={{0,2},{2,0},{1,3},{3,1},{4,6},{6,4},{5,7},{7,5},{8,10},{10,8},{9,1... | collective-permute-start | bytes 1376264 | tf_op jit(solution)/shard_map/ppermute | solution.py:19
  94.6 18.9 %collective-permute-start.14 = (bf16[512,512]{1,0:T(8,128)(2,1)}, bf16[512,512]{1,0:T(8,128)(2,1)}, u32[]{:S(2)}, u32[]{:S(2)}) collective-permute-start(bf16[512,512]{1,0:T(8,128)(2,1)} %collective-permute-done.10.refs_2_), channel_id=1, source_target_pairs={{0,4},{4,0},{1,5},{5,1},{2,6},{6,2},{3,7},{7,3},{8,12},{12,8},{9,1... | collective-permute-start | bytes 1572872 | tf_op jit(solution)/shard_map/ppermute | solution.py:19
  97.6 15.8 %collective-permute-start.15 = (bf16[224,512]{1,0:T(8,128)(2,1)S(1)}, bf16[224,512]{1,0:T(8,128)(2,1)}, u32[]{:S(2)}, u32[]{:S(2)}) collective-permute-start(bf16[224,512]{1,0:T(8,128)(2,1)S(1)} %slice.10), channel_id=1, source_target_pairs={{0,16},{16,0},{1,17},{17,1},{2,18},{18,2},{3,19},{19,3},{4,20},{20... | collective-permute-start | bytes 688136 | tf_op jit(solution)/shard_map/ppermute | solution.py:24
  114.6 7.0 %collective-permute-start.16 = (bf16[64,896]{1,0:T(8,128)(2,1)S(1)}, bf16[64,896]{1,0:T(8,128)(2,1)S(1)}, u32[]{:S(2)}, u32[]{:S(2)}) collective-permute-start(bf16[64,896]{1,0:T(8,128)(2,1)S(1)} %slice.14), channel_id=1, source_target_pairs={{0,4},{4,8},{8,12},{12,16},{16,20},{20,24},{24,28},{1,5},{5,9},{9,... | collective-permute-start | bytes 344072 | tf_op jit(solution)/shard_map/ppermute | solution.py:511
  122.4 18.2 %collective-permute-start.17 = (bf16[320,896]{1,0:T(8,128)(2,1)}, bf16[320,896]{1,0:T(8,128)(2,1)S(1)}, u32[]{:S(2)}, u32[]{:S(2)}) collective-permute-start(bf16[320,896]{1,0:T(8,128)(2,1)} %pad_maximum_fusion.2), channel_id=1, source_target_pairs={{0,2},{2,0},{1,3},{3,1},{4,6},{6,4},{5,7},{7,5},{8,10},{10,8},{9,1... | collective-permute-start | bytes 1720328 | tf_op jit(solution)/shard_map/ppermute | solution.py:19
  126.1 22.5 %collective-permute-start.18 = (bf16[960,512]{1,0:T(8,128)(2,1)}, bf16[960,512]{1,0:T(8,128)(2,1)}, u32[]{:S(2)}, u32[]{:S(2)}) collective-permute-start(bf16[960,512]{1,0:T(8,128)(2,1)} %constant_dynamic-update-slice_fusion.refs_5_), channel_id=1, source_target_pairs={{0,4},{4,0},{1,5},{5,1},{2,6},{6,2},{3,7},{7,3},{8,12},{12,8},{9,1... | collective-permute-start | bytes 2949128 | tf_op jit(solution)/shard_map/ppermute | solution.py:19
  133.2 54.4 %collective-permute-start.21 = (bf16[320,896]{1,0:T(8,128)(2,1)}, bf16[320,896]{1,0:T(8,128)(2,1)}, u32[]{:S(2)}, u32[]{:S(2)}) collective-permute-start(bf16[320,896]{1,0:T(8,128)(2,1)} %pad_maximum_fusion.2), channel_id=1, source_target_pairs={{0,10},{2,8},{8,2},{10,0},{1,11},{3,9},{9,3},{11,1},{4,14},{6,12},... | collective-permute-start | bytes 1720328 | tf_op jit(solution)/shard_map/ppermute | solution.py:518
  135.4 52.1 %collective-permute-start.20 = (bf16[320,896]{1,0:T(8,128)(2,1)}, bf16[320,896]{1,0:T(8,128)(2,1)}, u32[]{:S(2)}, u32[]{:S(2)}) collective-permute-start(bf16[320,896]{1,0:T(8,128)(2,1)} %pad_maximum_fusion.2), channel_id=1, source_target_pairs={{0,8},{8,0},{1,9},{9,1},{2,10},{10,2},{3,11},{11,3},{4,12},{12,4},... | collective-permute-start | bytes 1720328 | tf_op jit(solution)/shard_map/ppermute | solution.py:19
  138.4 49.2 %collective-permute-start.23 = (bf16[1024,512]{1,0:T(8,128)(2,1)}, bf16[1024,512]{1,0:T(8,128)(2,1)}, u32[]{:S(2)}, u32[]{:S(2)}) collective-permute-start(bf16[1024,512]{1,0:T(8,128)(2,1)} %pad_maximum_fusion.1), channel_id=1, source_target_pairs={{0,16},{16,0},{1,17},{17,1},{2,18},{18,2},{3,19},{19,3},{4,20},{20... | collective-permute-start | bytes 3145736 | tf_op jit(solution)/shard_map/ppermute | solution.py:24
  149.9 13.5 %collective-permute-start.19 = (bf16[640,896]{1,0:T(8,128)(2,1)S(1)}, bf16[640,896]{1,0:T(8,128)(2,1)}, u32[]{:S(2)}, u32[]{:S(2)}) collective-permute-start(bf16[640,896]{1,0:T(8,128)(2,1)S(1)} %pad_maximum_fusion.rows_ref), channel_id=1, source_target_pairs={{0,1},{1,0},{2,3},{3,2},{4,5},{5,4},{6,7},{7,6},{8,9},{9,8},{10,11... | collective-permute-start | bytes 3440648 | tf_op jit(solution)/shard_map/ppermute | solution.py:19
  188.7 25.7 %collective-permute-start.24 = (bf16[1024,512]{1,0:T(8,128)(2,1)}, bf16[1024,512]{1,0:T(8,128)(2,1)}, u32[]{:S(2)}, u32[]{:S(2)}) collective-permute-start(bf16[1024,512]{1,0:T(8,128)(2,1)} %collective-permute-done.23.refs_0_), channel_id=1, source_target_pairs={{0,4},{4,0},{1,5},{5,1},{2,6},{6,2},{3,7},{7,3},{8,12},{12,8},{9,1... | collective-permute-start | bytes 3145736 | tf_op jit(solution)/shard_map/ppermute | solution.py:19
  222.4 6.8 %collective-permute-start.25 = (bf16[2,512,1024]{2,1,0:T(8,128)(2,1)}, bf16[2,512,1024]{2,1,0:T(8,128)(2,1)}, u32[]{:S(2)}, u32[]{:S(2)}) collective-permute-start(bf16[2,512,1024]{2,1,0:T(8,128)(2,1)} %shard_map.127), channel_id=1, source_target_pairs={{0,1},{1,0},{2,3},{3,2},{4,5},{5,4},{6,7},{7,6},{8,9},{9,8},{10,11... | collective-permute-start | bytes 6291464 | tf_op jit(solution)/shard_map/ppermute | solution.py:19
  234.7 14.5 %collective-permute-start.26 = (bf16[256,1024]{1,0:T(8,128)(2,1)}, bf16[256,1024]{1,0:T(8,128)(2,1)S(1)}, u32[]{:S(2)}, u32[]{:S(2)}) collective-permute-start(bf16[256,1024]{1,0:T(8,128)(2,1)} %get-tuple-element.111), channel_id=1, source_target_pairs={{0,8},{8,0},{1,9},{9,1},{2,10},{10,2},{3,11},{11,3},{4,12},{12,4},... | collective-permute-start | bytes 1572872 | tf_op jit(solution)/shard_map/ppermute | solution.py:19
  234.7 14.6 %collective-permute-start.27 = (bf16[256,1024]{1,0:T(8,128)(2,1)}, bf16[256,1024]{1,0:T(8,128)(2,1)}, u32[]{:S(2)}, u32[]{:S(2)}) collective-permute-start(bf16[256,1024]{1,0:T(8,128)(2,1)} %get-tuple-element.112), channel_id=1, source_target_pairs={{0,2},{2,0},{1,3},{3,1},{4,6},{6,4},{5,7},{7,5},{8,10},{10,8},{9,1... | collective-permute-start | bytes 1572872 | tf_op jit(solution)/shard_map/ppermute | solution.py:19
  249.3 15.9 %collective-permute-start.28 = (bf16[256,1024]{1,0:T(8,128)(2,1)}, bf16[256,1024]{1,0:T(8,128)(2,1)}, u32[]{:S(2)}, u32[]{:S(2)}) collective-permute-start(bf16[256,1024]{1,0:T(8,128)(2,1)} %get-tuple-element.113), channel_id=1, source_target_pairs={{0,10},{2,8},{8,2},{10,0},{1,11},{3,9},{9,3},{11,1},{4,14},{6,12},... | collective-permute-start | bytes 1572872 | tf_op jit(solution)/shard_map/ppermute | solution.py:421
  259.2 16.7 %collective-permute-start.30 = (bf16[256,1024]{1,0:T(8,128)(2,1)}, bf16[256,1024]{1,0:T(8,128)(2,1)S(1)}, u32[]{:S(2)}, u32[]{:S(2)}) collective-permute-start(bf16[256,1024]{1,0:T(8,128)(2,1)} %get-tuple-element.119), channel_id=1, source_target_pairs={{0,8},{8,0},{1,9},{9,1},{2,10},{10,2},{3,11},{11,3},{4,12},{12,4},... | collective-permute-start | bytes 1572872 | tf_op jit(solution)/shard_map/ppermute | solution.py:19
  261.0 15.4 %collective-permute-start.31 = (bf16[256,1024]{1,0:T(8,128)(2,1)}, bf16[256,1024]{1,0:T(8,128)(2,1)S(1)}, u32[]{:S(2)}, u32[]{:S(2)}) collective-permute-start(bf16[256,1024]{1,0:T(8,128)(2,1)} %get-tuple-element.120), channel_id=1, source_target_pairs={{0,2},{2,0},{1,3},{3,1},{4,6},{6,4},{5,7},{7,5},{8,10},{10,8},{9,1... | collective-permute-start | bytes 1572872 | tf_op jit(solution)/shard_map/ppermute | solution.py:19
  262.0 25.3 %collective-permute-start.32 = (bf16[256,1024]{1,0:T(8,128)(2,1)}, bf16[256,1024]{1,0:T(8,128)(2,1)S(1)}, u32[]{:S(2)}, u32[]{:S(2)}) collective-permute-start(bf16[256,1024]{1,0:T(8,128)(2,1)} %get-tuple-element.121), channel_id=1, source_target_pairs={{0,10},{2,8},{8,2},{10,0},{1,11},{3,9},{9,3},{11,1},{4,14},{6,12},... | collective-permute-start | bytes 1572872 | tf_op jit(solution)/shard_map/ppermute | solution.py:421
  (18 other events, 180.5 us)
Sparse Core Ops, SparseCore 0:
  12.0 37.1 all-gather.4
  133.3 41.9 all-gather.6

commit v4 on v3

--- a/solution.py
+++ b/solution.py
@@ -323,43 +323,62 @@
     attn_ref[...] = stage[1 : toks + 1, :].astype(BF16)
 
 
-def backward_kernel(
-    span, head_dim, turn, at_ref, prob_ref, d_ref, k_ref, v_ref, k2_ref, v2_ref, dq_ref, stage, d_prob
-):
-    groups, inner = k_ref.shape[1], k_ref.shape[3]
-    heads = inner // head_dim
-    scale = head_dim ** (-0.5)
-    toks = dq_ref.shape[0]
-    for g in range(groups):
-        rows = pl.ds(g * span, span)
-        for h in range(heads):
-            cols = pl.ds(h * head_dim, head_dim)
-            d_prob[h, rows, :] = dot_t(d_ref[0, rows, cols], span_rows((v_ref, v2_ref), g, cols))
-    for g in range(groups):
-        rows = pl.ds(g * span, span)
-        for h in range(heads):
-            cols = pl.ds(h * head_dim, head_dim)
-            prob, slope = prob_ref[h, rows, :], d_prob[h, rows, :]
-            delta = jnp.sum(prob * slope, axis=-1, keepdims=True)
-            d_score = (prob * (slope - delta) * scale).astype(BF16)
-            stage[rows, cols] = dot(d_score, span_rows((k_ref, k2_ref), g, cols))
-    dq_ref[...] = stage[1 : toks + 1, :].astype(BF16)
-
-
-def over_shard(kernel, turn, at, padded, kv, span, head_dim, prob):
+def backward_kernel(span, head_dim, at_ref, *refs):
+    (d_ref, w_ref, w2_ref), shards, (dq_ref, dq2_ref, sent_ref, stage, d_prob) = refs[:3], refs[3:-5], refs[-5:]
+    for turn, out_ref in enumerate((dq_ref, dq2_ref)):
+        prob_ref, k_ref, v_ref, k2_ref, v2_ref = shards[5 * turn : 5 * turn + 5]
+        groups, inner = k_ref.shape[1], k_ref.shape[3]
+        heads = inner // head_dim
+        scale = head_dim ** (-0.5)
+        for g in range(groups):
+            rows = pl.ds(g * span, span)
+            for h in range(heads):
+                cols = pl.ds(h * head_dim, head_dim)
+                d_prob[turn, h, rows, :] = dot_t(d_ref[turn, rows, cols], span_rows((v_ref, v2_ref), g, cols))
+        for g in range(groups):
+            rows = pl.ds(g * span, span)
+            for h in range(heads):
+                cols = pl.ds(h * head_dim, head_dim)
+                prob, slope = prob_ref[h, rows, :], d_prob[turn, h, rows, :]
+                delta = jnp.sum(prob * slope, axis=-1, keepdims=True)
+                d_score = (prob * (slope - delta) * scale).astype(BF16)
+                stage[turn, rows, cols] = dot(d_score, span_rows((k_ref, k2_ref), g, cols))
+        out_ref[...] = stage[turn, 1 : out_ref.shape[0] + 1, :].astype(BF16)
+    rows = jnp.concatenate([dq_ref[...], dq2_ref[...]], axis=0)
+    sent_ref[0] = dot_t(rows, w_ref[...]).astype(BF16)
+    sent_ref[1] = dot_t(rows, w2_ref[...]).astype(BF16)
+
+
+def backward(probs, d_attn, kvs, w, span, head_dim):
+    y, c = lax.axis_index("y"), lax.axis_index("c")
+    wm = w.shape[0] // (2 * lax.axis_size("y"))
+    at = jnp.stack([(1 - y) * 2 + (1 - c), y * 2 + (1 - c)])
+    shards, rows, inner = d_attn.shape
+    toks = rows - span
+    operands = [(d_attn, d_attn.shape, whole_block(3))]
+    operands += [(w, (wm, inner), lambda i, at, j=j: (at[j], 0)) for j in range(2)]
+    for prob, kv in zip(probs, kvs):
+        operands += [(a, a.shape, whole_block(a.ndim)) for a in (prob, *kv)]
+    dims = [(toks, inner), (toks, inner), (2, 2 * toks, wm)]
+    return call(
+        functools.partial(backward_kernel, span, head_dim),
+        (1,),
+        at,
+        operands,
+        [(shape(d, BF16), d, whole_block(len(d))) for d in dims],
+        [pltpu.VMEM(d_attn.shape, F32), pltpu.VMEM((shards,) + probs[0].shape, F32)],
+    )
+
+
+def attend(turn, at, padded, kv, span, head_dim):
     _, rows, inner = padded.shape
     toks, heads = rows - span, inner // head_dim
     probs = shape((heads, rows, 2 * kv[0].shape[0] * kv[0].shape[2]), F32)
     operands = [(padded, (1, rows, inner), lambda i, at: (turn, 0, 0))]
     operands += [(a, a.shape, whole_block(4)) for a in kv]
-    outs = [(shape((toks, inner), BF16), (toks, inner), whole_block(2))]
+    outs = [(shape((toks, inner), BF16), (toks, inner), whole_block(2)), (probs, probs.shape, whole_block(3))]
     scratch = [pltpu.VMEM((rows, inner), F32)]
-    if prob is None:
-        outs.append((probs, probs.shape, whole_block(3)))
-    else:
-        operands.insert(0, (prob, prob.shape, whole_block(3)))
-        scratch.append(pltpu.VMEM(probs.shape, F32))
-    return call(functools.partial(kernel, span, head_dim, turn), (1,), at, operands, outs, scratch)
+    return call(functools.partial(attend_kernel, span, head_dim, turn), (1,), at, operands, outs, scratch)
 
 
 def sent_kernel(at_ref, own_ref, other_ref, w_ref, out_ref):
@@ -581,20 +600,17 @@
         far = keyval(at, tie(rows2, *near), wkv)
         return [a.reshape(kv_shape) for a in (*near, *far)]
 
-    def attend(turn, kv, query):
-        return over_shard(attend_kernel, turn, at, query, kv, span, head_dim, None)
-
     own_rows = jnp.concatenate(own_rows, axis=0)
     own_rows2 = flip(own_rows, "c")
     kv = keys_values(own_rows, own_rows2)
     query = project(every, states, 0, tie(wq, wo, *kv), hidden.shape[1], span, True)
-    attn, prob = attend(0, kv, query)
+    attn, prob = attend(0, at, query, kv, span, head_dim)
     other_rows = jnp.concatenate(lax.optimization_barrier((*other_rows, attn))[:-1], axis=0)
     other_rows2 = flip(other_rows, "c")
-    hop_out = tie(hop_out, attn)
+    hop_out = tie(hop_out, query)
     hop_out_x = flip(hop_out, "x")
     kv2 = keys_values(other_rows, other_rows2)
-    attn2, prob2 = attend(1, kv2, query)
+    attn2, prob2 = attend(1, at, query, kv2, span, head_dim)
     some = project(at_of(out_pieces), states, 1, tie(wo, attn2), rows_here, span, False)
 
     late = []
@@ -616,11 +632,7 @@
     d_attn = project(at_of(late), states, 1, wo, rows_here, span, True, some)
     cca_out, moved, arrived = sum_heads((attn[0], tie(attn[1], d_attn)), wo, out_sent)
     d_attn = tie(d_attn, *moved)
-    d_query = [
-        over_shard(backward_kernel, turn, at, d_attn, kv_here, span, head_dim, prob_here)[0]
-        for turn, kv_here, prob_here in ((0, kv, prob), (1, kv2, prob2))
-    ]
-    grad_sent = core_sums(d_query, wq)
+    *d_query, grad_sent = backward((prob, prob2), d_attn, (kv, kv2), wq, span, head_dim)
     if arrived:
         grad_sent = tie(grad_sent, *arrived[1:])
     hidden_grad, _, _ = sum_heads(d_query, wq, grad_sent)

time: 297 us -> 296 us (level)
  Pallas kernels: 107 us -> 102 us
    ppermute x24, waiting for transfers between devices: 46.5 us -> 61.6 us  [flip(): return lax.ppermute(shard, axis, [(0, 1), (1, 0)])]
    ppermute x2, waiting for transfers between devices: 13.4 us -> 1.21 us  [sum_heads(): lax.ppermute(to_both, ('zl', 'y'), [(i, 3 - i) for i in range(4)])]
    pallas_call x17 -> x15, Pallas kernels: 90.4 us -> 85.9 us  [call(): pl.pallas_call(kernel, grid_spec=pltpu.PrefetchScalarGridSpec(num_scalar_...]
    unnamed x33 -> x37, local copies, waits for them, and re-layouts: 4.43 us -> 7.21 us
  transfers between devices with their start and end apart: 35 -> 35, of which waited for: 20 -> 19; matrix products, arithmetic and copies ran while one was open for 14% -> 14% of each run, Pallas kernels for 30% -> 29%
where the time goes in v4:
time: 296 us; the launch traced here: 294 us
  Pallas kernels  102 us (34%)
  waiting for transfers between devices  87.9 us (30%)
  starting transfers between devices  40.9 us (14%)
  local copies, waits for them, and re-layouts  35.8 us (12%)
  between operations  14.3 us (5%)
  other arithmetic  13.2 us (4%)
    pallas_call x15, Pallas kernels, call(): pl.pallas_call(kernel, grid_spec=pltpu.PrefetchScalarGridSpec(num_scalar_...  85.9 us
    ppermute x24, waiting for transfers between devices, flip(): return lax.ppermute(shard, axis, [(0, 1), (1, 0)])  61.6 us
    ppermute x24, starting transfers between devices, flip(): return lax.ppermute(shard, axis, [(0, 1), (1, 0)])  22 us
    gather x1, local copies, waits for them, and re-layouts, per_device(): embed_table.at[clipped].get(mode='promise_in_bounds')  18.9 us
    ppermute x5, waiting for transfers between devices, onward(): lax.ppermute(shard, axis, [(i, (i + 1) % count) for i in range(count)])  17.9 us
    pallas_call x4, Pallas kernels, place(): pl.pallas_call(functools.partial(place_kernel, jobs, len(sources), int(th...  16.3 us
    ppermute x5, starting transfers between devices, onward(): lax.ppermute(shard, axis, [(i, (i + 1) % count) for i in range(count)])  10.1 us
    unnamed x37, local copies, waits for them, and re-layouts  7.21 us
  transfers between devices with their start and end apart: 35, of which 19 were waited for; matrix products, arithmetic and copies ran while one was open for 14% of the time, Pallas kernels for 29%

profile of v4, /device:TPU:0, one launch (start us, length us, event | category | flops | bytes accessed | tf_op | source)
XLA Modules:
  0.0 294.4 jit_solution(17376630538723301840)
XLA Ops:
  7.2 4.6 %shard_map.113 = (bf16[736,512]{1,0:T(8,128)(2,1)}, bf16[512,512]{1,0:T(8,128)(2,1)}, bf16[1248,512]{1,0:T(8,128)(2,1)}, bf16[512,512]{1,0:T(8,128)(2,1)}, bf16[...) custom-call(s32[1]{0:T(128)} %bitcast.6.at_ref, bf16[512,8,128]{2,1,0:T(8,128)(2,1)} %q_ref.1, ...), custom_call_target="tpu_custom_call" | custom-call | flops 20000000000 | bytes 1 | tf_op jit(solution)/shard_map/pallas_call | solution.py:45
  19.8 18.9 %gather_fusion = bf16[1024,896]{1,0:T(8,128)(2,1)S(1)} fusion(bf16[16000,896]{1,0:T(8,128)(2,1)} %param.14, s32[1024]{0:T(1024)S(1)} %fusion), kind=kCustom, calls=%fused_computation | custom fusion | bytes 3674112 | tf_op jit(solution)/shard_map/gather | solution.py:495
  38.8 4.6 %collective-permute-done.refs_4_ = bf16[512,512]{1,0:T(8,128)(2,1)} collective-permute-done((bf16[512,512]{1,0:T(8,128)(2,1)}, bf16[512,512]{1,0:T(8,128)(2,1)}, u32[]{:S(2)}, u32[]{:S(2)}) %collective-permute-start) | collective-permute-done | bytes 524320 | tf_op jit(solution)/shard_map/ppermute | solution.py:24
  44.5 3.4 %collective-permute-done.4.refs_1_.refs_2_ = bf16[1248,512]{1,0:T(8,128)(2,1)} collective-permute-done((bf16[1248,512]{1,0:T(8,128)(2,1)}, bf16[1248,512]{1,0:T(8,128)(2,1)}, u32[]{:S(2)}, u32[]{:S(2)}) %collective-permute-start.4) | collective-permute-done | bytes 1277984 | tf_op jit(solution)/shard_map/ppermute | solution.py:19
  57.1 12.8 %collective-permute-done.6 = bf16[512,896]{1,0:T(8,128)(2,1)S(1)} collective-permute-done((bf16[512,896]{1,0:T(8,128)(2,1)S(1)}, bf16[512,896]{1,0:T(8,128)(2,1)S(1)}, u32[]{:S(2)}, u32[]{:S(2)}) %collective-permute-start.6) | collective-permute-done | bytes 917536 | tf_op jit(solution)/shard_map/ppermute | solution.py:19
  71.1 7.0 %collective-permute-done.9 = bf16[512,512]{1,0:T(8,128)(2,1)S(1)} collective-permute-done((bf16[512,512]{1,0:T(8,128)(2,1)}, bf16[512,512]{1,0:T(8,128)(2,1)S(1)}, u32[]{:S(2)}, u32[]{:S(2)}) %collective-permute-start.9) | collective-permute-done | bytes 524320 | tf_op jit(solution)/shard_map/ppermute | solution.py:24
  83.4 9.3 %shard_map.114 = (bf16[512,896]{1,0:T(8,128)(2,1)}, f32[256,896]{1,0:T(8,128)}) custom-call(s32[1]{0:T(128)} %bitcast.9.at_ref, bf16[512,896]{1,0:T(8,128)(2,1)} %add.215.emb_ref, bf16[896,896]{1,0:T(8,128)(2,1)} %up_ref.1, bf16[896,896]{1,0:T(8,128)(2,1)} %down_ref.1, bf16[896,896]{1,0:T(8,128)(2,1)} %collective-permute-done.2.up2_ref, ...), custom_call_target="tpu_custom_call" | custom-call | flops 20000000000 | bytes 1 | tf_op jit(solution)/shard_map/pallas_call | solution.py:45
  99.7 5.6 %collective-permute-done.13 = bf16[256,896]{1,0:T(8,128)(2,1)S(1)} collective-permute-done((bf16[256,896]{1,0:T(8,128)(2,1)S(1)}, bf16[256,896]{1,0:T(8,128)(2,1)S(1)}, u32[]{:S(2)}, u32[]{:S(2)}) %collective-permute-start.13) | collective-permute-done | bytes 458784 | tf_op jit(solution)/shard_map/ppermute | solution.py:19
  107.3 6.2 %collective-permute-done.15 = bf16[224,512]{1,0:T(8,128)(2,1)} collective-permute-done((bf16[224,512]{1,0:T(8,128)(2,1)S(1)}, bf16[224,512]{1,0:T(8,128)(2,1)}, u32[]{:S(2)}, u32[]{:S(2)}) %collective-permute-start.15) | collective-permute-done | bytes 229408 | tf_op jit(solution)/shard_map/ppermute | solution.py:24
  114.6 3.6 %collective-permute-start.16 = (bf16[64,896]{1,0:T(8,128)(2,1)S(1)}, bf16[64,896]{1,0:T(8,128)(2,1)S(1)}, u32[]{:S(2)}, u32[]{:S(2)}) collective-permute-start(bf16[64,896]{1,0:T(8,128)(2,1)S(1)} %slice.14), channel_id=1, source_target_pairs={{0,4},{4,8},{8,12},{12,16},{16,20},{20,24},{24,28},{1,5},{5,9},{9,... | collective-permute-start | bytes 344072 | tf_op jit(solution)/shard_map/ppermute | solution.py:530
  128.9 4.3 %shard_map.116.w_ref.refs_2_ = bf16[4096,512]{1,0:T(8,128)(2,1)} custom-call(s32[4]{0:T(128)} %pad_add_fusion.3.at_ref, bf16[512,512]{1,0:T(8,128)(2,1)} %get-tuple-element.107.refs_0_, bf16[1248,512]{1,0:T(8,128)(2,1)} %collective-permute-done.4.refs_1_.refs_2_, bf16[512,512]{1,0:T(8,128)(2,1)} %collective-permute-done.10.refs_2_, ...), custom_call_target="tpu_custom_call" | custom-call | flops 20000000000 | bytes 1 | tf_op jit(solution)/shard_map/pallas_call | solution.py:164
  141.4 7.3 %collective-permute-done.18.refs_7_.refs_6_ = bf16[960,512]{1,0:T(8,128)(2,1)} collective-permute-done((bf16[960,512]{1,0:T(8,128)(2,1)}, bf16[960,512]{1,0:T(8,128)(2,1)}, u32[]{:S(2)}, u32[]{:S(2)}) %collective-permute-start.18) | collective-permute-done | bytes 983072 | tf_op jit(solution)/shard_map/ppermute | solution.py:19
  149.9 3.6 %shard_map.117.w_ref = bf16[2,896,512]{2,1,0:T(8,128)(2,1)} custom-call(s32[16]{0:T(128)} %stack.61.at_ref, bf16[224,512]{1,0:T(8,128)(2,1)} %get-tuple-element.91.refs_0_.refs_1_, bf16[224,512]{1,0:T(8,128)(2,1)} %get-tuple-element.91.refs_0_.refs_1_, bf16[1248,512]{1,0:T(8,128)(2,1)} %collective-permute-done.4.refs_1_.refs_2_, bf16[736,512]{1,0:T(8,128)(2,1)} %copy-done.5, ...), custom_call_target="tpu_custom_call" | custom-call | flops 20000000000 | bytes 1 | tf_op jit(solution)/shard_map/pallas_call | solution.py:164
  153.5 4.9 %shard_map.118 = (bf16[640,512]{1,0:T(8,128)(2,1)}, bf16[640,512]{1,0:T(8,128)(2,1)}) custom-call(s32[34]{0:T(128)} %concatenate.31.at_ref, bf16[640,896]{1,0:T(8,128)(2,1)} %copy-done, bf16[2,896,512]{2,1,0:T(8,128)(2,1)} %shard_map.117.w_ref), custom_call_target="tpu_custom_call" | custom-call | flops 20000000000 | bytes 1 | tf_op jit(solution)/shard_map/pallas_call | solution.py:45
  158.4 4.9 %shard_map.115.w_ref.refs_1_.refs_2_ = bf16[4096,512]{1,0:T(8,128)(2,1)} custom-call(s32[8]{0:T(128)} %stack.59.at_ref, bf16[512,512]{1,0:T(8,128)(2,1)} %get-tuple-element.89.refs_0_, bf16[1248,512]{1,0:T(8,128)(2,1)} %collective-permute-done.4.refs_1_.refs_2_, bf16[736,512]{1,0:T(8,128)(2,1)} %copy-done.5, ...), custom_call_target="tpu_custom_call" | custom-call | flops 20000000000 | bytes 1 | tf_op jit(solution)/shard_map/pallas_call | solution.py:164
  163.4 4.9 %shard_map.119 = (bf16[640,512]{1,0:T(8,128)(2,1)}, bf16[640,512]{1,0:T(8,128)(2,1)}) custom-call(s32[34]{0:T(128)} %concatenate.31.at_ref, bf16[640,896]{1,0:T(8,128)(2,1)} %collective-permute-done.19.rows_ref, bf16[2,896,512]{2,1,0:T(8,128)(2,1)} %shard_map.117.w_ref), custom_call_target="tpu_custom_call" | custom-call | flops 20000000000 | bytes 1 | tf_op jit(solution)/shard_map/pallas_call | solution.py:45
  168.2 7.1 %all-gather.7.cloned.1.call-done = bf16[8,256,1024]{2,1,0:T(8,128)(2,1)} async-done(((bf16[2,256,1024]{2,1,0:T(8,128)(2,1)}), bf16[8,256,1024]{2,1,0:T(8,128)(2,1)}) %all-gather.7.cloned.1.call-update) | async-done | bytes 4194320 | tf_op jit(solution)/shard_map/all_gather | solution.py:486
  175.9 7.3 %shard_map.120.q_ref = bf16[2,320,512]{2,1,0:T(8,128)(2,1)} custom-call(s32[4]{0:T(128)} %iota.13.at_ref, bf16[4,2,256,1024]{3,2,1,0:T(8,128)(2,1)} %bitcast.32, bf16[4,2,256,1024]{3,2,1,0:T(8,128)(2,1)} %bitcast.35, bf16[4096,512]{1,0:T(8,128)(2,1)} %shard_map.115.w_ref.refs_1_.refs_2_), custom_call_target="tpu_custom_call" | custom-call | flops 20000000000 | bytes 1 | tf_op jit(solution)/shard_map/pallas_call | solution.py:45
  183.2 4.4 %shard_map.121 = (bf16[256,512]{1,0:T(8,128)(2,1)}, f32[4,320,256]{2,1,0:T(8,128)}) custom-call(s32[34]{0:T(128)} %concatenate.31.at_ref, bf16[2,320,512]{2,1,0:T(8,128)(2,1)} %shard_map.120.q_ref, bf16[2,5,64,512]{3,2,1,0:T(8,128)(2,1)} %bitcast.38, bf16[2,5,64,512]{3,2,1,0:T(8,128)(2,1)} %bitcast.40, bf16[2,5,64,512]{3,2,1,0:T(8,128)(2,1)} %bitcast.42, ...), custom_call_target="tpu_custom_call" | custom-call | flops 20000000000 | bytes 1 | tf_op jit(solution)/shard_map/pallas_call | solution.py:45
  192.3 4.9 %shard_map.122 = (bf16[640,512]{1,0:T(8,128)(2,1)}, bf16[640,512]{1,0:T(8,128)(2,1)}) custom-call(s32[34]{0:T(128)} %concatenate.31.at_ref, bf16[640,896]{1,0:T(8,128)(2,1)} %copy-done.11, bf16[2,896,512]{2,1,0:T(8,128)(2,1)} %shard_map.117.w_ref), custom_call_target="tpu_custom_call" | custom-call | flops 20000000000 | bytes 1 | tf_op jit(solution)/shard_map/pallas_call | solution.py:45
  197.2 4.9 %shard_map.123 = (bf16[640,512]{1,0:T(8,128)(2,1)}, bf16[640,512]{1,0:T(8,128)(2,1)}) custom-call(s32[34]{0:T(128)} %concatenate.31.at_ref, bf16[640,896]{1,0:T(8,128)(2,1)} %collective-permute-done.22.rows_ref, bf16[2,896,512]{2,1,0:T(8,128)(2,1)} %shard_map.117.w_ref), custom_call_target="tpu_custom_call" | custom-call | flops 20000000000 | bytes 1 | tf_op jit(solution)/shard_map/pallas_call | solution.py:45
  202.0 4.4 %shard_map.124 = (bf16[256,512]{1,0:T(8,128)(2,1)}, f32[4,320,256]{2,1,0:T(8,128)}) custom-call(s32[34]{0:T(128)} %concatenate.31.at_ref, bf16[2,320,512]{2,1,0:T(8,128)(2,1)} %shard_map.120.q_ref, bf16[2,5,64,512]{3,2,1,0:T(8,128)(2,1)} %bitcast.46, bf16[2,5,64,512]{3,2,1,0:T(8,128)(2,1)} %bitcast.48, bf16[2,5,64,512]{3,2,1,0:T(8,128)(2,1)} %bitcast.50, ...), custom_call_target="tpu_custom_call" | custom-call | flops 20000000000 | bytes 1 | tf_op jit(solution)/shard_map/pallas_call | solution.py:45
  206.4 5.9 %shard_map.125.rest_0_ = f32[512,512]{1,0:T(8,128)} custom-call(s32[4]{0:T(128)} %pad_add_fusion.3.at_ref, bf16[4,2,256,1024]{3,2,1,0:T(8,128)(2,1)} %bitcast.33, bf16[4,2,256,1024]{3,2,1,0:T(8,128)(2,1)} %bitcast.36, bf16[4096,512]{1,0:T(8,128)(2,1)} %shard_map.116.w_ref.refs_2_), custom_call_target="tpu_custom_call" | custom-call | flops 20000000000 | bytes 1 | tf_op jit(solution)/shard_map/pallas_call | solution.py:45
  213.2 3.5 %shard_map.126.w_ref = bf16[4096,512]{1,0:T(8,128)(2,1)} custom-call(s32[4]{0:T(128)} %pad_add_fusion.4.at_ref, bf16[1024,512]{1,0:T(8,128)(2,1)} %collective-permute-done.23.refs_0_, bf16[1024,512]{1,0:T(8,128)(2,1)} %collective-permute-done.24.refs_1_, bf16[4096,512]{1,0:T(8,128)(2,1)} %shard_map.116.w_ref.refs_2_), custom_call_target="tpu_custom_call", output_to_operand_aliasing={{}: (3, {})} | custom-call | flops 20000000000 | bytes 1 | tf_op jit(solution)/shard_map/pallas_call | solution.py:164
  216.7 4.5 %shard_map.127 = bf16[2,512,1024]{2,1,0:T(8,128)(2,1)} custom-call(s32[2]{0:T(128)} %pad_add_fusion.5.at_ref, bf16[256,512]{1,0:T(8,128)(2,1)} %get-tuple-element.98.own_ref.own_rows_ref, bf16[256,512]{1,0:T(8,128)(2,1)} %get-tuple-element.112.other_ref.other_rows_ref, bf16[4096,512]{1,0:T(8,128)(2,1)} %shard_map.126.w_ref), custom_call_target="tpu_custom_call" | custom-call | flops 20000000000 | bytes 1 | tf_op jit(solution)/shard_map/pallas_call | solution.py:45
  221.9 6.2 %shard_map.128.refs_0_ = bf16[2,320,512]{2,1,0:T(8,128)(2,1)} custom-call(s32[4]{0:T(128)} %pad_add_fusion.4.at_ref, bf16[4,2,256,1024]{3,2,1,0:T(8,128)(2,1)} %bitcast.34, bf16[4,2,256,1024]{3,2,1,0:T(8,128)(2,1)} %bitcast.37, bf16[4096,512]{1,0:T(8,128)(2,1)} %shard_map.126.w_ref, f32[512,512]{1,0:T(8,128)} %shard_map.125.rest_0_), custom_call_target="tpu_custom_call" | custom-call | flops 20000000000 | bytes 1 | tf_op jit(solution)/shard_map/pallas_call | solution.py:45
  228.1 5.4 %shard_map.129 = (bf16[256,1024]{1,0:T(8,128)(2,1)}, bf16[256,1024]{1,0:T(8,128)(2,1)}, bf16[256,1024]{1,0:T(8,128)(2,1)}, f32[256,1024]{1,0:T(8,128)}) custom-call(s32[2]{0:T(128)} %pad_add_fusion.2.at_ref, bf16[256,512]{1,0:T(8,128)(2,1)} %get-tuple-element.98.own_ref.own_rows_ref, bf16[256,512]{1,0:T(8,128)(2,1)} %get-tuple-element.112.other_ref.other_rows_ref, ...), custom_call_target="tpu_custom_call" | custom-call | flops 20000000000 | bytes 1 | tf_op jit(solution)/shard_map/pallas_call | solution.py:45
  233.8 8.7 %shard_map.130 = (bf16[256,512]{1,0:T(8,128)(2,1)}, bf16[256,512]{1,0:T(8,128)(2,1)}, bf16[2,512,1024]{2,1,0:T(8,128)(2,1)}) custom-call(s32[2]{0:T(128)} %pad_add_fusion.5.at_ref, bf16[2,320,512]{2,1,0:T(8,128)(2,1)} %shard_map.128.refs_0_, bf16[4096,512]{1,0:T(8,128)(2,1)} %shard_map.115.w_ref.refs_1_.refs_2_, ...), custom_call_target="tpu_custom_call" | custom-call | flops 20000000000 | bytes 1 | tf_op jit(solution)/shard_map/pallas_call | solution.py:45
  242.5 5.5 %collective-permute-done.26 = bf16[256,1024]{1,0:T(8,128)(2,1)S(1)} collective-permute-done((bf16[256,1024]{1,0:T(8,128)(2,1)}, bf16[256,1024]{1,0:T(8,128)(2,1)S(1)}, u32[]{:S(2)}, u32[]{:S(2)}) %collective-permute-start.26) | collective-permute-done | bytes 524320 | tf_op jit(solution)/shard_map/ppermute | solution.py:19
  253.9 5.5 %shard_map.131 = (bf16[256,1024]{1,0:T(8,128)(2,1)}, bf16[256,1024]{1,0:T(8,128)(2,1)}, bf16[256,1024]{1,0:T(8,128)(2,1)}, f32[256,1024]{1,0:T(8,128)}) custom-call(s32[2]{0:T(128)} %pad_add_fusion.2.at_ref, bf16[256,512]{1,0:T(8,128)(2,1)} %get-tuple-element.120.own_rows_ref, bf16[256,512]{1,0:T(8,128)(2,1)} %get-tuple-element.121.other_rows_ref, ...), custom_call_target="tpu_custom_call" | custom-call | flops 20000000000 | bytes 1 | tf_op jit(solution)/shard_map/pallas_call | solution.py:45
  266.4 8.1 %collective-permute-done.30 = bf16[256,1024]{1,0:T(8,128)(2,1)S(1)} collective-permute-done((bf16[256,1024]{1,0:T(8,128)(2,1)}, bf16[256,1024]{1,0:T(8,128)(2,1)S(1)}, u32[]{:S(2)}, u32[]{:S(2)}) %collective-permute-start.30) | collective-permute-done | bytes 524320 | tf_op jit(solution)/shard_map/ppermute | solution.py:19
  274.5 11.9 %collective-permute-done.31 = bf16[256,1024]{1,0:T(8,128)(2,1)S(1)} collective-permute-done((bf16[256,1024]{1,0:T(8,128)(2,1)}, bf16[256,1024]{1,0:T(8,128)(2,1)S(1)}, u32[]{:S(2)}, u32[]{:S(2)}) %collective-permute-start.31) | collective-permute-done | bytes 524320 | tf_op jit(solution)/shard_map/ppermute | solution.py:19
  (137 shorter events, 75.8 us)
Async XLA Ops:
  7.2 72.0 %all-gather.5.cloned.1.call-start = ((), (), s32[]{:S(2)}) async-start(), calls=%async_computation | async-start | bytes 5242880 | tf_op jit(solution)/shard_map/all_gather | solution.py:486
  11.8 163.5 %all-gather.7.cloned.1.call-start = ((), (), s32[]{:S(2)}) async-start(), calls=%async_computation.1 | async-start | bytes 5242880 | tf_op jit(solution)/shard_map/all_gather | solution.py:486
  11.9 32.1 %collective-permute-start.2 = (bf16[896,896]{1,0:T(8,128)(2,1)}, bf16[896,896]{1,0:T(8,128)(2,1)}, u32[]{:S(2)}, u32[]{:S(2)}) collective-permute-start(bf16[896,896]{1,0:T(8,128)(2,1)} %up_ref.1), channel_id=1, source_target_pairs={{0,1},{1,0},{2,3},{3,2},{4,5},{5,4},{6,7},{7,6},{8,9},{9,8},{10,11... | collective-permute-start | bytes 4816904 | tf_op jit(solution)/shard_map/ppermute | solution.py:19
  12.4 31.6 %collective-permute-start.3 = (bf16[896,896]{1,0:T(8,128)(2,1)}, bf16[896,896]{1,0:T(8,128)(2,1)}, u32[]{:S(2)}, u32[]{:S(2)}) collective-permute-start(bf16[896,896]{1,0:T(8,128)(2,1)} %down_ref.1), channel_id=1, source_target_pairs={{0,1},{1,0},{2,3},{3,2},{4,5},{5,4},{6,7},{7,6},{8,9},{9,8},{10,11... | collective-permute-start | bytes 4816904 | tf_op jit(solution)/shard_map/ppermute | solution.py:19
  12.5 31.5 %collective-permute-start.1 = (bf16[736,512]{1,0:T(8,128)(2,1)}, bf16[736,512]{1,0:T(8,128)(2,1)S(1)}, u32[]{:S(2)}, u32[]{:S(2)}) collective-permute-start(bf16[736,512]{1,0:T(8,128)(2,1)} %get-tuple-element.66), channel_id=1, source_target_pairs={{0,8},{8,0},{1,9},{9,1},{2,10},{10,2},{3,11},{11,3},{4,12},{12,4},... | collective-permute-start | bytes 2261000 | tf_op jit(solution)/shard_map/ppermute | solution.py:19
  15.5 27.9 %collective-permute-start = (bf16[512,512]{1,0:T(8,128)(2,1)}, bf16[512,512]{1,0:T(8,128)(2,1)}, u32[]{:S(2)}, u32[]{:S(2)}) collective-permute-start(bf16[512,512]{1,0:T(8,128)(2,1)} %get-tuple-element.89.refs_0_), channel_id=1, source_target_pairs={{0,16},{16,0},{1,17},{17,1},{2,18},{18,2},{3,19},{19,3},{4,20},{20... | collective-permute-start | bytes 1572872 | tf_op jit(solution)/shard_map/ppermute | solution.py:24
  18.1 29.8 %collective-permute-start.4 = (bf16[1248,512]{1,0:T(8,128)(2,1)}, bf16[1248,512]{1,0:T(8,128)(2,1)}, u32[]{:S(2)}, u32[]{:S(2)}) collective-permute-start(bf16[1248,512]{1,0:T(8,128)(2,1)} %get-tuple-element.70), channel_id=1, source_target_pairs={{0,4},{4,0},{1,5},{5,1},{2,6},{6,2},{3,7},{7,3},{8,12},{12,8},{9,1... | collective-permute-start | bytes 3833864 | tf_op jit(solution)/shard_map/ppermute | solution.py:19
  48.2 21.7 %collective-permute-start.6 = (bf16[512,896]{1,0:T(8,128)(2,1)S(1)}, bf16[512,896]{1,0:T(8,128)(2,1)S(1)}, u32[]{:S(2)}, u32[]{:S(2)}) collective-permute-start(bf16[512,896]{1,0:T(8,128)(2,1)S(1)} %add.214), channel_id=1, source_target_pairs={{0,2},{2,0},{1,3},{3,1},{4,6},{6,4},{5,7},{7,5},{8,10},{10,8},{9,1... | collective-permute-start | bytes 2752520 | tf_op jit(solution)/shard_map/ppermute | solution.py:19
  49.7 29.4 %collective-permute-start.7 = (bf16[736,512]{1,0:T(8,128)(2,1)}, bf16[736,512]{1,0:T(8,128)(2,1)}, u32[]{:S(2)}, u32[]{:S(2)}) collective-permute-start(bf16[736,512]{1,0:T(8,128)(2,1)} %copy-done.5), channel_id=1, source_target_pairs={{0,4},{4,0},{1,5},{5,1},{2,6},{6,2},{3,7},{7,3},{8,12},{12,8},{9,1... | collective-permute-start | bytes 2261000 | tf_op jit(solution)/shard_map/ppermute | solution.py:19
  53.1 25.0 %collective-permute-start.9 = (bf16[512,512]{1,0:T(8,128)(2,1)}, bf16[512,512]{1,0:T(8,128)(2,1)S(1)}, u32[]{:S(2)}, u32[]{:S(2)}) collective-permute-start(bf16[512,512]{1,0:T(8,128)(2,1)} %slice.9), channel_id=1, source_target_pairs={{0,16},{16,0},{1,17},{17,1},{2,18},{18,2},{3,19},{19,3},{4,20},{20... | collective-permute-start | bytes 1572872 | tf_op jit(solution)/shard_map/ppermute | solution.py:24
  55.0 24.2 %collective-permute-start.8 = (bf16[512,512]{1,0:T(8,128)(2,1)}, bf16[512,512]{1,0:T(8,128)(2,1)}, u32[]{:S(2)}, u32[]{:S(2)}) collective-permute-start(bf16[512,512]{1,0:T(8,128)(2,1)} %collective-permute-done.refs_4_), channel_id=1, source_target_pairs={{0,4},{4,0},{1,5},{5,1},{2,6},{6,2},{3,7},{7,3},{8,12},{12,8},{9,1... | collective-permute-start | bytes 1572872 | tf_op jit(solution)/shard_map/ppermute | solution.py:19
  55.5 23.6 %collective-permute-start.10 = (bf16[512,512]{1,0:T(8,128)(2,1)}, bf16[512,512]{1,0:T(8,128)(2,1)}, u32[]{:S(2)}, u32[]{:S(2)}) collective-permute-start(bf16[512,512]{1,0:T(8,128)(2,1)} %get-tuple-element.75), channel_id=1, source_target_pairs={{0,8},{8,0},{1,9},{9,1},{2,10},{10,2},{3,11},{11,3},{4,12},{12,4},... | collective-permute-start | bytes 1572872 | tf_op jit(solution)/shard_map/ppermute | solution.py:19
  79.2 13.6 %collective-permute-start.12 = (bf16[224,512]{1,0:T(8,128)(2,1)}, bf16[224,512]{1,0:T(8,128)(2,1)S(1)}, u32[]{:S(2)}, u32[]{:S(2)}) collective-permute-start(bf16[224,512]{1,0:T(8,128)(2,1)} %get-tuple-element.91.refs_0_.refs_1_), channel_id=1, source_target_pairs={{0,16},{16,0},{1,17},{17,1},{2,18},{18,2},{3,19},{19,3},{4,20},{20... | collective-permute-start | bytes 688136 | tf_op jit(solution)/shard_map/ppermute | solution.py:24
  81.8 32.5 %collective-permute-start.11 = (bf16[2,256,1024]{2,1,0:T(8,128)(2,1)S(1)}, bf16[2,256,1024]{2,1,0:T(8,128)(2,1)}, u32[]{:S(2)}, u32[]{:S(2)}) collective-permute-start(bf16[2,256,1024]{2,1,0:T(8,128)(2,1)S(1)} %copy-done.3), channel_id=1, source_target_pairs={{0,8},{8,0},{1,9},{9,1},{2,10},{10,2},{3,11},{11,3},{4,12},{12,4},... | collective-permute-start | bytes 3145736 | tf_op jit(solution)/shard_map/ppermute | solution.py:19
  94.5 10.9 %collective-permute-start.13 = (bf16[256,896]{1,0:T(8,128)(2,1)S(1)}, bf16[256,896]{1,0:T(8,128)(2,1)S(1)}, u32[]{:S(2)}, u32[]{:S(2)}) collective-permute-start(bf16[256,896]{1,0:T(8,128)(2,1)S(1)} %constant_dynamic-slice_fusion), channel_id=1, source_target_pairs={{0,2},{2,0},{1,3},{3,1},{4,6},{6,4},{5,7},{7,5},{8,10},{10,8},{9,1... | collective-permute-start | bytes 1376264 | tf_op jit(solution)/shard_map/ppermute | solution.py:19
  95.1 18.3 %collective-permute-start.14 = (bf16[512,512]{1,0:T(8,128)(2,1)}, bf16[512,512]{1,0:T(8,128)(2,1)}, u32[]{:S(2)}, u32[]{:S(2)}) collective-permute-start(bf16[512,512]{1,0:T(8,128)(2,1)} %collective-permute-done.10.refs_2_), channel_id=1, source_target_pairs={{0,4},{4,0},{1,5},{5,1},{2,6},{6,2},{3,7},{7,3},{8,12},{12,8},{9,1... | collective-permute-start | bytes 1572872 | tf_op jit(solution)/shard_map/ppermute | solution.py:19
  98.2 15.2 %collective-permute-start.15 = (bf16[224,512]{1,0:T(8,128)(2,1)S(1)}, bf16[224,512]{1,0:T(8,128)(2,1)}, u32[]{:S(2)}, u32[]{:S(2)}) collective-permute-start(bf16[224,512]{1,0:T(8,128)(2,1)S(1)} %slice.10), channel_id=1, source_target_pairs={{0,16},{16,0},{1,17},{17,1},{2,18},{18,2},{3,19},{19,3},{4,20},{20... | collective-permute-start | bytes 688136 | tf_op jit(solution)/shard_map/ppermute | solution.py:24
  114.6 7.0 %collective-permute-start.16 = (bf16[64,896]{1,0:T(8,128)(2,1)S(1)}, bf16[64,896]{1,0:T(8,128)(2,1)S(1)}, u32[]{:S(2)}, u32[]{:S(2)}) collective-permute-start(bf16[64,896]{1,0:T(8,128)(2,1)S(1)} %slice.14), channel_id=1, source_target_pairs={{0,4},{4,8},{8,12},{12,16},{16,20},{20,24},{24,28},{1,5},{5,9},{9,... | collective-permute-start | bytes 344072 | tf_op jit(solution)/shard_map/ppermute | solution.py:530
  122.4 18.1 %collective-permute-start.17 = (bf16[320,896]{1,0:T(8,128)(2,1)}, bf16[320,896]{1,0:T(8,128)(2,1)S(1)}, u32[]{:S(2)}, u32[]{:S(2)}) collective-permute-start(bf16[320,896]{1,0:T(8,128)(2,1)} %pad_maximum_fusion.2), channel_id=1, source_target_pairs={{0,2},{2,0},{1,3},{3,1},{4,6},{6,4},{5,7},{7,5},{8,10},{10,8},{9,1... | collective-permute-start | bytes 1720328 | tf_op jit(solution)/shard_map/ppermute | solution.py:19
  126.1 22.5 %collective-permute-start.18 = (bf16[960,512]{1,0:T(8,128)(2,1)}, bf16[960,512]{1,0:T(8,128)(2,1)}, u32[]{:S(2)}, u32[]{:S(2)}) collective-permute-start(bf16[960,512]{1,0:T(8,128)(2,1)} %constant_dynamic-update-slice_fusion.refs_5_), channel_id=1, source_target_pairs={{0,4},{4,0},{1,5},{5,1},{2,6},{6,2},{3,7},{7,3},{8,12},{12,8},{9,1... | collective-permute-start | bytes 2949128 | tf_op jit(solution)/shard_map/ppermute | solution.py:19
  133.2 55.8 %collective-permute-start.21 = (bf16[320,896]{1,0:T(8,128)(2,1)}, bf16[320,896]{1,0:T(8,128)(2,1)}, u32[]{:S(2)}, u32[]{:S(2)}) collective-permute-start(bf16[320,896]{1,0:T(8,128)(2,1)} %pad_maximum_fusion.2), channel_id=1, source_target_pairs={{0,10},{2,8},{8,2},{10,0},{1,11},{3,9},{9,3},{11,1},{4,14},{6,12},... | collective-permute-start | bytes 1720328 | tf_op jit(solution)/shard_map/ppermute | solution.py:537
  135.5 53.5 %collective-permute-start.20 = (bf16[320,896]{1,0:T(8,128)(2,1)}, bf16[320,896]{1,0:T(8,128)(2,1)}, u32[]{:S(2)}, u32[]{:S(2)}) collective-permute-start(bf16[320,896]{1,0:T(8,128)(2,1)} %pad_maximum_fusion.2), channel_id=1, source_target_pairs={{0,8},{8,0},{1,9},{9,1},{2,10},{10,2},{3,11},{11,3},{4,12},{12,4},... | collective-permute-start | bytes 1720328 | tf_op jit(solution)/shard_map/ppermute | solution.py:19
  138.3 49.3 %collective-permute-start.23 = (bf16[1024,512]{1,0:T(8,128)(2,1)}, bf16[1024,512]{1,0:T(8,128)(2,1)}, u32[]{:S(2)}, u32[]{:S(2)}) collective-permute-start(bf16[1024,512]{1,0:T(8,128)(2,1)} %pad_maximum_fusion.1), channel_id=1, source_target_pairs={{0,16},{16,0},{1,17},{17,1},{2,18},{18,2},{3,19},{19,3},{4,20},{20... | collective-permute-start | bytes 3145736 | tf_op jit(solution)/shard_map/ppermute | solution.py:24
  149.8 13.5 %collective-permute-start.19 = (bf16[640,896]{1,0:T(8,128)(2,1)S(1)}, bf16[640,896]{1,0:T(8,128)(2,1)}, u32[]{:S(2)}, u32[]{:S(2)}) collective-permute-start(bf16[640,896]{1,0:T(8,128)(2,1)S(1)} %pad_maximum_fusion.rows_ref), channel_id=1, source_target_pairs={{0,1},{1,0},{2,3},{3,2},{4,5},{5,4},{6,7},{7,6},{8,9},{9,8},{10,11... | collective-permute-start | bytes 3440648 | tf_op jit(solution)/shard_map/ppermute | solution.py:19
  187.6 25.6 %collective-permute-start.24 = (bf16[1024,512]{1,0:T(8,128)(2,1)}, bf16[1024,512]{1,0:T(8,128)(2,1)}, u32[]{:S(2)}, u32[]{:S(2)}) collective-permute-start(bf16[1024,512]{1,0:T(8,128)(2,1)} %collective-permute-done.23.refs_0_), channel_id=1, source_target_pairs={{0,4},{4,0},{1,5},{5,1},{2,6},{6,2},{3,7},{7,3},{8,12},{12,8},{9,1... | collective-permute-start | bytes 3145736 | tf_op jit(solution)/shard_map/ppermute | solution.py:19
  221.3 6.9 %collective-permute-start.25 = (bf16[2,512,1024]{2,1,0:T(8,128)(2,1)}, bf16[2,512,1024]{2,1,0:T(8,128)(2,1)}, u32[]{:S(2)}, u32[]{:S(2)}) collective-permute-start(bf16[2,512,1024]{2,1,0:T(8,128)(2,1)} %shard_map.127), channel_id=1, source_target_pairs={{0,1},{1,0},{2,3},{3,2},{4,5},{5,4},{6,7},{7,6},{8,9},{9,8},{10,11... | collective-permute-start | bytes 6291464 | tf_op jit(solution)/shard_map/ppermute | solution.py:19
  233.5 14.5 %collective-permute-start.26 = (bf16[256,1024]{1,0:T(8,128)(2,1)}, bf16[256,1024]{1,0:T(8,128)(2,1)S(1)}, u32[]{:S(2)}, u32[]{:S(2)}) collective-permute-start(bf16[256,1024]{1,0:T(8,128)(2,1)} %get-tuple-element.114), channel_id=1, source_target_pairs={{0,8},{8,0},{1,9},{9,1},{2,10},{10,2},{3,11},{11,3},{4,12},{12,4},... | collective-permute-start | bytes 1572872 | tf_op jit(solution)/shard_map/ppermute | solution.py:19
  233.5 14.7 %collective-permute-start.27 = (bf16[256,1024]{1,0:T(8,128)(2,1)}, bf16[256,1024]{1,0:T(8,128)(2,1)}, u32[]{:S(2)}, u32[]{:S(2)}) collective-permute-start(bf16[256,1024]{1,0:T(8,128)(2,1)} %get-tuple-element.115), channel_id=1, source_target_pairs={{0,2},{2,0},{1,3},{3,1},{4,6},{6,4},{5,7},{7,5},{8,10},{10,8},{9,1... | collective-permute-start | bytes 1572872 | tf_op jit(solution)/shard_map/ppermute | solution.py:19
  248.2 15.9 %collective-permute-start.28 = (bf16[256,1024]{1,0:T(8,128)(2,1)}, bf16[256,1024]{1,0:T(8,128)(2,1)}, u32[]{:S(2)}, u32[]{:S(2)}) collective-permute-start(bf16[256,1024]{1,0:T(8,128)(2,1)} %get-tuple-element.116), channel_id=1, source_target_pairs={{0,10},{2,8},{8,2},{10,0},{1,11},{3,9},{9,3},{11,1},{4,14},{6,12},... | collective-permute-start | bytes 1572872 | tf_op jit(solution)/shard_map/ppermute | solution.py:440
  259.4 15.1 %collective-permute-start.30 = (bf16[256,1024]{1,0:T(8,128)(2,1)}, bf16[256,1024]{1,0:T(8,128)(2,1)S(1)}, u32[]{:S(2)}, u32[]{:S(2)}) collective-permute-start(bf16[256,1024]{1,0:T(8,128)(2,1)} %get-tuple-element.125), channel_id=1, source_target_pairs={{0,8},{8,0},{1,9},{9,1},{2,10},{10,2},{3,11},{11,3},{4,12},{12,4},... | collective-permute-start | bytes 1572872 | tf_op jit(solution)/shard_map/ppermute | solution.py:19
  261.2 25.2 %collective-permute-start.31 = (bf16[256,1024]{1,0:T(8,128)(2,1)}, bf16[256,1024]{1,0:T(8,128)(2,1)S(1)}, u32[]{:S(2)}, u32[]{:S(2)}) collective-permute-start(bf16[256,1024]{1,0:T(8,128)(2,1)} %get-tuple-element.126), channel_id=1, source_target_pairs={{0,2},{2,0},{1,3},{3,1},{4,6},{6,4},{5,7},{7,5},{8,10},{10,8},{9,1... | collective-permute-start | bytes 1572872 | tf_op jit(solution)/shard_map/ppermute | solution.py:19
  261.5 24.9 %collective-permute-start.32 = (bf16[256,1024]{1,0:T(8,128)(2,1)}, bf16[256,1024]{1,0:T(8,128)(2,1)S(1)}, u32[]{:S(2)}, u32[]{:S(2)}) collective-permute-start(bf16[256,1024]{1,0:T(8,128)(2,1)} %get-tuple-element.127), channel_id=1, source_target_pairs={{0,10},{2,8},{8,2},{10,0},{1,11},{3,9},{9,3},{11,1},{4,14},{6,12},... | collective-permute-start | bytes 1572872 | tf_op jit(solution)/shard_map/ppermute | solution.py:440
  (20 other events, 164.9 us)
Sparse Core Ops, SparseCore 0:
  12.0 37.1 all-gather.4
  133.3 42.0 all-gather.6
